TPU v7x, 512 devices: a whole 4x4x16 slice. The times are simulated.
512 devices in a mesh: ka: 32 (over y_hi, z), ga: 16 (over y_lo, x, core).
Axes of the slice: x: 4, y: 4 (y_hi: 2, y_lo: 2; y = y_hi * 2 + y_lo), z: 16, core: 2. Of those that a mesh axis runs over, the one named last changes fastest.
Arguments:
- cond: bfloat16 [32, 8, 4096], P('ka', None, 'ga'), may hold values from -6 to 6
- vale: bfloat16 [32, 8, 4096], P('ka', None, 'ga'), may hold values from -6 to 6
- screen: bfloat16 [32, 4096, 4096], P('ka', 'ga'), may hold values from -0.0014648438 to 0.0014648438
- qtable: int32 [32, 32], replicated, may hold values from 0 to 31, as said below
- gmap: int32 [32, 4096], P('ka', 'ga'), may hold values from 0 to 4095, as said below
Outputs:
- kernel: float32 [32, 3, 4096], P('ka', None, 'ga')
Inputs may be any that keep to these rules, and one draw needn't show every extreme that they name: qtable[k,k2] depends only on (k - k2) mod 32, and each row names every k-difference once. `gmap`: each aligned block of 256 entries of a row is an ordering of that block's own grid indices.
All inputs are finite; a program needn't handle non-finite values.
Results may differ from a plain program's by a relative error of at most 0.0041.
Values may be sent and summed in bfloat16 or wider, within the bound.
No kernel may reach another device: no remote copies, remote signals or barrier semaphores. Data moves between devices by JAX's collectives and lax.ppermute only.
A program may use at most 64 MiB of HBM per device.

v0:
```python
import jax
import jax.numpy as jnp
from jax import lax
from jax.sharding import PartitionSpec as P

NSHIFT = 2


def passed_along(array, axis, by):
    peers = lax.axis_size(axis)
    return lax.ppermute(array, axis, [(i, (i + by) % peers) for i in range(peers)])


def broadcast(value, axis, source):
    kept = jnp.where(lax.axis_index(axis) == source, value, 0).astype(value.dtype)
    return lax.psum(kept, axis)


def pair_density(own, far):
    product = own.astype(jnp.float32)[:, None, :] * far.astype(jnp.float32)[None, :, :]
    return product.astype(jnp.bfloat16).reshape(-1, own.shape[-1])


def per_device(cond, vale, screen, qtable, gmap):
    local_k = cond.shape[0]
    g_width = cond.shape[2]
    cycle_len = lax.axis_size("ka")
    all_k = local_k * cycle_len
    start = lax.axis_index("ga") * g_width
    local_map = gmap - start
    cond_mapped = jnp.take_along_axis(cond, local_map[:, None, :], axis=2)
    vale_mapped = jnp.take_along_axis(vale, local_map[:, None, :], axis=2)
    blocks = {}
    vale_full = lax.all_gather(vale, "ga", axis=2, tiled=True)
    slabs = [(cond_mapped, vale_mapped)]
    for offset in range(NSHIFT):
        previous = slabs[-1]
        slabs.append(passed_along((previous[0], previous[1]), "ka", 1))
    tiles = [(entry[0], lax.all_gather(entry[1], "ga", axis=2, tiled=True)) for entry in slabs]
    for shift_d in range(1 - local_k, (NSHIFT + 1) * local_k):
        pairs = [
            (offset, left, right)
            for offset in range(NSHIFT + 1)
            for left in range(local_k)
            for right in range(local_k)
            if offset * local_k + left - right == shift_d
        ]
        qindex = qtable[shift_d % all_k, 0]
        owner = qindex // local_k
        holder = qindex % local_k
        slab = broadcast(lax.dynamic_index_in_dim(screen, holder, 0, keepdims=False), "ka", owner)
        stacked = jnp.concatenate(
            [
                pair_density(vale_full[left], tiles[offset][1][right])
                for offset, left, right in pairs
            ],
            axis=0,
        )
        image = lax.dot_general(
            slab, stacked, (((1,), (1,)), ((), ())), preferred_element_type=jnp.float32
        )
        for number, (offset, left, right) in enumerate(pairs):
            dens_c = pair_density(cond[left], tiles[offset][0][right])
            tile = jnp.dot(dens_c.astype(jnp.float32), image, precision=lax.Precision.HIGHEST)
            blocks[left, offset * local_k + right] = tile.reshape(-1)
    terms = jnp.stack([jnp.stack([blocks[0, column] for column in range((NSHIFT + 1) * local_k)])])
    return lax.psum_scatter(terms, "ga", scatter_dimension=2, tiled=True)


def solution(mesh):
    in_specs = (P("ka", None, "ga"), P("ka", None, "ga"), P("ka", "ga", None), P(), P("ka", "ga"))
    out_specs = P("ka", None, "ga")
    return jax.shard_map(
        per_device, mesh=mesh, in_specs=in_specs, out_specs=out_specs, check_vma=False
    )
```

profile of v0, /device:TPU:1, one launch (start us, length us, event | category | flops | bytes accessed | tf_op | source)
XLA Modules:
  0.0 440.7 jit_solution(7951815830204761134)
XLA Ops:
  6.5 0.0 all-reduce.3.cloned.1.call-start
  6.5 1.4 fusion.30
  9.9 4.4 %select_bitcast_fusion.2 = (bf16[256,4096]{1,0:T(8,128)(2,1)}, bf16[256,4096]{1,0:T(8,128)(2,1)}, bf16[256,4096]{1,0:T(8,128)(2,1)}) fusion(bf16[1,256,4096]{2,1,0:T(8,128)(2,1)} %param.9, pred[]{:T(512)S(6)} %eq.13, pred[]{:T(512)S(6)} %eq.15, pred[]{:T(512)S(6)} %eq.14), kind=kLoop, calls=%fused_computation.5 | loop fusion | flops 3145728 | bytes 8388611 | tf_op jit(solution)/shard_map/jit(_where)/select_n | solution.py:15
  14.3 0.0 copy-start.1
  14.3 0.0 copy-start
  14.3 0.0 copy-start.2
  14.3 0.0 all-reduce.3.cloned.1.call-update
  14.3 0.0 reduce-scatter.4.cloned.1.call-start
  14.4 0.6 copy-done.1
  15.0 0.1 copy.14
  15.1 0.0 copy-done
  15.1 0.1 copy.16
  15.2 0.0 copy-done.2
  15.3 0.9 gather_fusion
  16.1 0.9 gather_fusion.1
  17.0 0.1 bitcast_convert_fusion.6
  17.1 4.4 collective-permute-start.1
  21.5 3.5 collective-permute-start
  25.0 21.0 %all_gather.12 = bf16[1,8,4096]{2,1,0:T(8,128)(2,1)S(1)} all-gather(bf16[1,8,256]{2,1,0:T(8,128)(2,1)S(1)} %copy-done), channel_id=1, replica_groups=mesh['ka'=32,'ga'=16] {'ga'}, dimensions={2}, use_global_device_ids=true | all-gather | bytes 69632 | tf_op jit(solution)/shard_map/all_gather | solution.py:34
  46.0 21.4 %all_gather.13 = bf16[1,8,4096]{1,2,0:T(8,128)(2,1)S(1)} all-gather(bf16[1,8,256]{1,2,0:T(8,128)(2,1)S(1)} %get-tuple-element.19), channel_id=1, replica_groups=mesh['ka'=32,'ga'=16] {'ga'}, dimensions={2}, use_global_device_ids=true | all-gather | bytes 69632 | tf_op jit(solution)/shard_map/all_gather | solution.py:39
  67.4 0.1 bitcast_convert_fusion.2
  67.6 0.6 copy.17
  68.2 0.1 copy.15
  68.2 0.0 collective-permute-done.1
  68.2 22.7 %all_gather.14 = bf16[1,8,4096]{1,2,0:T(8,128)(2,1)S(1)} all-gather(bf16[1,8,256]{1,2,0:T(8,128)(2,1)S(1)} %collective-permute-done.1), channel_id=1, replica_groups=mesh['ka'=32,'ga'=16] {'ga'}, dimensions={2}, use_global_device_ids=true | all-gather | bytes 69632 | tf_op jit(solution)/shard_map/all_gather | solution.py:39
  90.9 0.1 bitcast_convert_fusion.1
  91.1 1.9 collective-permute-start.3
  93.0 0.0 collective-permute-done
  93.0 0.6 copy.19
  93.6 0.1 copy.18
  93.7 2.0 collective-permute-start.2
  95.7 7.4 %collective-permute-done.3 = bf16[1,8,256]{1,2,0:T(8,128)(2,1)S(1)} collective-permute-done((bf16[1,8,256]{1,2,0:T(8,128)(2,1)S(1)}, bf16[1,8,256]{1,2,0:T(8,128)(2,1)S(1)}, u32[]{:S(2)}, u32[]{:S(2)}) %collective-permute-start.3) | collective-permute-done | bytes 4128 | tf_op jit(solution)/shard_map/ppermute | solution.py:11
  103.1 21.5 %all_gather.15 = bf16[1,8,4096]{1,2,0:T(8,128)(2,1)S(1)} all-gather(bf16[1,8,256]{1,2,0:T(8,128)(2,1)S(1)} %collective-permute-done.3), channel_id=1, replica_groups=mesh['ka'=32,'ga'=16] {'ga'}, dimensions={2}, use_global_device_ids=true | all-gather | bytes 69632 | tf_op jit(solution)/shard_map/all_gather | solution.py:39
  124.7 0.1 bitcast_convert_fusion
  124.8 0.6 copy.21
  125.4 0.0 collective-permute-done.2
  125.4 0.1 copy.20
  125.5 204.0 %all-reduce.3.cloned.1.call-done = (bf16[256,4096]{1,0:T(8,128)(2,1)}, bf16[256,4096]{1,0:T(8,128)(2,1)}, bf16[256,4096]{1,0:T(8,128)(2,1)}) async-done(((bf16[256,4096]{1,0:T(8,128)(2,1)}, bf16[256,4096]{1,0:T(8,128)(2,1)}, bf16[256,4096]{1,0:T(8,128)(2,1)}), (bf16[256,4096]{1,0:T(8,128)(2,1)}, bf16[256,4096]{1,0:T(8,128)(2,1)}, bf16[256,4096]{1,0:T(8,128)(2,1)})) %all-reduce.3.cloned.1.call-update) | async-done | bytes 6291472 | tf_op jit(solution)/shard_map/psum | solution.py:16
  329.5 2.3 fusion.4
  331.8 0.0 copy-start.3
  331.8 0.2 fusion.19
  331.9 0.1 stack_reshape.10
  332.0 2.4 fusion.7
  334.5 0.2 fusion.22
  334.7 0.1 stack_reshape.11
  334.8 0.0 copy-done.3
  334.8 0.7 fusion.1
  335.5 0.2 fusion.16
  335.7 0.1 stack_reshape.9
  335.8 5.9 %copy.22 = f32[1,3,4096]{0,1,2:T(4,128)} copy(f32[1,3,4096]{2,0,1:T(1,128)S(1)} %stack.7) | data formatting | bytes 98304
  341.7 9.8 %bitcast_reduce_fusion = f32[4096,3]{1,0:T(8,128)} fusion(f32[1,3,4096]{0,1,2:T(4,128)} %copy.22), kind=kLoop, calls=%fused_computation.2 | loop fusion | bytes 98304
  351.6 0.0 reduce-scatter.4.cloned.1.call-update
  351.6 80.3 %reduce-scatter.4.cloned.1.call-done = f32[256,3]{1,0:T(8,128)} async-done(((f32[4096,3]{1,0:T(8,128)}), f32[256,3]{1,0:T(8,128)}) %reduce-scatter.4.cloned.1.call-update) | async-done | bytes 3088
  431.9 1.2 reshape_bitcast_fusion
  433.1 0.8 copy.23
  (8 shorter events, 0.2 us)
Async XLA Ops:
  6.5 322.9 %all-reduce.3.cloned.1.call-start = ((), (), s32[]{:S(2)}) async-start(), calls=%async_computation.2 | async-start | bytes 12582912 | tf_op jit(solution)/shard_map/psum | solution.py:16
  14.3 0.7 copy-start.1
  14.3 0.8 copy-start
  14.3 0.9 copy-start.2
  14.3 417.6 %reduce-scatter.4.cloned.1.call-start = ((), (), s32[]{:S(2)}) async-start(), calls=%async_computation.1 | async-start | bytes 2228224
  17.1 51.1 %collective-permute-start.1 = (bf16[1,8,256]{1,2,0:T(8,128)(2,1)S(1)}, bf16[1,8,256]{1,2,0:T(8,128)(2,1)S(1)}, u32[]{:S(2)}, u32[]{:S(2)}) collective-permute-start(bf16[1,8,256]{1,2,0:T(8,128)(2,1)S(1)} %get-tuple-element.19), channel_id=1, source_target_pairs={{0,16},{16,32},{32,48},{48,64},{64,80},{80,96},{96,112},{112,128},... | collective-permute-start | bytes 12296 | tf_op jit(solution)/shard_map/ppermute | solution.py:11
  21.5 71.5 %collective-permute-start = (bf16[1,8,256]{1,2,0:T(8,128)(2,1)S(1)}, bf16[1,8,256]{1,2,0:T(8,128)(2,1)S(1)}, u32[]{:S(2)}, u32[]{:S(2)}) collective-permute-start(bf16[1,8,256]{1,2,0:T(8,128)(2,1)S(1)} %get-tuple-element.10), channel_id=1, source_target_pairs={{0,16},{16,32},{32,48},{48,64},{64,80},{80,96},{96,112},{112,128},... | collective-permute-start | bytes 12296 | tf_op jit(solution)/shard_map/ppermute | solution.py:11
  91.1 12.0 %collective-permute-start.3 = (bf16[1,8,256]{1,2,0:T(8,128)(2,1)S(1)}, bf16[1,8,256]{1,2,0:T(8,128)(2,1)S(1)}, u32[]{:S(2)}, u32[]{:S(2)}) collective-permute-start(bf16[1,8,256]{1,2,0:T(8,128)(2,1)S(1)} %collective-permute-done.1), channel_id=1, source_target_pairs={{0,16},{16,32},{32,48},{48,64},{64,80},{80,96},{96,112},{112,128},... | collective-permute-start | bytes 12296 | tf_op jit(solution)/shard_map/ppermute | solution.py:11
  93.7 31.7 %collective-permute-start.2 = (bf16[1,8,256]{1,2,0:T(8,128)(2,1)S(1)}, bf16[1,8,256]{1,2,0:T(8,128)(2,1)S(1)}, u32[]{:S(2)}, u32[]{:S(2)}) collective-permute-start(bf16[1,8,256]{1,2,0:T(8,128)(2,1)S(1)} %collective-permute-done), channel_id=1, source_target_pairs={{0,16},{16,32},{32,48},{48,64},{64,80},{80,96},{96,112},{112,128},... | collective-permute-start | bytes 12296 | tf_op jit(solution)/shard_map/ppermute | solution.py:11
  331.8 3.0 copy-start.3
Sparse Core Ops, SparseCore 0:
  14.4 314.9 all-reduce.2
  351.7 80.1 reduce-scatter.3
where the time goes:
time: 442 us; the launch traced here: 441 us
  waiting for transfers between devices  292 us (66%)
  blocking collectives  86.6 us (20%)
  local copies, waits for them, and re-layouts  23.8 us (5%)
  between operations  15.6 us (4%)
  starting transfers between devices  11.9 us (3%)
  matrix products  5.95 us (1%)
  other arithmetic  5.05 us (1%)
    psum x1, waiting for transfers between devices, broadcast(): return lax.psum(kept, axis)  204 us
    unnamed x3, waiting for transfers between devices  80.3 us
    all_gather x3, blocking collectives, per_device(): lax.all_gather(entry[1], 'ga', axis=2, tiled=True)  65.7 us
    all_gather x1, blocking collectives, per_device(): vale_full = lax.all_gather(vale, 'ga', axis=2, tiled=True)  21 us
    unnamed x14, local copies, waits for them, and re-layouts  18.6 us
    ppermute x4, starting transfers between devices, passed_along(): lax.ppermute(array, axis, [(i, (i + by) % peers) for i in range(peers)])  11.9 us
  transfers between devices with their start and end apart: 6, of which 3 were waited for; matrix products, arithmetic and copies ran while one was open for 1% of the time, Pallas kernels for 0%

commit v1 on v0

v1 whole, which is shorter than its diff:
```python
import jax
import jax.numpy as jnp
from jax import lax
from jax.experimental import pallas as pl
from jax.experimental.pallas import tpu as pltpu
from jax.sharding import PartitionSpec as P

NSHIFT = 2
STEP_K = 4


def last_dims(a, b):
    return lax.dot_general(a, b, (((1,), (1,)), ((), ())), preferred_element_type=jnp.float32)


def density(pair):
    pair = pair.astype(jnp.float32)
    own, far = pair[:8], pair[8:]
    product = own[:, None, :] * far[None, :, :]
    return product.reshape(64, pair.shape[-1]).astype(jnp.bfloat16)


def tile_kernel(w_own, w_mate, vale, c_own, c_mate, out, pv, pc_own, pc_mate):
    blocks, _, _, width = vale.shape
    for k in range(STEP_K):
        rows = pl.ds(64 * k, 64)
        for block in range(blocks):
            pv[rows, pl.ds(block * width, width)] = density(vale[block, k])
        pc_own[rows, :] = density(c_own[k])
        pc_mate[rows, :] = density(c_mate[k])
    image_own = last_dims(pv[...], w_own[...]).astype(jnp.bfloat16)
    image_mate = last_dims(pv[...], w_mate[...]).astype(jnp.bfloat16)
    full = last_dims(pc_own[...], image_own) + last_dims(pc_mate[...], image_mate)
    low = lax.broadcasted_iota(jnp.int32, (64, 128), 1) < 64
    for pair in range(STEP_K // 2):
        base = 128 * pair
        strip = full[:, base : base + 128]
        tile = jnp.where(low, strip[base : base + 64], strip[base + 64 : base + 128])
        out[:, pl.ds(4 * pair, 4), :] = tile.reshape(16, 4, 128)


def tiles(w_own, w_mate, vale, c_own, c_mate):
    blocks, n_k, rows, width = vale.shape
    grid_h = w_own.shape[1]
    return pl.pallas_call(
        tile_kernel,
        grid=(n_k // STEP_K,),
        in_specs=[
            pl.BlockSpec(w_own.shape, lambda i: (0, 0)),
            pl.BlockSpec(w_mate.shape, lambda i: (0, 0)),
            pl.BlockSpec((blocks, STEP_K, rows, width), lambda i: (0, i, 0, 0)),
            pl.BlockSpec((STEP_K, rows, width), lambda i: (i, 0, 0)),
            pl.BlockSpec((STEP_K, rows, width), lambda i: (i, 0, 0)),
        ],
        out_specs=pl.BlockSpec((16, 2 * STEP_K, 128), lambda i: (0, i, 0)),
        out_shape=jax.ShapeDtypeStruct((16, 2 * n_k, 128), jnp.float32),
        scratch_shapes=[
            pltpu.VMEM((64 * STEP_K, grid_h), jnp.bfloat16),
            pltpu.VMEM((64 * STEP_K, width), jnp.bfloat16),
            pltpu.VMEM((64 * STEP_K, width), jnp.bfloat16),
        ],
        compiler_params=pltpu.CompilerParams(vmem_limit_bytes=40 * 1024 * 1024),
    )(w_own, w_mate, vale, c_own, c_mate)


def per_device(cond, vale, screen, qtable, gmap):
    n_ka = lax.axis_size("ka")
    n_ga = lax.axis_size("ga")
    n_z = n_ka // 2
    g_width = cond.shape[2]
    my_ka = lax.axis_index("ka")
    my_ga = lax.axis_index("ga")
    core = my_ga % 2
    swap_core = [(i, i ^ 1) for i in range(n_ga)]
    swap_y = [(i, i ^ n_z) for i in range(n_ka)]
    z_groups = [list(range(n_z)), list(range(n_z, n_ka))]

    slab = screen[0]
    slab_mate = lax.ppermute(slab, "ga", swap_core)

    local_map = gmap[0] - my_ga * g_width
    own = jnp.concatenate([vale[0], cond[0]], axis=0)
    mapped = jnp.take(own, local_map, axis=1)
    data = jnp.stack([own, mapped])
    other = lax.ppermute(data, "ka", swap_y)
    first = my_ka < n_z
    both = jnp.stack([jnp.where(first, data, other), jnp.where(first, other, data)])
    sent = jnp.broadcast_to(both[None], (n_z,) + both.shape)
    got = lax.all_to_all(sent, "ka", 0, 0, axis_index_groups=z_groups)
    every = jnp.swapaxes(got, 0, 1).reshape(n_ka, 2, 16, g_width)

    wanted = qtable[: NSHIFT + 1, 0]
    offset = jnp.sum(jnp.where(wanted == my_ka, jnp.arange(NSHIFT + 1, dtype=jnp.int32), 0))
    far = every[:, 1]
    far = jnp.concatenate([far[n_ka - NSHIFT :], far], axis=0)
    far = lax.dynamic_slice_in_dim(far, NSHIFT - offset, n_ka, 0)
    near = every[:, 0]
    v_pairs = jnp.concatenate([near[:, :8], far[:, :8]], axis=1).reshape(2, n_z, 16, g_width)
    c_pairs = jnp.concatenate([near[:, 8:], far[:, 8:]], axis=1).reshape(2, n_z, 16, g_width)
    c_own = lax.dynamic_index_in_dim(c_pairs, core, 0, keepdims=False)
    c_mate = lax.ppermute(
        lax.dynamic_index_in_dim(c_pairs, 1 - core, 0, keepdims=False), "ga", swap_core
    )
    v_sent = jnp.broadcast_to(v_pairs[None], (n_ga // 2,) + v_pairs.shape)
    v_all = lax.all_to_all(v_sent.reshape(n_ga, n_z, 16, g_width), "ga", 0, 0)

    part = tiles(slab, slab_mate, v_all, c_own, c_mate)
    shares = lax.all_to_all(part, "ga", 0, 0)
    total = shares.reshape(n_ga // 2, 2, n_z // 2, 1, 4, 128).sum(0)
    spread = jnp.broadcast_to(total, (2, n_z // 2, 2, 4, 128)).reshape(n_ka, 4, 128)
    rows = lax.all_to_all(spread, "ka", 0, 0)
    mine = jnp.take(rows, wanted, axis=0)
    mine = jnp.where(my_ka % 2 == 0, mine[..., :64], mine[..., 64:])
    return mine.reshape(1, NSHIFT + 1, g_width)


def solution(mesh):
    in_specs = (P("ka", None, "ga"), P("ka", None, "ga"), P("ka", "ga", None), P(), P("ka", "ga"))
    out_specs = P("ka", None, "ga")
    return jax.shard_map(
        per_device, mesh=mesh, in_specs=in_specs, out_specs=out_specs, check_vma=False
    )
```

time: 442 us -> 137 us (0.31)
  waiting for transfers between devices: 292 us -> 55.9 us
  blocking collectives: 86.6 us -> 11.9 us
  starting transfers between devices: 11.9 us -> 48.6 us
  local copies, waits for them, and re-layouts: 23.8 us -> 5.43 us
  between operations: 15.6 us -> 1.46 us
  Pallas kernels: 0 us -> 8.9 us
  matrix products: 5.95 us -> 0 us
    psum x1 -> x0, waiting for transfers between devices: 204 us -> none  [broadcast(): return lax.psum(kept, axis)]
    all_gather x4 -> x0, blocking collectives: 86.6 us -> none  [the longest x3 65.7 us: per_device(): lax.all_gather(entry[1], 'ga', axis=2, tiled=True)]
    unnamed x3 -> x0, waiting for transfers between devices: 80.3 us -> none
    all_to_all x0 -> x3, waiting for transfers between devices: none -> 53.6 us  [the longest x1 24.4 us: per_device(): v_all = lax.all_to_all(v_sent.reshape(n_ga, n_z, 16, g_width), 'ga', 0, 0)]
    all_to_all x0 -> x3, starting transfers between devices: none -> 36.9 us  [the longest x1 15 us: per_device(): got = lax.all_to_all(sent, 'ka', 0, 0, axis_index_groups=z_groups)]
    unnamed x14 -> x0, local copies, waits for them, and re-layouts: 18.6 us -> none
    all_to_all x0 -> x1, blocking collectives: none -> 11.9 us  [per_device(): shares = lax.all_to_all(part, 'ga', 0, 0)]
    pallas_call x0 -> x1, Pallas kernels: none -> 8.9 us  [tiles(): pl.pallas_call(tile_kernel, grid=(n_k // STEP_K,), in_specs=[pl.BlockSpec...]
  transfers between devices with their start and end apart: 6 -> 6, of which waited for: 3 -> 5; matrix products, arithmetic and copies ran while one was open for 1% -> 3% of each run, Pallas kernels for 0% -> 0%
where the time goes in v1:
time: 137 us; the launch traced here: 136 us
  waiting for transfers between devices  55.9 us (41%)
  starting transfers between devices  48.6 us (35%)
  blocking collectives  11.9 us (9%)
  Pallas kernels  8.9 us (6%)
  local copies, waits for them, and re-layouts  5.43 us (4%)
  other arithmetic  4.1 us (3%)
  between operations  1.46 us (1%)
    all_to_all x1, waiting for transfers between devices, per_device(): v_all = lax.all_to_all(v_sent.reshape(n_ga, n_z, 16, g_width), 'ga', 0, 0)  24.4 us
    all_to_all x1, waiting for transfers between devices, per_device(): got = lax.all_to_all(sent, 'ka', 0, 0, axis_index_groups=z_groups)  15.3 us
    all_to_all x1, starting transfers between devices, per_device(): got = lax.all_to_all(sent, 'ka', 0, 0, axis_index_groups=z_groups)  15 us
    all_to_all x1, waiting for transfers between devices, per_device(): rows = lax.all_to_all(spread, 'ka', 0, 0)  13.9 us
    all_to_all x1, starting transfers between devices, per_device(): v_all = lax.all_to_all(v_sent.reshape(n_ga, n_z, 16, g_width), 'ga', 0, 0)  12.8 us
    all_to_all x1, blocking collectives, per_device(): shares = lax.all_to_all(part, 'ga', 0, 0)  11.9 us
    all_to_all x1, starting transfers between devices, per_device(): rows = lax.all_to_all(spread, 'ka', 0, 0)  9.2 us
    pallas_call x1, Pallas kernels, tiles(): pl.pallas_call(tile_kernel, grid=(n_k // STEP_K,), in_specs=[pl.BlockSpec...  8.9 us
  transfers between devices with their start and end apart: 6, of which 5 were waited for; matrix products, arithmetic and copies ran while one was open for 3% of the time, Pallas kernels for 0%

profile of v1, /device:TPU:1, one launch (start us, length us, event | category | flops | bytes accessed | tf_op | source)
XLA Modules:
  0.0 136.3 jit_solution(14951213561333645495)
XLA Ops:
  0.0 0.7 compare_select_fusion
  0.7 0.7 fusion.2
  1.4 0.1 copy.15
  1.5 0.9 gather_fusion
  2.4 0.1 bitcast_select_fusion
  2.5 0.1 copy.16
  2.6 5.7 %collective-permute-start.1 = (bf16[2,16,256]{2,1,0:T(8,128)(2,1)S(1)}, bf16[2,16,256]{2,1,0:T(8,128)(2,1)S(1)}, u32[]{:S(2)}, u32[]{:S(2)}) collective-permute-start(bf16[2,16,256]{2,1,0:T(8,128)(2,1)S(1)} %pad_maximum_fusion.3), channel_id=1, source_target_pairs={{0,256},{16,272},{32,288},{48,304},{64,320},{80,336},{96,352},{112... | collective-permute-start | bytes 49160 | tf_op jit(solution)/shard_map/ppermute | solution.py:85
  8.2 1.1 collective-permute-done.1
  9.4 0.9 broadcast_in_dim.43
  10.2 15.0 %all-to-all-start = ((bf16[16,2,2,16,256]{4,3,1,2,0:T(8,128)(2,1)}), bf16[16,2,2,16,256]{4,3,1,2,0:T(8,128)(2,1)S(1)}, u32[]{:S(2)}, u32[]{:S(2)}) async-start(bf16[16,2,2,16,256]{4,3,1,2,0:T(8,128)(2,1)} %broadcast_in_dim.43), calls=%async_computation | async-start | bytes 1048576 | tf_op jit(solution)/shard_map/all_to_all | solution.py:89
  25.2 4.0 %collective-permute-start = (bf16[256,4096]{1,0:T(8,128)(2,1)}, bf16[256,4096]{1,0:T(8,128)(2,1)}, u32[]{:S(2)}, u32[]{:S(2)}) collective-permute-start(bf16[256,4096]{1,0:T(8,128)(2,1)} %bitcast.w_own), channel_id=1, source_target_pairs={{0,1},{1,0},{2,3},{3,2},{4,5},{5,4},{6,7},{7,6},{8,9},{9,8},{10,11... | collective-permute-start | bytes 6291464 | tf_op jit(solution)/shard_map/ppermute | solution.py:79
  29.2 0.8 and_reduce_fusion
  30.1 0.6 select_reduce_fusion
  32.0 15.3 %all-to-all-done = bf16[16,2,2,16,256]{4,3,1,2,0:T(8,128)(2,1)S(1)} async-done(((bf16[16,2,2,16,256]{4,3,1,2,0:T(8,128)(2,1)}), bf16[16,2,2,16,256]{4,3,1,2,0:T(8,128)(2,1)S(1)}, u32[]{:S(2)}, u32[]{:S(2)}) %all-to-all-start) | async-done | bytes 524320 | tf_op jit(solution)/shard_map/all_to_all | solution.py:89
  47.3 0.1 copy.18
  47.5 1.5 %broadcast_in_dim.45 = bf16[8,2,16,16,256]{4,3,2,1,0:T(8,128)(2,1)} broadcast(bf16[2,16,16,256]{3,2,1,0:T(8,128)(2,1)S(1)} %bitcast.42), dimensions={1,2,3,4} | broadcast | bytes 2359296 | tf_op jit(solution)/shard_map/broadcast_in_dim | solution.py:104
  49.0 12.8 %all-to-all-start.1 = ((bf16[16,16,16,256]{3,2,1,0:T(8,128)(2,1)}), bf16[16,16,16,256]{3,2,1,0:T(8,128)(2,1)S(1)}, u32[]{:S(2)}, u32[]{:S(2)}) async-start(bf16[16,16,16,256]{3,2,1,0:T(8,128)(2,1)} %bitcast.39), calls=%async_computation.1 | async-start | bytes 4194304 | tf_op jit(solution)/shard_map/all_to_all | solution.py:105
  61.8 2.0 %collective-permute-start.2 = (bf16[16,16,256]{2,1,0:T(8,128)(2,1)S(1)}, bf16[16,16,256]{2,1,0:T(8,128)(2,1)S(1)}, u32[]{:S(2)}, u32[]{:S(2)}) collective-permute-start(bf16[16,16,256]{2,1,0:T(8,128)(2,1)S(1)} %get-tuple-element.11), channel_id=1, source_target_pairs={{0,1},{1,0},{2,3},{3,2},{4,5},{5,4},{6,7},{7,6},{8,9},{9,8},{10,11... | collective-permute-start | bytes 393224 | tf_op jit(solution)/shard_map/ppermute | solution.py:101
  63.9 0.0 collective-permute-done.w_mate
  63.9 1.2 collective-permute-done.2.c_mate
  65.1 24.4 %all-to-all-done.1.vale = bf16[16,16,16,256]{3,2,1,0:T(8,128)(2,1)S(1)} async-done(((bf16[16,16,16,256]{3,2,1,0:T(8,128)(2,1)}), bf16[16,16,16,256]{3,2,1,0:T(8,128)(2,1)S(1)}, u32[]{:S(2)}, u32[]{:S(2)}) %all-to-all-start.1) | async-done | bytes 2097184 | tf_op jit(solution)/shard_map/all_to_all | solution.py:105
  89.5 8.9 %shard_map.55 = f32[16,32,128]{2,1,0:T(8,128)S(1)} custom-call(bf16[256,4096]{1,0:T(8,128)(2,1)} %bitcast.w_own, bf16[256,4096]{1,0:T(8,128)(2,1)} %collective-permute-done.w_mate, bf16[16,16,16,256]{3,2,1,0:T(8,128)(2,1)S(1)} %all-to-all-done.1.vale, bf16[16,16,256]{2,1,0:T(8,128)(2,1)S(1)} %get-tuple-element.12.c_own, ...), custom_call_target="tpu_custom_call" | custom-call | tf_op jit(solution)/shard_map/pallas_call | solution.py:45
  98.4 11.9 %all_to_all.20 = f32[16,32,128]{2,1,0:T(8,128)S(1)} all-to-all(f32[16,32,128]{2,1,0:T(8,128)S(1)} %shard_map.55), channel_id=1, replica_groups=mesh['ka'=32,'ga'=16] {'ga'}, dimensions={0} | all-to-all | bytes 524288 | tf_op jit(solution)/shard_map/all_to_all | solution.py:108
  110.4 0.6 broadcast_in_dim.46
  111.0 9.2 %all-to-all-start.3 = ((f32[32,4,128]{2,1,0:T(4,128)}), f32[32,4,128]{2,1,0:T(4,128)S(1)}, u32[]{:S(2)}, u32[]{:S(2)}) async-start(f32[32,4,128]{2,1,0:T(4,128)} %bitcast.23), calls=%async_computation.3 | async-start | bytes 131072 | tf_op jit(solution)/shard_map/all_to_all | solution.py:111
  120.2 0.8 fusion.1
  121.0 13.9 %all-to-all-done.3 = f32[32,4,128]{2,1,0:T(4,128)S(1)} async-done(((f32[32,4,128]{2,1,0:T(4,128)}), f32[32,4,128]{2,1,0:T(4,128)S(1)}, u32[]{:S(2)}, u32[]{:S(2)}) %all-to-all-start.3) | async-done | bytes 65568 | tf_op jit(solution)/shard_map/all_to_all | solution.py:111
  134.9 0.6 gather_fusion.1
  135.5 0.1 broadcast_select_fusion
  135.6 0.1 slice_select_fusion
  135.6 0.7 reshape.90
  (15 shorter events, 0.3 us)
Async XLA Ops:
  2.6 6.8 %collective-permute-start.1 = (bf16[2,16,256]{2,1,0:T(8,128)(2,1)S(1)}, bf16[2,16,256]{2,1,0:T(8,128)(2,1)S(1)}, u32[]{:S(2)}, u32[]{:S(2)}) collective-permute-start(bf16[2,16,256]{2,1,0:T(8,128)(2,1)S(1)} %pad_maximum_fusion.3), channel_id=1, source_target_pairs={{0,256},{16,272},{32,288},{48,304},{64,320},{80,336},{96,352},{112... | collective-permute-start | bytes 49160 | tf_op jit(solution)/shard_map/ppermute | solution.py:85
  10.2 37.0 %all-to-all-start = ((bf16[16,2,2,16,256]{4,3,1,2,0:T(8,128)(2,1)}), bf16[16,2,2,16,256]{4,3,1,2,0:T(8,128)(2,1)S(1)}, u32[]{:S(2)}, u32[]{:S(2)}) async-start(bf16[16,2,2,16,256]{4,3,1,2,0:T(8,128)(2,1)} %broadcast_in_dim.43), calls=%async_computation | async-start | bytes 1048576 | tf_op jit(solution)/shard_map/all_to_all | solution.py:89
  25.2 38.7 %collective-permute-start = (bf16[256,4096]{1,0:T(8,128)(2,1)}, bf16[256,4096]{1,0:T(8,128)(2,1)}, u32[]{:S(2)}, u32[]{:S(2)}) collective-permute-start(bf16[256,4096]{1,0:T(8,128)(2,1)} %bitcast.w_own), channel_id=1, source_target_pairs={{0,1},{1,0},{2,3},{3,2},{4,5},{5,4},{6,7},{7,6},{8,9},{9,8},{10,11... | collective-permute-start | bytes 6291464 | tf_op jit(solution)/shard_map/ppermute | solution.py:79
  49.0 40.5 %all-to-all-start.1 = ((bf16[16,16,16,256]{3,2,1,0:T(8,128)(2,1)}), bf16[16,16,16,256]{3,2,1,0:T(8,128)(2,1)S(1)}, u32[]{:S(2)}, u32[]{:S(2)}) async-start(bf16[16,16,16,256]{3,2,1,0:T(8,128)(2,1)} %bitcast.39), calls=%async_computation.1 | async-start | bytes 4194304 | tf_op jit(solution)/shard_map/all_to_all | solution.py:105
  61.8 3.2 %collective-permute-start.2 = (bf16[16,16,256]{2,1,0:T(8,128)(2,1)S(1)}, bf16[16,16,256]{2,1,0:T(8,128)(2,1)S(1)}, u32[]{:S(2)}, u32[]{:S(2)}) collective-permute-start(bf16[16,16,256]{2,1,0:T(8,128)(2,1)S(1)} %get-tuple-element.11), channel_id=1, source_target_pairs={{0,1},{1,0},{2,3},{3,2},{4,5},{5,4},{6,7},{7,6},{8,9},{9,8},{10,11... | collective-permute-start | bytes 393224 | tf_op jit(solution)/shard_map/ppermute | solution.py:101
  111.0 23.9 %all-to-all-start.3 = ((f32[32,4,128]{2,1,0:T(4,128)}), f32[32,4,128]{2,1,0:T(4,128)S(1)}, u32[]{:S(2)}, u32[]{:S(2)}) async-start(f32[32,4,128]{2,1,0:T(4,128)} %bitcast.23), calls=%async_computation.3 | async-start | bytes 131072 | tf_op jit(solution)/shard_map/all_to_all | solution.py:111

commit v2 on v1

v2 whole, which is shorter than its diff:
```python
import jax
import jax.numpy as jnp
from jax import lax
from jax.experimental import pallas as pl
from jax.experimental.pallas import tpu as pltpu
from jax.sharding import PartitionSpec as P

NSHIFT = 2
STEP_K = 4
VMEM = pl.BlockSpec(memory_space=pltpu.VMEM)
SMEM = pl.BlockSpec(memory_space=pltpu.SMEM)


def last_dims(a, b):
    return lax.dot_general(a, b, (((1,), (1,)), ((), ())), preferred_element_type=jnp.float32)


def density(own, far):
    product = own[:, None, :] * far[None, :, :]
    return product.reshape(64, own.shape[-1]).astype(jnp.bfloat16)


def lane_gather(source, places):
    return jnp.take_along_axis(source, places, axis=1, mode="promise_in_bounds")


def mapped(source, places):
    low, high = source[:, :128], source[:, 128:]
    sides = []
    for part in (places[:, :128], places[:, 128:]):
        inner = part & 127
        sides.append(jnp.where(part < 128, lane_gather(low, inner), lane_gather(high, inner)))
    return jnp.concatenate(sides, axis=1)


def map_entries(entries, count, store):
    maps = [entries[count + part].astype(jnp.float32).astype(jnp.int32) for part in range(2)]
    for entry in range(count):
        row = maps[entry // 8][entry % 8 : entry % 8 + 1]
        places = jnp.broadcast_to(row, (8, row.shape[1]))
        store(entry, mapped(entries[entry].astype(jnp.float32), places))


def tile_kernel(table, place, w_own, w_mate, vale, c_own, c_mate, out, far_v, far_c, pv, pc):
    sources, entries, _, width = vale.shape
    n_blocks = sources // 2
    count = entries - 2
    half_z = count - NSHIFT
    my_ka, core = place[0], place[1] % 2
    shift = sum(jnp.where(table[by, 0] == my_ka, by, 0) for by in range(1, NSHIFT + 1))

    @pl.loop(0, sources)
    def _(source):
        y, block = source // n_blocks, source % n_blocks
        lanes = pl.ds(pl.multiple_of(block * width, width), width)

        def store(entry, value):
            far_v[y * count + entry, :, lanes] = value

        map_entries(vale.at[source], count, store)

    for side, c_ref in enumerate((c_own, c_mate)):
        for y in range(2):

            def store(entry, value, y=y, side=side):
                far_c[y * count + entry, :, pl.ds(side * width, width)] = value

            map_entries(c_ref.at[y], count, store)

    low = lax.broadcasted_iota(jnp.int32, (64, 128), 1) < 64
    for y in range(2):
        for part in range(half_z // STEP_K):
            step = y * (half_z // STEP_K) + part
            for k in range(STEP_K):
                entry = NSHIFT + part * STEP_K + k
                other = entry - shift
                crossed = jnp.logical_and(core == 0, other < NSHIFT)
                partner = jnp.where(crossed, 1 - y, y) * count + other
                rows = pl.ds(64 * k, 64)
                for block in range(n_blocks):
                    lanes = pl.ds(block * width, width)
                    own = vale[y * n_blocks + block, entry].astype(jnp.float32)
                    pv[step, rows, lanes] = density(own, far_v[partner, :, lanes])
                for side, c_ref in enumerate((c_own, c_mate)):
                    lanes = pl.ds(side * width, width)
                    own = c_ref[y, entry].astype(jnp.float32)
                    pc[step, rows, lanes] = density(own, far_c[partner, :, lanes])
            full = None
            for side, w_ref in enumerate((w_own, w_mate)):
                image = last_dims(pv[step], w_ref[...]).astype(jnp.bfloat16)
                term = last_dims(pc[step, :, pl.ds(side * width, width)], image)
                full = term if full is None else full + term
            for pair in range(STEP_K // 2):
                base = 128 * pair
                strip = full[:, base : base + 128]
                tile = jnp.where(low, strip[base : base + 64], strip[base + 64 : base + 128])
                out[pl.ds(16 * y, 16), pl.ds(8 * part + 4 * pair, 4), :] = tile.reshape(16, 4, 128)


def tiles(table, place, w_own, w_mate, vale, c_own, c_mate):
    sources, entries, _, width = vale.shape
    count = entries - 2
    grid_h = w_own.shape[1]
    half_z = count - NSHIFT
    steps = 2 * half_z // STEP_K
    return pl.pallas_call(
        tile_kernel,
        in_specs=[SMEM, SMEM] + [VMEM] * 5,
        out_specs=VMEM,
        out_shape=jax.ShapeDtypeStruct((sources, 2 * half_z, 128), jnp.float32),
        scratch_shapes=[
            pltpu.VMEM((2 * count, 8, grid_h), jnp.float32),
            pltpu.VMEM((2 * count, 8, 2 * width), jnp.float32),
            pltpu.VMEM((steps, 64 * STEP_K, grid_h), jnp.bfloat16),
            pltpu.VMEM((steps, 64 * STEP_K, 2 * width), jnp.bfloat16),
        ],
        compiler_params=pltpu.CompilerParams(vmem_limit_bytes=36 * 1024 * 1024),
    )(table, place, w_own, w_mate, vale, c_own, c_mate)


def pack_kernel(got, v_out, c_out):
    n_z, _, _, width = got.shape
    half_z = n_z // 2
    count = half_z + NSHIFT
    row_id = lax.broadcasted_iota(jnp.int32, (8, width), 0)
    for half in range(2):
        spots = [(half * half_z + entry - NSHIFT) % n_z for entry in range(count)]
        packs = []
        for first in range(0, count, 8):
            rows = jnp.zeros((8, width), jnp.float32)
            for entry in range(first, min(first + 8, count)):
                rows = jnp.where(row_id == entry - first, got[spots[entry], 2].astype(jnp.float32), rows)
            packs.append(rows.astype(jnp.bfloat16))
        for part, rows in enumerate(packs):
            c_out[half, count + part] = rows
        for entry, spot in enumerate(spots):
            c_out[half, entry] = got[spot, 1]
        for dest in range(half, v_out.shape[0], 2):
            for part, rows in enumerate(packs):
                v_out[dest, count + part] = rows
            for entry, spot in enumerate(spots):
                v_out[dest, entry] = got[spot, 0]


def pack(got, dests):
    n_z, _, _, width = got.shape
    entries = n_z // 2 + NSHIFT + 2
    return pl.pallas_call(
        pack_kernel,
        in_specs=[VMEM],
        out_specs=[VMEM, VMEM],
        out_shape=[
            jax.ShapeDtypeStruct((dests, entries, 8, width), jnp.bfloat16),
            jax.ShapeDtypeStruct((2, entries, 8, width), jnp.bfloat16),
        ],
        compiler_params=pltpu.CompilerParams(vmem_limit_bytes=8 * 1024 * 1024),
    )(got)


def total_kernel(shares, out):
    sources, rows, _ = shares.shape
    for y in range(2):
        for core in range(2):
            first = y * (sources // 2) + core
            total = shares[first]
            for source in range(first + 2, first + sources // 2, 2):
                total = total + shares[source]
            for pair in range(rows // 4):
                strip = total[4 * pair : 4 * pair + 4]
                for odd in range(2):
                    z = core * (rows // 2) + 2 * pair + odd
                    out[z, pl.ds(4 * y, 4), :] = strip


def totals(shares):
    n_z = shares.shape[1]
    return pl.pallas_call(
        total_kernel,
        in_specs=[VMEM],
        out_specs=VMEM,
        out_shape=jax.ShapeDtypeStruct((n_z, 8, 128), jnp.float32),
        compiler_params=pltpu.CompilerParams(vmem_limit_bytes=4 * 1024 * 1024),
    )(shares)


def pick_kernel(table, place, rows, out):
    n_z = rows.shape[0]
    odd = place[0] % 2 == 1
    low = lax.broadcasted_iota(jnp.int32, (4, 128), 1) < 64
    for by in range(NSHIFT + 1):
        holder = table[by, 0]
        both = rows[holder % n_z]
        strip = jnp.where(holder // n_z == 0, both[:4], both[4:])
        turned = pltpu.roll(strip, 64, 1)
        left = jnp.where(odd, turned, strip)
        right = jnp.where(odd, strip, turned)
        for side in range(2):
            line = jnp.where(low[:1], left[2 * side : 2 * side + 1], right[2 * side + 1 : 2 * side + 2])
            out[0, pl.ds(by, 1), pl.ds(128 * side, 128)] = line


def pick(table, place, rows):
    return pl.pallas_call(
        pick_kernel,
        in_specs=[SMEM, SMEM, VMEM],
        out_specs=VMEM,
        out_shape=jax.ShapeDtypeStruct((1, NSHIFT + 1, 256), jnp.float32),
        compiler_params=pltpu.CompilerParams(vmem_limit_bytes=4 * 1024 * 1024),
    )(table, place, rows)


def per_device(cond, vale, screen, qtable, gmap):
    n_ka = lax.axis_size("ka")
    n_ga = lax.axis_size("ga")
    n_z = n_ka // 2
    g_width = cond.shape[2]
    my_ka = lax.axis_index("ka")
    my_ga = lax.axis_index("ga")
    core = my_ga % 2
    place = jnp.stack([my_ka, my_ga]).astype(jnp.int32)
    swap_core = [(i, i ^ 1) for i in range(n_ga)]
    swap_y = [(i, i ^ n_z) for i in range(n_ka)]
    along_z = [list(range(n_z)), list(range(n_z, n_ka))]
    planes = [
        [(y * n_z + z) * n_ga + g for y in range(2) for g in range(n_ga)] for z in range(n_z)
    ]

    slab = screen[0]
    slab_mate = lax.ppermute(slab, "ga", swap_core)

    local_map = (gmap - my_ga * g_width).astype(jnp.bfloat16)
    data = jnp.stack([vale[0], cond[0], jnp.broadcast_to(local_map, (8, g_width))])
    sent = jnp.broadcast_to(data[None], (n_z,) + data.shape)
    got = lax.all_to_all(sent, "ka", 0, 0, axis_index_groups=along_z)

    v_sent, c_here = pack(got, 2 * n_ga)
    c_other = lax.ppermute(c_here, "ka", swap_y)
    v_all = lax.all_to_all(v_sent, ("ka", "ga"), 0, 0, axis_index_groups=planes)
    first = my_ka < n_z
    c_both = jnp.stack([jnp.where(first, c_here, c_other), jnp.where(first, c_other, c_here)], 1)
    c_own = lax.dynamic_index_in_dim(c_both, core, 0, keepdims=False)
    c_mate = lax.ppermute(
        lax.dynamic_index_in_dim(c_both, 1 - core, 0, keepdims=False), "ga", swap_core
    )

    part = tiles(qtable, place, slab, slab_mate, v_all, c_own, c_mate)
    shares = lax.all_to_all(part, ("ka", "ga"), 0, 0, axis_index_groups=planes)
    rows = lax.all_to_all(totals(shares), "ka", 0, 0, axis_index_groups=along_z)
    return pick(qtable, place, rows)


def solution(mesh):
    in_specs = (P("ka", None, "ga"), P("ka", None, "ga"), P("ka", "ga", None), P(), P("ka", "ga"))
    out_specs = P("ka", None, "ga")
    return jax.shard_map(
        per_device, mesh=mesh, in_specs=in_specs, out_specs=out_specs, check_vma=False
    )
```

time: 137 us -> 115 us (0.84)
  waiting for transfers between devices: 55.9 us -> 27.9 us
  blocking collectives: 11.9 us -> 30.7 us
  starting transfers between devices: 48.6 us -> 38.1 us
  Pallas kernels: 8.9 us -> 13.6 us
  other arithmetic: 4.1 us -> 1.53 us
  local copies, waits for them, and re-layouts: 5.43 us -> 2.87 us
    all_to_all x3 -> x2, waiting for transfers between devices: 53.6 us -> 9.67 us  [the longest x1 9.67 us: per_device(): got = lax.all_to_all(sent, 'ka', 0, 0, axis_index_groups=along_z)]
    all_to_all x1 -> x2, blocking collectives: 11.9 us -> 30.7 us  [the longest x1 16 us: per_device(): rows = lax.all_to_all(totals(shares), 'ka', 0, 0, axis_index_groups=along_z)]
    ppermute x2, waiting for transfers between devices: 2.29 us -> 18.2 us  [the longest x1 17.4 us: per_device(): c_other = lax.ppermute(c_here, 'ka', swap_y)]
    all_to_all x3 -> x2, starting transfers between devices: 36.9 us -> 27.7 us  [the longest x1 15.7 us: per_device(): got = lax.all_to_all(sent, 'ka', 0, 0, axis_index_groups=along_z)]
    pallas_call x1 -> x4, Pallas kernels: 8.9 us -> 13.6 us  [the longest x1 11.4 us: tiles(): pl.pallas_call(tile_kernel, in_specs=[SMEM, SMEM] + [VMEM] * 5, out_specs...]
    broadcast_in_dim x3 -> x1, local copies, waits for them, and re-layouts: 3 us -> 0.68 us  [per_device(): sent = jnp.broadcast_to(data[None], (n_z,) + data.shape)]
    select_n x5 -> x0, other arithmetic: 1.74 us -> none  [the longest x2 0.88 us: per_device(): mine = jnp.take(rows, wanted, axis=0)]
    unnamed x0 -> x4, local copies, waits for them, and re-layouts: none -> 1.59 us
  transfers between devices with their start and end apart: 6 -> 5, of which waited for: 5 -> 3; matrix products, arithmetic and copies ran while one was open for 3% -> 0% of each run, Pallas kernels for 0% -> 1%
where the time goes in v2:
time: 115 us
  starting transfers between devices  38.1 us (33%)
  blocking collectives  30.7 us (27%)
  waiting for transfers between devices  27.9 us (24%)
  Pallas kernels  13.6 us (12%)
  local copies, waits for them, and re-layouts  2.87 us (2%)
  other arithmetic  1.53 us (1%)
    ppermute x1, waiting for transfers between devices, per_device(): c_other = lax.ppermute(c_here, 'ka', swap_y)  17.4 us
    all_to_all x1, blocking collectives, per_device(): rows = lax.all_to_all(totals(shares), 'ka', 0, 0, axis_index_groups=along_z)  16 us
    all_to_all x1, starting transfers between devices, per_device(): got = lax.all_to_all(sent, 'ka', 0, 0, axis_index_groups=along_z)  15.7 us
    all_to_all x1, blocking collectives, per_device(): shares = lax.all_to_all(part, ('ka', 'ga'), 0, 0, axis_index_groups=planes)  14.7 us
    all_to_all x1, starting transfers between devices, per_device(): v_all = lax.all_to_all(v_sent, ('ka', 'ga'), 0, 0, axis_index_groups=planes)  11.9 us
    pallas_call x1, Pallas kernels, tiles(): pl.pallas_call(tile_kernel, in_specs=[SMEM, SMEM] + [VMEM] * 5, out_specs...  11.4 us
    all_to_all x1, waiting for transfers between devices, per_device(): got = lax.all_to_all(sent, 'ka', 0, 0, axis_index_groups=along_z)  9.67 us
    ppermute x1, starting transfers between devices, per_device(): c_other = lax.ppermute(c_here, 'ka', swap_y)  4.81 us
  transfers between devices with their start and end apart: 5, of which 3 were waited for; matrix products, arithmetic and copies ran while one was open for 0% of the time, Pallas kernels for 1%

profile of v2, /device:TPU:1, one launch (start us, length us, event | category | flops | bytes accessed | tf_op | source)
XLA Modules:
  0.0 114.8 jit_solution(12398920303988910804)
XLA Ops:
  0.0 0.7 convert_reduce_fusion
  0.7 0.7 pad_maximum_fusion
  1.4 0.7 broadcast_in_dim.2
  2.1 15.7 %all-to-all-start = ((bf16[16,3,8,256]{3,2,1,0:T(8,128)(2,1)}), bf16[16,3,8,256]{3,2,1,0:T(8,128)(2,1)S(1)}, u32[]{:S(2)}, u32[]{:S(2)}) async-start(bf16[16,3,8,256]{3,2,1,0:T(8,128)(2,1)} %broadcast_in_dim.2), calls=%async_computation | async-start | bytes 393216 | tf_op jit(solution)/shard_map/all_to_all | solution.py:234
  17.9 0.0 copy-start.1
  17.9 2.9 %collective-permute-start = (bf16[256,4096]{1,0:T(8,128)(2,1)}, bf16[256,4096]{1,0:T(8,128)(2,1)}, u32[]{:S(2)}, u32[]{:S(2)}) collective-permute-start(bf16[256,4096]{1,0:T(8,128)(2,1)} %bitcast.11), channel_id=1, source_target_pairs={{0,1},{1,0},{2,3},{3,2},{4,5},{5,4},{6,7},{7,6},{8,9},{9,8},{10,11... | collective-permute-start | bytes 6291464 | tf_op jit(solution)/shard_map/ppermute | solution.py:229
  20.7 9.7 %all-to-all-done.got = bf16[16,3,8,256]{3,2,1,0:T(8,128)(2,1)S(1)} async-done(((bf16[16,3,8,256]{3,2,1,0:T(8,128)(2,1)}), bf16[16,3,8,256]{3,2,1,0:T(8,128)(2,1)S(1)}, u32[]{:S(2)}, u32[]{:S(2)}) %all-to-all-start) | async-done | bytes 196640 | tf_op jit(solution)/shard_map/all_to_all | solution.py:234
  30.4 1.3 %shard_map.55 = (bf16[32,12,8,256]{3,2,1,0:T(8,128)(2,1)}, bf16[2,12,8,256]{3,2,1,0:T(8,128)(2,1)S(1)}) custom-call(bf16[16,3,8,256]{3,2,1,0:T(8,128)(2,1)S(1)} %all-to-all-done.got), custom_call_target="tpu_custom_call" | custom-call | tf_op jit(solution)/shard_map/pallas_call | solution.py:148
  31.7 11.9 %all-to-all-start.1 = ((bf16[32,12,8,256]{3,2,1,0:T(8,128)(2,1)}), bf16[32,12,8,256]{3,2,1,0:T(8,128)(2,1)S(1)}, u32[]{:S(2)}, u32[]{:S(2)}) async-start(bf16[32,12,8,256]{3,2,1,0:T(8,128)(2,1)} %get-tuple-element.7), calls=%async_computation.1 | async-start | bytes 3145728 | tf_op jit(solution)/shard_map/all_to_all | solution.py:238
  43.6 4.8 %collective-permute-start.1 = (bf16[2,12,8,256]{3,2,1,0:T(8,128)(2,1)S(1)}, bf16[2,12,8,256]{3,2,1,0:T(8,128)(2,1)S(1)}, u32[]{:S(2)}, u32[]{:S(2)}) collective-permute-start(bf16[2,12,8,256]{3,2,1,0:T(8,128)(2,1)S(1)} %get-tuple-element.8), channel_id=1, source_target_pairs={{0,256},{16,272},{32,288},{48,304},{64,320},{80,336},{96,352},{112... | collective-permute-start | bytes 294920 | tf_op jit(solution)/shard_map/ppermute | solution.py:237
  48.5 17.4 %collective-permute-done.1 = bf16[2,12,8,256]{3,2,1,0:T(8,128)(2,1)S(1)} collective-permute-done((bf16[2,12,8,256]{3,2,1,0:T(8,128)(2,1)S(1)}, bf16[2,12,8,256]{3,2,1,0:T(8,128)(2,1)S(1)}, u32[]{:S(2)}, u32[]{:S(2)}) %collective-permute-start.1) | collective-permute-done | bytes 98336 | tf_op jit(solution)/shard_map/ppermute | solution.py:237
  65.9 2.8 %collective-permute-start.2 = (bf16[2,12,8,256]{3,2,1,0:T(8,128)(2,1)S(1)}, bf16[2,12,8,256]{3,2,1,0:T(8,128)(2,1)S(1)}, u32[]{:S(2)}, u32[]{:S(2)}) collective-permute-start(bf16[2,12,8,256]{3,2,1,0:T(8,128)(2,1)S(1)} %get-tuple-element.9), channel_id=1, source_target_pairs={{0,1},{1,0},{2,3},{3,2},{4,5},{5,4},{6,7},{7,6},{8,9},{9,8},{10,11... | collective-permute-start | bytes 294920 | tf_op jit(solution)/shard_map/ppermute | solution.py:242
  68.7 0.1 pad_add_fusion.place
  68.7 0.8 collective-permute-done.2.c_mate
  69.6 0.0 collective-permute-done.w_mate
  69.6 0.0 all-to-all-done.1.vale
  69.6 0.0 copy-done.1
  69.6 0.0 copy-start
  69.6 1.6 %copy-done = bf16[1,256,4096]{2,1,0:T(8,128)(2,1)S(1)} copy-done((bf16[1,256,4096]{2,1,0:T(8,128)(2,1)S(1)}, bf16[1,256,4096]{2,1,0:T(8,128)(2,1)}, u32[]{:S(2)}) %copy-start) | copy-done | bytes 2097176
  71.2 11.4 %shard_map.56 = f32[32,16,128]{2,1,0:T(8,128)S(1)} custom-call(s32[32,32]{1,0:T(8,128)S(1)} %copy-done.1, s32[2]{0:T(128)S(1)} %pad_add_fusion.place, bf16[256,4096]{1,0:T(8,128)(2,1)S(1)} %bitcast.12, bf16[256,4096]{1,0:T(8,128)(2,1)} %collective-permute-done.w_mate, bf16[32,12,8,256]{3,2,1,0:T(8,128)(2,1)S(1)} %all-to-all-done.1.vale, ...), custom_call_target="tpu_custom_call" | custom-call | tf_op jit(solution)/shard_map/pallas_call | solution.py:106
  82.6 14.7 %all_to_all.20.shares = f32[32,16,128]{2,1,0:T(8,128)S(1)} all-to-all(f32[32,16,128]{2,1,0:T(8,128)S(1)} %shard_map.56), channel_id=1, replica_groups={{0,1,2,3,4,5,6,7,8,9,10,11,12,13,14,15,256,257,258,259,260,261,262,263,..., dimensions={0} | all-to-all | bytes 524288 | tf_op jit(solution)/shard_map/all_to_all | solution.py:247
  97.3 16.0 %all_to_all.21.rows = f32[16,8,128]{2,1,0:T(8,128)S(1)} all-to-all(f32[16,8,128]{2,1,0:T(8,128)S(1)} %shard_map.57), channel_id=1, replica_groups={{0,16,32,48,64,80,96,112,128,144,160,176,192,208,224,240},{256,272,288,..., dimensions={0} | all-to-all | bytes 131072 | tf_op jit(solution)/shard_map/all_to_all | solution.py:248
  113.3 0.9 shard_map.58
  114.2 0.6 copy.6
  (4 shorter events, 0.1 us)
Async XLA Ops:
  2.1 28.3 %all-to-all-start = ((bf16[16,3,8,256]{3,2,1,0:T(8,128)(2,1)}), bf16[16,3,8,256]{3,2,1,0:T(8,128)(2,1)S(1)}, u32[]{:S(2)}, u32[]{:S(2)}) async-start(bf16[16,3,8,256]{3,2,1,0:T(8,128)(2,1)} %broadcast_in_dim.2), calls=%async_computation | async-start | bytes 393216 | tf_op jit(solution)/shard_map/all_to_all | solution.py:234
  17.9 51.7 %copy-start.1 = (s32[32,32]{1,0:T(8,128)S(1)}, s32[32,32]{1,0:T(8,128)}, u32[]{:S(2)}) copy-start(s32[32,32]{1,0:T(8,128)} %table.3) | copy-start | bytes 12292
  17.9 51.7 %collective-permute-start = (bf16[256,4096]{1,0:T(8,128)(2,1)}, bf16[256,4096]{1,0:T(8,128)(2,1)}, u32[]{:S(2)}, u32[]{:S(2)}) collective-permute-start(bf16[256,4096]{1,0:T(8,128)(2,1)} %bitcast.11), channel_id=1, source_target_pairs={{0,1},{1,0},{2,3},{3,2},{4,5},{5,4},{6,7},{7,6},{8,9},{9,8},{10,11... | collective-permute-start | bytes 6291464 | tf_op jit(solution)/shard_map/ppermute | solution.py:229
  31.7 37.9 %all-to-all-start.1 = ((bf16[32,12,8,256]{3,2,1,0:T(8,128)(2,1)}), bf16[32,12,8,256]{3,2,1,0:T(8,128)(2,1)S(1)}, u32[]{:S(2)}, u32[]{:S(2)}) async-start(bf16[32,12,8,256]{3,2,1,0:T(8,128)(2,1)} %get-tuple-element.7), calls=%async_computation.1 | async-start | bytes 3145728 | tf_op jit(solution)/shard_map/all_to_all | solution.py:238
  43.6 22.2 %collective-permute-start.1 = (bf16[2,12,8,256]{3,2,1,0:T(8,128)(2,1)S(1)}, bf16[2,12,8,256]{3,2,1,0:T(8,128)(2,1)S(1)}, u32[]{:S(2)}, u32[]{:S(2)}) collective-permute-start(bf16[2,12,8,256]{3,2,1,0:T(8,128)(2,1)S(1)} %get-tuple-element.8), channel_id=1, source_target_pairs={{0,256},{16,272},{32,288},{48,304},{64,320},{80,336},{96,352},{112... | collective-permute-start | bytes 294920 | tf_op jit(solution)/shard_map/ppermute | solution.py:237
  65.9 3.7 %collective-permute-start.2 = (bf16[2,12,8,256]{3,2,1,0:T(8,128)(2,1)S(1)}, bf16[2,12,8,256]{3,2,1,0:T(8,128)(2,1)S(1)}, u32[]{:S(2)}, u32[]{:S(2)}) collective-permute-start(bf16[2,12,8,256]{3,2,1,0:T(8,128)(2,1)S(1)} %get-tuple-element.9), channel_id=1, source_target_pairs={{0,1},{1,0},{2,3},{3,2},{4,5},{5,4},{6,7},{7,6},{8,9},{9,8},{10,11... | collective-permute-start | bytes 294920 | tf_op jit(solution)/shard_map/ppermute | solution.py:242
  69.6 1.6 %copy-start = (bf16[1,256,4096]{2,1,0:T(8,128)(2,1)S(1)}, bf16[1,256,4096]{2,1,0:T(8,128)(2,1)}, u32[]{:S(2)}) copy-start(bf16[1,256,4096]{2,1,0:T(8,128)(2,1)} %param.7) | copy-start | bytes 6291460

commit v3 on v2

v3 whole, which is shorter than its diff:
```python
import jax
import jax.numpy as jnp
from jax import lax
from jax.experimental import pallas as pl
from jax.experimental.pallas import tpu as pltpu
from jax.sharding import PartitionSpec as P

NSHIFT = 2
STEP_K = 4
CHUNK = 2
VMEM = pl.BlockSpec(memory_space=pltpu.VMEM)
SMEM = pl.BlockSpec(memory_space=pltpu.SMEM)
ANY = pl.BlockSpec(memory_space=pl.ANY)


def last_dims(a, b):
    return lax.dot_general(a, b, (((1,), (1,)), ((), ())), preferred_element_type=jnp.float32)


def density(own, far):
    product = own[:, None, :] * far[None, :, :]
    return product.reshape(64, own.shape[-1]).astype(jnp.bfloat16)


def lane_gather(source, places):
    return jnp.take_along_axis(source, places, axis=1, mode="promise_in_bounds")


def mapped(source, places):
    low, high = source[:, :128], source[:, 128:]
    sides = []
    for part in (places[:, :128], places[:, 128:]):
        inner = part & 127
        sides.append(jnp.where(part < 128, lane_gather(low, inner), lane_gather(high, inner)))
    return jnp.concatenate(sides, axis=1)


def map_entries(entries, count, store):
    maps = [entries[count + part].astype(jnp.float32).astype(jnp.int32) for part in range(2)]
    for entry in range(count):
        row = maps[entry // 8][entry % 8 : entry % 8 + 1]
        places = jnp.broadcast_to(row, (8, row.shape[1]))
        store(entry, mapped(entries[entry].astype(jnp.float32), places))


def tile_kernel(
    table, place, w_own, w_mate, vale, c_keep, c_y, c_core, c_diag, out,
    slab, far_v, far_c, c_all, pv, pc, image, arrived,
):
    sources, entries, _, width = vale.shape
    n_blocks = sources // 2
    count = entries - 2
    half_z = count - NSHIFT
    n_z = 2 * half_z
    my_ka, core = place[0], place[1] % 2
    my_y = my_ka // n_z
    shift = sum(jnp.where(table[by, 0] == my_ka, by, 0) for by in range(1, NSHIFT + 1))
    fetch = pltpu.make_async_copy(w_own, slab, arrived)
    fetch.start()

    def partner(y, entry):
        other = entry - shift
        crossed = jnp.logical_and(core == 0, other < NSHIFT)
        return jnp.where(crossed, 1 - y, y) * count + other

    def form(chunk):
        slot = chunk % far_v.shape[0]
        for y in range(2):
            for inner in range(CHUNK):
                block = chunk * CHUNK + inner

                def store(entry, value):
                    far_v[slot, y * count + entry, :, pl.ds(inner * width, width)] = value

                map_entries(vale.at[y * n_blocks + block], count, store)
        for y in range(2):
            for z in range(half_z):
                rows = pl.ds(64 * (y * half_z + z), 64)
                row = partner(y, z + NSHIFT)
                for inner in range(CHUNK):
                    block = chunk * CHUNK + inner
                    lanes = pl.ds(inner * width, width)
                    own = vale[y * n_blocks + block, z + NSHIFT].astype(jnp.float32)
                    pv[chunk, rows, lanes] = density(own, far_v[slot, row, :, lanes])

    def form_c():
        for side, (mine, other) in enumerate(((c_keep, c_y), (c_core, c_diag))):
            c_all[side, my_y] = mine[...]
            c_all[side, 1 - my_y] = other[...]
        for side in range(2):
            lanes = pl.ds(side * width, width)
            for y in range(2):

                def store(entry, value):
                    far_c[y * count + entry, :, lanes] = value

                map_entries(c_all.at[side, y], count, store)
            for y in range(2):
                for z in range(half_z):
                    own = c_all[side, y, z + NSHIFT].astype(jnp.float32)
                    rows = pl.ds(64 * (y * half_z + z), 64)
                    pc[rows, lanes] = density(own, far_c[partner(y, z + NSHIFT), :, lanes])

    chunks = n_blocks // CHUNK
    form(0)
    fetch.wait()
    for chunk in range(chunks):
        if chunk + 1 < chunks:
            form(chunk + 1)
        else:
            form_c()
        span = pl.ds(chunk * CHUNK * width, CHUNK * width)
        for side, w_ref in enumerate((slab, w_mate)):
            lanes = pl.ds(side * width, width)
            term = last_dims(pv[chunk], w_ref[:, span])
            image[:, lanes] = term if chunk == 0 else image[:, lanes] + term

    low = lax.broadcasted_iota(jnp.int32, (64, 128), 1) < 64
    for y in range(2):
        for part in range(half_z // STEP_K):
            rows = pl.ds(64 * (y * half_z + part * STEP_K), 64 * STEP_K)
            full = last_dims(pc[rows, :], image[rows, :].astype(jnp.bfloat16))
            for pair in range(STEP_K // 2):
                base = 128 * pair
                strip = full[:, base : base + 128]
                tile = jnp.where(low, strip[base : base + 64], strip[base + 64 : base + 128])
                out[pl.ds(16 * y, 16), pl.ds(8 * part + 4 * pair, 4), :] = tile.reshape(16, 4, 128)


def tiles(table, place, w_own, w_mate, vale, c_keep, c_y, c_core, c_diag):
    sources, entries, _, width = vale.shape
    count = entries - 2
    grid_h = w_own.shape[1]
    half_z = count - NSHIFT
    rows = 2 * half_z * 64
    chunks = sources // 2 // CHUNK
    return pl.pallas_call(
        tile_kernel,
        in_specs=[SMEM, SMEM, ANY] + [VMEM] * 6,
        out_specs=VMEM,
        out_shape=jax.ShapeDtypeStruct((sources, 2 * half_z, 128), jnp.float32),
        scratch_shapes=[
            pltpu.VMEM(w_own.shape, jnp.bfloat16),
            pltpu.VMEM((2, 2 * count, 8, CHUNK * width), jnp.float32),
            pltpu.VMEM((2 * count, 8, 2 * width), jnp.float32),
            pltpu.VMEM((2, 2) + c_keep.shape, jnp.bfloat16),
            pltpu.VMEM((chunks, rows, CHUNK * width), jnp.bfloat16),
            pltpu.VMEM((rows, 2 * width), jnp.bfloat16),
            pltpu.VMEM((rows, 2 * width), jnp.float32),
            pltpu.SemaphoreType.DMA(()),
        ],
        compiler_params=pltpu.CompilerParams(vmem_limit_bytes=36 * 1024 * 1024),
    )(table, place, w_own, w_mate, vale, c_keep, c_y, c_core, c_diag)


def spread_kernel(place, cond_in, vale_in, gmap_in, out, cond, vale, gmap, arrived):
    width = cond.shape[2]
    fetches = [
        pltpu.make_async_copy(source, target, arrived.at[number])
        for number, (source, target) in enumerate(((cond_in, cond), (vale_in, vale), (gmap_in, gmap)))
    ]
    for fetch in fetches:
        fetch.start()
    for fetch in fetches:
        fetch.wait()
    places = (gmap[...] - place[1] * width).astype(jnp.float32).astype(jnp.bfloat16)
    places = jnp.broadcast_to(places, (8, width))
    for dest in range(out.shape[0]):
        out[dest, 0] = vale[0]
        out[dest, 1] = cond[0]
        out[dest, 2] = places


def spread(place, cond, vale, gmap, dests):
    return pl.pallas_call(
        spread_kernel,
        in_specs=[SMEM] + [ANY] * 3,
        out_specs=VMEM,
        out_shape=jax.ShapeDtypeStruct((dests, 3) + cond.shape[1:], jnp.bfloat16),
        scratch_shapes=[
            pltpu.VMEM(cond.shape, jnp.bfloat16),
            pltpu.VMEM(vale.shape, jnp.bfloat16),
            pltpu.VMEM(gmap.shape, jnp.int32),
            pltpu.SemaphoreType.DMA((3,)),
        ],
        compiler_params=pltpu.CompilerParams(vmem_limit_bytes=4 * 1024 * 1024),
    )(place, cond, vale, gmap)


def pack_kernel(place, got, v_out, keep, give):
    n_z, _, _, width = got.shape
    half_z = n_z // 2
    count = half_z + NSHIFT
    core = place[1] % 2
    row_id = lax.broadcasted_iota(jnp.int32, (8, width), 0)
    for half in range(2):
        spots = [(half * half_z + entry - NSHIFT) % n_z for entry in range(count)]
        packs = []
        for first in range(0, count, 8):
            rows = jnp.zeros((8, width), jnp.float32)
            for entry in range(first, min(first + 8, count)):
                rows = jnp.where(row_id == entry - first, got[spots[entry], 2].astype(jnp.float32), rows)
            packs.append(rows.astype(jnp.bfloat16))
        for mine, c_out in ((True, keep), (False, give)):

            @pl.when((core == half) == mine)
            def _(c_out=c_out, spots=spots, packs=packs):
                for part, rows in enumerate(packs):
                    c_out[count + part] = rows
                for entry, spot in enumerate(spots):
                    c_out[entry] = got[spot, 1]

        for dest in range(half, v_out.shape[0], 2):
            for part, rows in enumerate(packs):
                v_out[dest, count + part] = rows
            for entry, spot in enumerate(spots):
                v_out[dest, entry] = got[spot, 0]


def pack(place, got, dests):
    n_z, _, _, width = got.shape
    entries = n_z // 2 + NSHIFT + 2
    shape = (entries, 8, width)
    return pl.pallas_call(
        pack_kernel,
        in_specs=[SMEM, VMEM],
        out_specs=[VMEM] * 3,
        out_shape=[
            jax.ShapeDtypeStruct((dests,) + shape, jnp.bfloat16),
            jax.ShapeDtypeStruct(shape, jnp.bfloat16),
            jax.ShapeDtypeStruct(shape, jnp.bfloat16),
        ],
        compiler_params=pltpu.CompilerParams(vmem_limit_bytes=8 * 1024 * 1024),
    )(place, got)


def total_kernel(shares, out):
    sources, rows, _ = shares.shape
    for y in range(2):
        for core in range(2):
            first = y * (sources // 2) + core
            total = shares[first]
            for source in range(first + 2, first + sources // 2, 2):
                total = total + shares[source]
            for pair in range(rows // 4):
                strip = total[4 * pair : 4 * pair + 4]
                for odd in range(2):
                    z = core * (rows // 2) + 2 * pair + odd
                    out[z, pl.ds(4 * y, 4), :] = strip


def totals(shares):
    n_z = shares.shape[1]
    return pl.pallas_call(
        total_kernel,
        in_specs=[VMEM],
        out_specs=VMEM,
        out_shape=jax.ShapeDtypeStruct((n_z, 8, 128), jnp.float32),
        compiler_params=pltpu.CompilerParams(vmem_limit_bytes=4 * 1024 * 1024),
    )(shares)


def pick_kernel(table, place, rows, out):
    n_z = rows.shape[0]
    odd = place[0] % 2 == 1
    low = lax.broadcasted_iota(jnp.int32, (4, 128), 1) < 64
    for by in range(NSHIFT + 1):
        holder = table[by, 0]
        both = rows[holder % n_z]
        strip = jnp.where(holder // n_z == 0, both[:4], both[4:])
        turned = pltpu.roll(strip, 64, 1)
        left = jnp.where(odd, turned, strip)
        right = jnp.where(odd, strip, turned)
        for side in range(2):
            line = jnp.where(low[:1], left[2 * side : 2 * side + 1], right[2 * side + 1 : 2 * side + 2])
            out[by, :, pl.ds(128 * side, 128)] = line


def pick(table, place, rows):
    return pl.pallas_call(
        pick_kernel,
        in_specs=[SMEM, SMEM, VMEM],
        out_specs=VMEM,
        out_shape=jax.ShapeDtypeStruct((NSHIFT + 1, 1, 256), jnp.float32),
        compiler_params=pltpu.CompilerParams(vmem_limit_bytes=4 * 1024 * 1024),
    )(table, place, rows)


def per_device(cond, vale, screen, qtable, gmap):
    n_ka = lax.axis_size("ka")
    n_ga = lax.axis_size("ga")
    n_z = n_ka // 2
    my_ka = lax.axis_index("ka")
    my_ga = lax.axis_index("ga")
    place = jnp.stack([my_ka, my_ga]).astype(jnp.int32)
    swap_core = [(i, i ^ 1) for i in range(n_ga)]
    swap_y = [(i, i ^ n_z) for i in range(n_ka)]
    swap_both = [(k * n_ga + g, (k ^ n_z) * n_ga + (g ^ 1)) for k in range(n_ka) for g in range(n_ga)]
    along_z = [list(range(n_z)), list(range(n_z, n_ka))]
    planes = [
        [(y * n_z + z) * n_ga + g for y in range(2) for g in range(n_ga)] for z in range(n_z)
    ]

    slab = screen[0]
    slab_mate = lax.ppermute(slab, "ga", swap_core)

    sent = spread(place, cond, vale, gmap, n_z)
    got = lax.all_to_all(sent, "ka", 0, 0, axis_index_groups=along_z)

    v_sent, c_keep, c_give = pack(place, got, 2 * n_ga)
    c_y = lax.ppermute(c_keep, "ka", swap_y)
    c_core = lax.ppermute(c_give, "ga", swap_core)
    c_diag = lax.ppermute(c_give, ("ka", "ga"), swap_both)
    v_all = lax.all_to_all(v_sent, ("ka", "ga"), 0, 0, axis_index_groups=planes)

    part = tiles(qtable, place, slab, slab_mate, v_all, c_keep, c_y, c_core, c_diag)
    shares = lax.all_to_all(part, ("ka", "ga"), 0, 0, axis_index_groups=planes)
    rows = lax.all_to_all(totals(shares), "ka", 0, 0, axis_index_groups=along_z)
    return jnp.transpose(pick(qtable, place, rows), (1, 0, 2))


def solution(mesh):
    in_specs = (P("ka", None, "ga"), P("ka", None, "ga"), P("ka", "ga", None), P(), P("ka", "ga"))
    out_specs = P("ka", None, "ga")
    return jax.shard_map(
        per_device, mesh=mesh, in_specs=in_specs, out_specs=out_specs, check_vma=False
    )
```

time: 115 us -> 110 us (0.957)
  waiting for transfers between devices: 27.9 us -> 23.2 us
  Pallas kernels: 13.6 us -> 11.7 us
  starting transfers between devices: 38.1 us -> 39.8 us
  other arithmetic: 1.53 us -> 0.07 us
    ppermute x2 -> x3, waiting for transfers between devices: 18.2 us -> 13.1 us  [the longest x1 10.8 us: per_device(): c_y = lax.ppermute(c_keep, 'ka', swap_y)]
    pallas_call x2 -> x3, Pallas kernels: 12.7 us -> 10.2 us  [the longest x1 7.04 us: tiles(): pl.pallas_call(tile_kernel, in_specs=[SMEM, SMEM, ANY] + [VMEM] * 6, out_...]
    unnamed x4 -> x10, local copies, waits for them, and re-layouts: 1.59 us -> 3.65 us
    ppermute x2 -> x3, starting transfers between devices: 7.58 us -> 9.28 us  [the longest x1 4.81 us: per_device(): c_y = lax.ppermute(c_keep, 'ka', swap_y)]
  transfers between devices with their start and end apart: 5 -> 6, of which waited for: 3 -> 4; matrix products, arithmetic and copies ran while one was open for 0% -> 0% of each run, Pallas kernels for 1% -> 2%
where the time goes in v3:
time: 110 us; the launch traced here: 109 us
  starting transfers between devices  39.8 us (36%)
  blocking collectives  30.6 us (28%)
  waiting for transfers between devices  23.2 us (21%)
  Pallas kernels  11.7 us (11%)
  local copies, waits for them, and re-layouts  3.65 us (3%)
    all_to_all x1, blocking collectives, per_device(): rows = lax.all_to_all(totals(shares), 'ka', 0, 0, axis_index_groups=along_z)  16 us
    all_to_all x1, starting transfers between devices, per_device(): got = lax.all_to_all(sent, 'ka', 0, 0, axis_index_groups=along_z)  15.8 us
    all_to_all x1, blocking collectives, per_device(): shares = lax.all_to_all(part, ('ka', 'ga'), 0, 0, axis_index_groups=planes)  14.6 us
    all_to_all x1, starting transfers between devices, per_device(): v_all = lax.all_to_all(v_sent, ('ka', 'ga'), 0, 0, axis_index_groups=planes)  11.9 us
    ppermute x1, waiting for transfers between devices, per_device(): c_y = lax.ppermute(c_keep, 'ka', swap_y)  10.8 us
    all_to_all x1, waiting for transfers between devices, per_device(): got = lax.all_to_all(sent, 'ka', 0, 0, axis_index_groups=along_z)  9.68 us
    pallas_call x1, Pallas kernels, tiles(): pl.pallas_call(tile_kernel, in_specs=[SMEM, SMEM, ANY] + [VMEM] * 6, out_...  7.04 us
    ppermute x1, starting transfers between devices, per_device(): c_y = lax.ppermute(c_keep, 'ka', swap_y)  4.81 us
  transfers between devices with their start and end apart: 6, of which 4 were waited for; matrix products, arithmetic and copies ran while one was open for 0% of the time, Pallas kernels for 2%

profile of v3, /device:TPU:1, one launch (start us, length us, event | category | flops | bytes accessed | tf_op | source)
XLA Modules:
  0.0 109.1 jit_solution(16441033871480009771)
XLA Ops:
  0.0 0.0 copy-start.1
  0.0 0.1 pad_add_fusion.place
  0.1 0.0 copy-start.2
  0.1 0.7 copy-done.2
  0.8 0.0 copy-start.3
  0.8 0.7 copy-done.3
  1.5 0.0 copy-start.4
  1.5 0.7 copy-done.4
  2.1 1.3 %shard_map.55 = bf16[16,3,8,256]{3,2,1,0:T(8,128)(2,1)} custom-call(s32[2]{0:T(128)S(1)} %pad_add_fusion.place, bf16[1,8,256]{2,1,0:T(8,128)(2,1)S(1)} %copy-done.2, bf16[1,8,256]{2,1,0:T(8,128)(2,1)S(1)} %copy-done.3, s32[1,256]{1,0:T(1,128)S(1)} %copy-done.4), custom_call_target="tpu_custom_call" | custom-call | tf_op jit(solution)/shard_map/pallas_call | solution.py:175
  3.4 15.8 %all-to-all-start = ((bf16[16,3,8,256]{3,2,1,0:T(8,128)(2,1)}), bf16[16,3,8,256]{3,2,1,0:T(8,128)(2,1)S(1)}, u32[]{:S(2)}, u32[]{:S(2)}) async-start(bf16[16,3,8,256]{3,2,1,0:T(8,128)(2,1)} %shard_map.55), calls=%async_computation | async-start | bytes 393216 | tf_op jit(solution)/shard_map/all_to_all | solution.py:308
  19.2 2.9 %collective-permute-start = (bf16[256,4096]{1,0:T(8,128)(2,1)}, bf16[256,4096]{1,0:T(8,128)(2,1)}, u32[]{:S(2)}, u32[]{:S(2)}) collective-permute-start(bf16[256,4096]{1,0:T(8,128)(2,1)} %bitcast.4), channel_id=1, source_target_pairs={{0,1},{1,0},{2,3},{3,2},{4,5},{5,4},{6,7},{7,6},{8,9},{9,8},{10,11... | collective-permute-start | bytes 6291464 | tf_op jit(solution)/shard_map/ppermute | solution.py:305
  22.0 9.7 %all-to-all-done.got = bf16[16,3,8,256]{3,2,1,0:T(8,128)(2,1)S(1)} async-done(((bf16[16,3,8,256]{3,2,1,0:T(8,128)(2,1)}), bf16[16,3,8,256]{3,2,1,0:T(8,128)(2,1)S(1)}, u32[]{:S(2)}, u32[]{:S(2)}) %all-to-all-start) | async-done | bytes 196640 | tf_op jit(solution)/shard_map/all_to_all | solution.py:308
  31.7 1.9 %shard_map.56 = (bf16[32,12,8,256]{3,2,1,0:T(8,128)(2,1)}, bf16[12,8,256]{2,1,0:T(8,128)(2,1)S(1)}, bf16[12,8,256]{2,1,0:T(8,128)(2,1)S(1)}) custom-call(s32[2]{0:T(128)S(1)} %pad_add_fusion.place, bf16[16,3,8,256]{3,2,1,0:T(8,128)(2,1)S(1)} %all-to-all-done.got), custom_call_target="tpu_custom_call" | custom-call | tf_op jit(solution)/shard_map/pallas_call | solution.py:224
  33.6 11.9 %all-to-all-start.1 = ((bf16[32,12,8,256]{3,2,1,0:T(8,128)(2,1)}), bf16[32,12,8,256]{3,2,1,0:T(8,128)(2,1)S(1)}, u32[]{:S(2)}, u32[]{:S(2)}) async-start(bf16[32,12,8,256]{3,2,1,0:T(8,128)(2,1)} %get-tuple-element.8), calls=%async_computation.1 | async-start | bytes 3145728 | tf_op jit(solution)/shard_map/all_to_all | solution.py:314
  45.5 4.8 %collective-permute-start.1 = (bf16[12,8,256]{2,1,0:T(8,128)(2,1)S(1)}, bf16[12,8,256]{2,1,0:T(8,128)(2,1)S(1)}, u32[]{:S(2)}, u32[]{:S(2)}) collective-permute-start(bf16[12,8,256]{2,1,0:T(8,128)(2,1)S(1)} %get-tuple-element.9.c_keep), channel_id=1, source_target_pairs={{0,256},{16,272},{32,288},{48,304},{64,320},{80,336},{96,352},{112... | collective-permute-start | bytes 147464 | tf_op jit(solution)/shard_map/ppermute | solution.py:311
  50.3 2.4 %collective-permute-start.3 = (bf16[12,8,256]{2,1,0:T(8,128)(2,1)S(1)}, bf16[12,8,256]{2,1,0:T(8,128)(2,1)S(1)}, u32[]{:S(2)}, u32[]{:S(2)}) collective-permute-start(bf16[12,8,256]{2,1,0:T(8,128)(2,1)S(1)} %get-tuple-element.10), channel_id=1, source_target_pairs={{0,257},{1,256},{2,259},{3,258},{4,261},{5,260},{6,263},{7,262},{8... | collective-permute-start | bytes 147464 | tf_op jit(solution)/shard_map/ppermute | solution.py:313
  52.7 2.1 %collective-permute-start.2 = (bf16[12,8,256]{2,1,0:T(8,128)(2,1)S(1)}, bf16[12,8,256]{2,1,0:T(8,128)(2,1)S(1)}, u32[]{:S(2)}, u32[]{:S(2)}) collective-permute-start(bf16[12,8,256]{2,1,0:T(8,128)(2,1)S(1)} %get-tuple-element.10), channel_id=1, source_target_pairs={{0,1},{1,0},{2,3},{3,2},{4,5},{5,4},{6,7},{7,6},{8,9},{9,8},{10,11... | collective-permute-start | bytes 147464 | tf_op jit(solution)/shard_map/ppermute | solution.py:312
  54.8 10.8 %collective-permute-done.1.c_y = bf16[12,8,256]{2,1,0:T(8,128)(2,1)S(1)} collective-permute-done((bf16[12,8,256]{2,1,0:T(8,128)(2,1)S(1)}, bf16[12,8,256]{2,1,0:T(8,128)(2,1)S(1)}, u32[]{:S(2)}, u32[]{:S(2)}) %collective-permute-start.1) | collective-permute-done | bytes 49184 | tf_op jit(solution)/shard_map/ppermute | solution.py:311
  65.6 2.3 %collective-permute-done.3.c_diag = bf16[12,8,256]{2,1,0:T(8,128)(2,1)S(1)} collective-permute-done((bf16[12,8,256]{2,1,0:T(8,128)(2,1)S(1)}, bf16[12,8,256]{2,1,0:T(8,128)(2,1)S(1)}, u32[]{:S(2)}, u32[]{:S(2)}) %collective-permute-start.3) | collective-permute-done | bytes 49184 | tf_op jit(solution)/shard_map/ppermute | solution.py:313
  67.9 0.0 collective-permute-done.2.c_core
  67.9 0.0 collective-permute-done.w_mate
  67.9 0.5 all-to-all-done.1.vale
  68.4 0.0 copy-done.1
  68.4 0.0 copy-start
  68.4 1.6 %copy-done = bf16[1,256,4096]{2,1,0:T(8,128)(2,1)S(1)} copy-done((bf16[1,256,4096]{2,1,0:T(8,128)(2,1)S(1)}, bf16[1,256,4096]{2,1,0:T(8,128)(2,1)}, u32[]{:S(2)}) %copy-start) | copy-done | bytes 2097176
  69.9 7.0 %shard_map.57 = f32[32,16,128]{2,1,0:T(8,128)S(1)} custom-call(s32[32,32]{1,0:T(8,128)S(1)} %copy-done.1, s32[2]{0:T(128)S(1)} %pad_add_fusion.place, bf16[256,4096]{1,0:T(8,128)(2,1)S(1)} %bitcast.5, bf16[256,4096]{1,0:T(8,128)(2,1)} %collective-permute-done.w_mate, bf16[32,12,8,256]{3,2,1,0:T(8,128)(2,1)S(1)} %all-to-all-done.1.vale, ...), custom_call_target="tpu_custom_call" | custom-call | tf_op jit(solution)/shard_map/pallas_call | solution.py:137
  77.0 14.6 %all_to_all.20.shares = f32[32,16,128]{2,1,0:T(8,128)S(1)} all-to-all(f32[32,16,128]{2,1,0:T(8,128)S(1)} %shard_map.57), channel_id=1, replica_groups={{0,1,2,3,4,5,6,7,8,9,10,11,12,13,14,15,256,257,258,259,260,261,262,263,..., dimensions={0} | all-to-all | bytes 524288 | tf_op jit(solution)/shard_map/all_to_all | solution.py:317
  91.6 16.0 %all_to_all.21.rows = f32[16,8,128]{2,1,0:T(8,128)S(1)} all-to-all(f32[16,8,128]{2,1,0:T(8,128)S(1)} %shard_map.58), channel_id=1, replica_groups={{0,16,32,48,64,80,96,112,128,144,160,176,192,208,224,240},{256,272,288,..., dimensions={0} | all-to-all | bytes 131072 | tf_op jit(solution)/shard_map/all_to_all | solution.py:318
  107.6 1.5 %shard_map.59 = f32[3,1,256]{2,1,0:T(1,128)} custom-call(s32[32,32]{1,0:T(8,128)S(1)} %copy-done.1, s32[2]{0:T(128)S(1)} %pad_add_fusion.place, f32[16,8,128]{2,1,0:T(8,128)S(1)} %all_to_all.21.rows), custom_call_target="tpu_custom_call" | custom-call | tf_op jit(solution)/shard_map/pallas_call | solution.py:280
  (1 shorter events, 0.0 us)
Async XLA Ops:
  0.0 68.4 %copy-start.1 = (s32[32,32]{1,0:T(8,128)S(1)}, s32[32,32]{1,0:T(8,128)}, u32[]{:S(2)}) copy-start(s32[32,32]{1,0:T(8,128)} %table.3) | copy-start | bytes 12292
  0.1 0.7 copy-start.2
  0.8 0.7 copy-start.3
  1.5 0.7 copy-start.4
  3.4 28.3 %all-to-all-start = ((bf16[16,3,8,256]{3,2,1,0:T(8,128)(2,1)}), bf16[16,3,8,256]{3,2,1,0:T(8,128)(2,1)S(1)}, u32[]{:S(2)}, u32[]{:S(2)}) async-start(bf16[16,3,8,256]{3,2,1,0:T(8,128)(2,1)} %shard_map.55), calls=%async_computation | async-start | bytes 393216 | tf_op jit(solution)/shard_map/all_to_all | solution.py:308
  19.2 48.7 %collective-permute-start = (bf16[256,4096]{1,0:T(8,128)(2,1)}, bf16[256,4096]{1,0:T(8,128)(2,1)}, u32[]{:S(2)}, u32[]{:S(2)}) collective-permute-start(bf16[256,4096]{1,0:T(8,128)(2,1)} %bitcast.4), channel_id=1, source_target_pairs={{0,1},{1,0},{2,3},{3,2},{4,5},{5,4},{6,7},{7,6},{8,9},{9,8},{10,11... | collective-permute-start | bytes 6291464 | tf_op jit(solution)/shard_map/ppermute | solution.py:305
  33.6 34.8 %all-to-all-start.1 = ((bf16[32,12,8,256]{3,2,1,0:T(8,128)(2,1)}), bf16[32,12,8,256]{3,2,1,0:T(8,128)(2,1)S(1)}, u32[]{:S(2)}, u32[]{:S(2)}) async-start(bf16[32,12,8,256]{3,2,1,0:T(8,128)(2,1)} %get-tuple-element.8), calls=%async_computation.1 | async-start | bytes 3145728 | tf_op jit(solution)/shard_map/all_to_all | solution.py:314
  45.5 20.1 %collective-permute-start.1 = (bf16[12,8,256]{2,1,0:T(8,128)(2,1)S(1)}, bf16[12,8,256]{2,1,0:T(8,128)(2,1)S(1)}, u32[]{:S(2)}, u32[]{:S(2)}) collective-permute-start(bf16[12,8,256]{2,1,0:T(8,128)(2,1)S(1)} %get-tuple-element.9.c_keep), channel_id=1, source_target_pairs={{0,256},{16,272},{32,288},{48,304},{64,320},{80,336},{96,352},{112... | collective-permute-start | bytes 147464 | tf_op jit(solution)/shard_map/ppermute | solution.py:311
  50.3 17.6 %collective-permute-start.3 = (bf16[12,8,256]{2,1,0:T(8,128)(2,1)S(1)}, bf16[12,8,256]{2,1,0:T(8,128)(2,1)S(1)}, u32[]{:S(2)}, u32[]{:S(2)}) collective-permute-start(bf16[12,8,256]{2,1,0:T(8,128)(2,1)S(1)} %get-tuple-element.10), channel_id=1, source_target_pairs={{0,257},{1,256},{2,259},{3,258},{4,261},{5,260},{6,263},{7,262},{8... | collective-permute-start | bytes 147464 | tf_op jit(solution)/shard_map/ppermute | solution.py:313
  52.7 15.2 %collective-permute-start.2 = (bf16[12,8,256]{2,1,0:T(8,128)(2,1)S(1)}, bf16[12,8,256]{2,1,0:T(8,128)(2,1)S(1)}, u32[]{:S(2)}, u32[]{:S(2)}) collective-permute-start(bf16[12,8,256]{2,1,0:T(8,128)(2,1)S(1)} %get-tuple-element.10), channel_id=1, source_target_pairs={{0,1},{1,0},{2,3},{3,2},{4,5},{5,4},{6,7},{7,6},{8,9},{9,8},{10,11... | collective-permute-start | bytes 147464 | tf_op jit(solution)/shard_map/ppermute | solution.py:312
  68.4 1.6 %copy-start = (bf16[1,256,4096]{2,1,0:T(8,128)(2,1)S(1)}, bf16[1,256,4096]{2,1,0:T(8,128)(2,1)}, u32[]{:S(2)}) copy-start(bf16[1,256,4096]{2,1,0:T(8,128)(2,1)} %param.7) | copy-start | bytes 6291460

commit v4 on v3

--- a/solution.py
+++ b/solution.py
@@ -10,7 +10,12 @@
 CHUNK = 2
 VMEM = pl.BlockSpec(memory_space=pltpu.VMEM)
 SMEM = pl.BlockSpec(memory_space=pltpu.SMEM)
+HBM = pl.BlockSpec(memory_space=pltpu.HBM)
 ANY = pl.BlockSpec(memory_space=pl.ANY)
+
+
+def in_hbm(*arrays):
+    return [pltpu.with_memory_space_constraint(array, pltpu.HBM) for array in arrays]
 
 
 def last_dims(a, b):
@@ -35,28 +40,53 @@
     return jnp.concatenate(sides, axis=1)
 
 
-def map_entries(entries, count, store):
-    maps = [entries[count + part].astype(jnp.float32).astype(jnp.int32) for part in range(2)]
+def entry_lanes(entry, width):
+    return pl.ds(entry * width, width)
+
+
+def map_entries(packed, count, width, store):
+    maps = []
+    for first in range(0, 2 * count, 8):
+        lanes = pl.ds(count * width + 16 * first, 128)
+        maps.append(packed[:, lanes].astype(jnp.float32).astype(jnp.int32))
     for entry in range(count):
-        row = maps[entry // 8][entry % 8 : entry % 8 + 1]
-        places = jnp.broadcast_to(row, (8, row.shape[1]))
-        store(entry, mapped(entries[entry].astype(jnp.float32), places))
+        sides = []
+        for side in range(2):
+            row = 2 * entry + side
+            places = maps[row // 8][row % 8 : row % 8 + 1]
+            sides.append(jnp.broadcast_to(places, (8, 128)))
+        source = packed[:, entry_lanes(entry, width)].astype(jnp.float32)
+        store(entry, mapped(source, jnp.concatenate(sides, axis=1)))
 
 
 def tile_kernel(
-    table, place, w_own, w_mate, vale, c_keep, c_y, c_core, c_diag, out,
-    slab, far_v, far_c, c_all, pv, pc, image, arrived,
+    table, place, w_own, w_mate, vale, c_keep, c_y, c_core, c_diag, out, plan,
+    slabs, far_v, far_c, c_all, pv, pc, image, arrived,
 ):
-    sources, entries, _, width = vale.shape
-    n_blocks = sources // 2
-    count = entries - 2
-    half_z = count - NSHIFT
-    n_z = 2 * half_z
+    n_blocks = vale.shape[0] // 2
+    width = w_own.shape[0]
+    n_z = out.shape[1]
+    half_z = n_z // 2
+    count = half_z + NSHIFT
     my_ka, core = place[0], place[1] % 2
     my_y = my_ka // n_z
     shift = sum(jnp.where(table[by, 0] == my_ka, by, 0) for by in range(1, NSHIFT + 1))
-    fetch = pltpu.make_async_copy(w_own, slab, arrived)
-    fetch.start()
+    fetches = [
+        pltpu.make_async_copy(source, slabs.at[side], arrived.at[side])
+        for side, source in enumerate((w_own, w_mate))
+    ]
+    for fetch in fetches:
+        fetch.start()
+
+    upper = lax.broadcasted_iota(jnp.int32, (8, 128), 0) >= 4
+    for z in range(n_z):
+        tile = jnp.full((8, 128), -1, jnp.int32)
+        for by in range(NSHIFT + 1):
+            holder = table[by, 0]
+            row = jnp.where(upper, holder - n_z, holder)
+            tile = jnp.where(row == z, by, tile)
+        plan[z] = tile
+    plan[n_z] = jnp.full((8, 128), my_ka % 2, jnp.int32)
 
     def partner(y, entry):
         other = entry - shift
@@ -72,7 +102,7 @@
                 def store(entry, value):
                     far_v[slot, y * count + entry, :, pl.ds(inner * width, width)] = value
 
-                map_entries(vale.at[y * n_blocks + block], count, store)
+                map_entries(vale.at[y * n_blocks + block], count, width, store)
         for y in range(2):
             for z in range(half_z):
                 rows = pl.ds(64 * (y * half_z + z), 64)
@@ -80,7 +110,8 @@
                 for inner in range(CHUNK):
                     block = chunk * CHUNK + inner
                     lanes = pl.ds(inner * width, width)
-                    own = vale[y * n_blocks + block, z + NSHIFT].astype(jnp.float32)
+                    own = vale[y * n_blocks + block, :, entry_lanes(z + NSHIFT, width)]
+                    own = own.astype(jnp.float32)
                     pv[chunk, rows, lanes] = density(own, far_v[slot, row, :, lanes])
 
     def form_c():
@@ -94,25 +125,26 @@
                 def store(entry, value):
                     far_c[y * count + entry, :, lanes] = value
 
-                map_entries(c_all.at[side, y], count, store)
+                map_entries(c_all.at[side, y], count, width, store)
             for y in range(2):
                 for z in range(half_z):
-                    own = c_all[side, y, z + NSHIFT].astype(jnp.float32)
+                    own = c_all[side, y, :, entry_lanes(z + NSHIFT, width)].astype(jnp.float32)
                     rows = pl.ds(64 * (y * half_z + z), 64)
                     pc[rows, lanes] = density(own, far_c[partner(y, z + NSHIFT), :, lanes])
 
     chunks = n_blocks // CHUNK
     form(0)
-    fetch.wait()
+    for fetch in fetches:
+        fetch.wait()
     for chunk in range(chunks):
         if chunk + 1 < chunks:
             form(chunk + 1)
         else:
             form_c()
         span = pl.ds(chunk * CHUNK * width, CHUNK * width)
-        for side, w_ref in enumerate((slab, w_mate)):
+        for side in range(2):
             lanes = pl.ds(side * width, width)
-            term = last_dims(pv[chunk], w_ref[:, span])
+            term = last_dims(pv[chunk], slabs[side, :, span])
             image[:, lanes] = term if chunk == 0 else image[:, lanes] + term
 
     low = lax.broadcasted_iota(jnp.int32, (64, 128), 1) < 64
@@ -128,29 +160,32 @@
 
 
 def tiles(table, place, w_own, w_mate, vale, c_keep, c_y, c_core, c_diag):
-    sources, entries, _, width = vale.shape
-    count = entries - 2
-    grid_h = w_own.shape[1]
-    half_z = count - NSHIFT
-    rows = 2 * half_z * 64
+    sources = vale.shape[0]
+    width, grid_h = w_own.shape
+    n_z = table.shape[0] // 2
+    count = n_z // 2 + NSHIFT
+    rows = n_z * 64
     chunks = sources // 2 // CHUNK
     return pl.pallas_call(
         tile_kernel,
-        in_specs=[SMEM, SMEM, ANY] + [VMEM] * 6,
-        out_specs=VMEM,
-        out_shape=jax.ShapeDtypeStruct((sources, 2 * half_z, 128), jnp.float32),
+        in_specs=[SMEM, SMEM, HBM, ANY] + [VMEM] * 5,
+        out_specs=[VMEM, VMEM],
+        out_shape=[
+            jax.ShapeDtypeStruct((sources, n_z, 128), jnp.float32),
+            jax.ShapeDtypeStruct((n_z + 1, 8, 128), jnp.int32),
+        ],
         scratch_shapes=[
-            pltpu.VMEM(w_own.shape, jnp.bfloat16),
+            pltpu.VMEM((2,) + w_own.shape, jnp.bfloat16),
             pltpu.VMEM((2, 2 * count, 8, CHUNK * width), jnp.float32),
             pltpu.VMEM((2 * count, 8, 2 * width), jnp.float32),
             pltpu.VMEM((2, 2) + c_keep.shape, jnp.bfloat16),
             pltpu.VMEM((chunks, rows, CHUNK * width), jnp.bfloat16),
             pltpu.VMEM((rows, 2 * width), jnp.bfloat16),
             pltpu.VMEM((rows, 2 * width), jnp.float32),
-            pltpu.SemaphoreType.DMA(()),
+            pltpu.SemaphoreType.DMA((2,)),
         ],
         compiler_params=pltpu.CompilerParams(vmem_limit_bytes=36 * 1024 * 1024),
-    )(table, place, w_own, w_mate, vale, c_keep, c_y, c_core, c_diag)
+    )(table, place, *in_hbm(w_own), w_mate, vale, c_keep, c_y, c_core, c_diag)
 
 
 def spread_kernel(place, cond_in, vale_in, gmap_in, out, cond, vale, gmap, arrived):
@@ -163,20 +198,21 @@
         fetch.start()
     for fetch in fetches:
         fetch.wait()
-    places = (gmap[...] - place[1] * width).astype(jnp.float32).astype(jnp.bfloat16)
-    places = jnp.broadcast_to(places, (8, width))
+    places = (gmap[...] - place[1] * width).astype(jnp.float32)
+    top = lax.broadcasted_iota(jnp.int32, (8, 128), 0) == 0
+    places = jnp.where(top, places[:, :128], places[:, 128:]).astype(jnp.bfloat16)
     for dest in range(out.shape[0]):
-        out[dest, 0] = vale[0]
-        out[dest, 1] = cond[0]
-        out[dest, 2] = places
+        out[dest, :, :width] = vale[0]
+        out[dest, :, width : 2 * width] = cond[0]
+        out[dest, :, 2 * width :] = places
 
 
 def spread(place, cond, vale, gmap, dests):
     return pl.pallas_call(
         spread_kernel,
-        in_specs=[SMEM] + [ANY] * 3,
+        in_specs=[SMEM] + [HBM] * 3,
         out_specs=VMEM,
-        out_shape=jax.ShapeDtypeStruct((dests, 3) + cond.shape[1:], jnp.bfloat16),
+        out_shape=jax.ShapeDtypeStruct((dests, 8, 2 * cond.shape[2] + 128), jnp.bfloat16),
         scratch_shapes=[
             pltpu.VMEM(cond.shape, jnp.bfloat16),
             pltpu.VMEM(vale.shape, jnp.bfloat16),
@@ -184,43 +220,55 @@
             pltpu.SemaphoreType.DMA((3,)),
         ],
         compiler_params=pltpu.CompilerParams(vmem_limit_bytes=4 * 1024 * 1024),
-    )(place, cond, vale, gmap)
+    )(place, *in_hbm(cond, vale, gmap))
 
 
 def pack_kernel(place, got, v_out, keep, give):
-    n_z, _, _, width = got.shape
+    n_z = got.shape[0]
+    width = (got.shape[2] - 128) // 2
     half_z = n_z // 2
     count = half_z + NSHIFT
     core = place[1] % 2
-    row_id = lax.broadcasted_iota(jnp.int32, (8, width), 0)
+    row_id = lax.broadcasted_iota(jnp.int32, (8, 128), 0)
     for half in range(2):
         spots = [(half * half_z + entry - NSHIFT) % n_z for entry in range(count)]
-        packs = []
-        for first in range(0, count, 8):
-            rows = jnp.zeros((8, width), jnp.float32)
-            for entry in range(first, min(first + 8, count)):
-                rows = jnp.where(row_id == entry - first, got[spots[entry], 2].astype(jnp.float32), rows)
-            packs.append(rows.astype(jnp.bfloat16))
+        maps = []
+        for first in range(0, count, 4):
+            tile = jnp.zeros((8, 128), jnp.float32)
+            for entry in range(first, min(first + 4, count)):
+                pair = got[spots[entry], :, 2 * width :].astype(jnp.float32)
+                tile = jnp.where(row_id == 2 * (entry - first), pair[0:1], tile)
+                tile = jnp.where(row_id == 2 * (entry - first) + 1, pair[1:2], tile)
+            maps.append(tile.astype(jnp.bfloat16))
+
+        def fill(write, column, spots=spots, maps=maps):
+            for entry, spot in enumerate(spots):
+                write(entry_lanes(entry, width), got[spot, :, column * width : (column + 1) * width])
+            for number, tile in enumerate(maps):
+                write(pl.ds(count * width + 128 * number, 128), tile)
+
         for mine, c_out in ((True, keep), (False, give)):
 
             @pl.when((core == half) == mine)
-            def _(c_out=c_out, spots=spots, packs=packs):
-                for part, rows in enumerate(packs):
-                    c_out[count + part] = rows
-                for entry, spot in enumerate(spots):
-                    c_out[entry] = got[spot, 1]
+            def _(c_out=c_out, fill=fill):
+                def write(lanes, value):
+                    c_out[:, lanes] = value
+
+                fill(write, 1)
 
         for dest in range(half, v_out.shape[0], 2):
-            for part, rows in enumerate(packs):
-                v_out[dest, count + part] = rows
-            for entry, spot in enumerate(spots):
-                v_out[dest, entry] = got[spot, 0]
+
+            def write(lanes, value, dest=dest):
+                v_out[dest, :, lanes] = value
+
+            fill(write, 0)
 
 
 def pack(place, got, dests):
-    n_z, _, _, width = got.shape
-    entries = n_z // 2 + NSHIFT + 2
-    shape = (entries, 8, width)
+    n_z = got.shape[0]
+    width = (got.shape[2] - 128) // 2
+    count = n_z // 2 + NSHIFT
+    shape = (8, count * width + 128 * (-(-count // 4)))
     return pl.pallas_call(
         pack_kernel,
         in_specs=[SMEM, VMEM],
@@ -260,30 +308,31 @@
     )(shares)
 
 
-def pick_kernel(table, place, rows, out):
+def pick_kernel(plan, rows, out):
     n_z = rows.shape[0]
-    odd = place[0] % 2 == 1
-    low = lax.broadcasted_iota(jnp.int32, (4, 128), 1) < 64
+    odd = plan[n_z, 0:4] == 1
+    low = lax.broadcasted_iota(jnp.int32, (1, 128), 1) < 64
     for by in range(NSHIFT + 1):
-        holder = table[by, 0]
-        both = rows[holder % n_z]
-        strip = jnp.where(holder // n_z == 0, both[:4], both[4:])
+        both = jnp.zeros((8, 128), jnp.float32)
+        for z in range(n_z):
+            both = jnp.where(plan[z] == by, rows[z], both)
+        strip = both[:4] + both[4:]
         turned = pltpu.roll(strip, 64, 1)
         left = jnp.where(odd, turned, strip)
         right = jnp.where(odd, strip, turned)
         for side in range(2):
-            line = jnp.where(low[:1], left[2 * side : 2 * side + 1], right[2 * side + 1 : 2 * side + 2])
+            line = jnp.where(low, left[2 * side : 2 * side + 1], right[2 * side + 1 : 2 * side + 2])
             out[by, :, pl.ds(128 * side, 128)] = line
 
 
-def pick(table, place, rows):
+def pick(plan, rows):
     return pl.pallas_call(
         pick_kernel,
-        in_specs=[SMEM, SMEM, VMEM],
+        in_specs=[VMEM, VMEM],
         out_specs=VMEM,
         out_shape=jax.ShapeDtypeStruct((NSHIFT + 1, 1, 256), jnp.float32),
         compiler_params=pltpu.CompilerParams(vmem_limit_bytes=4 * 1024 * 1024),
-    )(table, place, rows)
+    )(plan, rows)
 
 
 def per_device(cond, vale, screen, qtable, gmap):
@@ -301,11 +350,11 @@
         [(y * n_z + z) * n_ga + g for y in range(2) for g in range(n_ga)] for z in range(n_z)
     ]
 
-    slab = screen[0]
-    slab_mate = lax.ppermute(slab, "ga", swap_core)
-
     sent = spread(place, cond, vale, gmap, n_z)
     got = lax.all_to_all(sent, "ka", 0, 0, axis_index_groups=along_z)
+
+    got, slab = lax.optimization_barrier((got, screen[0]))
+    slab_mate = lax.ppermute(slab, "ga", swap_core)
 
     v_sent, c_keep, c_give = pack(place, got, 2 * n_ga)
     c_y = lax.ppermute(c_keep, "ka", swap_y)
@@ -313,10 +362,10 @@
     c_diag = lax.ppermute(c_give, ("ka", "ga"), swap_both)
     v_all = lax.all_to_all(v_sent, ("ka", "ga"), 0, 0, axis_index_groups=planes)
 
-    part = tiles(qtable, place, slab, slab_mate, v_all, c_keep, c_y, c_core, c_diag)
+    part, plan = tiles(qtable, place, slab, slab_mate, v_all, c_keep, c_y, c_core, c_diag)
     shares = lax.all_to_all(part, ("ka", "ga"), 0, 0, axis_index_groups=planes)
     rows = lax.all_to_all(totals(shares), "ka", 0, 0, axis_index_groups=along_z)
-    return jnp.transpose(pick(qtable, place, rows), (1, 0, 2))
+    return jnp.transpose(pick(plan, rows), (1, 0, 2))
 
 
 def solution(mesh):

time: 110 us -> 106 us (0.964)
  blocking collectives: 30.6 us -> 57.7 us
  starting transfers between devices: 39.8 us -> 22.7 us
  waiting for transfers between devices: 23.2 us -> 12.8 us
  local copies, waits for them, and re-layouts: 3.65 us -> 0.01 us
    all_to_all x0 -> x1, blocking collectives: none -> 27.8 us  [per_device(): got = lax.all_to_all(sent, 'ka', 0, 0, axis_index_groups=along_z)]
    all_to_all x1 -> x0, starting transfers between devices: 15.8 us -> none  [per_device(): got = lax.all_to_all(sent, 'ka', 0, 0, axis_index_groups=along_z)]
    all_to_all x1 -> x0, waiting for transfers between devices: 9.68 us -> none  [per_device(): got = lax.all_to_all(sent, 'ka', 0, 0, axis_index_groups=along_z)]
    all_to_all x1, starting transfers between devices: 11.9 us -> 7.2 us  [per_device(): v_all = lax.all_to_all(v_sent, ('ka', 'ga'), 0, 0, axis_index_groups=planes)]
    unnamed x10 -> x2, local copies, waits for them, and re-layouts: 3.65 us -> 0.01 us
    ppermute x1, starting transfers between devices: 2.87 us -> 6.27 us  [per_device(): slab_mate = lax.ppermute(slab, 'ga', swap_core)]
  transfers between devices with their start and end apart: 6 -> 5, of which waited for: 4 -> 3; matrix products, arithmetic and copies ran while one was open for 0% -> 0% of each run, Pallas kernels for 2% -> 2%
where the time goes in v4:
time: 106 us; the launch traced here: 105 us
  blocking collectives  57.7 us (54%)
  starting transfers between devices  22.7 us (21%)
  waiting for transfers between devices  12.8 us (12%)
  Pallas kernels  11.8 us (11%)
    all_to_all x1, blocking collectives, per_device(): got = lax.all_to_all(sent, 'ka', 0, 0, axis_index_groups=along_z)  27.8 us
    all_to_all x1, blocking collectives, per_device(): rows = lax.all_to_all(totals(shares), 'ka', 0, 0, axis_index_groups=along_z)  15.4 us
    all_to_all x1, blocking collectives, per_device(): shares = lax.all_to_all(part, ('ka', 'ga'), 0, 0, axis_index_groups=planes)  14.5 us
    ppermute x1, waiting for transfers between devices, per_device(): c_y = lax.ppermute(c_keep, 'ka', swap_y)  10.1 us
    pallas_call x1, Pallas kernels, tiles(): pl.pallas_call(tile_kernel, in_specs=[SMEM, SMEM, HBM, ANY] + [VMEM] * 5,...  8.03 us
    all_to_all x1, starting transfers between devices, per_device(): v_all = lax.all_to_all(v_sent, ('ka', 'ga'), 0, 0, axis_index_groups=planes)  7.2 us
    ppermute x1, starting transfers between devices, per_device(): slab_mate = lax.ppermute(slab, 'ga', swap_core)  6.27 us
    ppermute x1, starting transfers between devices, per_device(): c_y = lax.ppermute(c_keep, 'ka', swap_y)  4.81 us
  transfers between devices with their start and end apart: 5, of which 3 were waited for; matrix products, arithmetic and copies ran while one was open for 0% of the time, Pallas kernels for 2%

profile of v4, /device:TPU:1, one launch (start us, length us, event | category | flops | bytes accessed | tf_op | source)
XLA Modules:
  0.0 105.2 jit_solution(18003217565978471070)
XLA Ops:
  0.0 0.0 copy-start
  0.0 0.1 pad_add_fusion.place
  0.1 1.3 %shard_map.55 = bf16[16,8,640]{2,1,0:T(8,128)(2,1)S(1)} custom-call(s32[2]{0:T(128)S(1)} %pad_add_fusion.place, bf16[1,8,256]{2,1,0:T(8,128)(2,1)} %cond_in.1, bf16[1,8,256]{2,1,0:T(8,128)(2,1)} %vale_in.1, s32[1,256]{1,0:T(1,128)} %gmap_in.1), custom_call_target="tpu_custom_call" | custom-call | tf_op jit(solution)/shard_map/pallas_call | solution.py:211
  1.4 27.8 %all_to_all.20.got = bf16[16,8,640]{2,1,0:T(8,128)(2,1)S(1)} all-to-all(bf16[16,8,640]{2,1,0:T(8,128)(2,1)S(1)} %shard_map.55), channel_id=1, replica_groups={{0,16,32,48,64,80,96,112,128,144,160,176,192,208,224,240},{256,272,288,..., dimensions={0} | all-to-all | bytes 327680 | tf_op jit(solution)/shard_map/all_to_all | solution.py:354
  29.1 6.3 %collective-permute-start = (bf16[256,4096]{1,0:T(8,128)(2,1)}, bf16[256,4096]{1,0:T(8,128)(2,1)}, u32[]{:S(2)}, u32[]{:S(2)}) collective-permute-start(bf16[256,4096]{1,0:T(8,128)(2,1)} %bitcast.4), channel_id=1, source_target_pairs={{0,1},{1,0},{2,3},{3,2},{4,5},{5,4},{6,7},{7,6},{8,9},{9,8},{10,11... | collective-permute-start | bytes 6291464 | tf_op jit(solution)/shard_map/ppermute | solution.py:357
  35.4 1.8 %shard_map.56 = (bf16[32,8,2944]{2,1,0:T(8,128)(2,1)}, bf16[8,2944]{1,0:T(8,128)(2,1)S(1)}, bf16[8,2944]{1,0:T(8,128)(2,1)S(1)}) custom-call(s32[2]{0:T(128)S(1)} %pad_add_fusion.place, bf16[16,8,640]{2,1,0:T(8,128)(2,1)S(1)} %all_to_all.20.got), custom_call_target="tpu_custom_call" | custom-call | tf_op jit(solution)/shard_map/pallas_call | solution.py:272
  37.2 7.2 %all-to-all-start.1 = ((bf16[32,8,2944]{2,1,0:T(8,128)(2,1)}), bf16[32,8,2944]{2,1,0:T(8,128)(2,1)S(1)}, u32[]{:S(2)}, u32[]{:S(2)}) async-start(bf16[32,8,2944]{2,1,0:T(8,128)(2,1)} %get-tuple-element.14), calls=%async_computation.1 | async-start | bytes 3014656 | tf_op jit(solution)/shard_map/all_to_all | solution.py:363
  44.4 4.8 %collective-permute-start.1 = (bf16[8,2944]{1,0:T(8,128)(2,1)S(1)}, bf16[8,2944]{1,0:T(8,128)(2,1)S(1)}, u32[]{:S(2)}, u32[]{:S(2)}) collective-permute-start(bf16[8,2944]{1,0:T(8,128)(2,1)S(1)} %get-tuple-element.15.c_keep), channel_id=1, source_target_pairs={{0,256},{16,272},{32,288},{48,304},{64,320},{80,336},{96,352},{112... | collective-permute-start | bytes 141320 | tf_op jit(solution)/shard_map/ppermute | solution.py:360
  49.2 2.4 %collective-permute-start.3 = (bf16[8,2944]{1,0:T(8,128)(2,1)S(1)}, bf16[8,2944]{1,0:T(8,128)(2,1)S(1)}, u32[]{:S(2)}, u32[]{:S(2)}) collective-permute-start(bf16[8,2944]{1,0:T(8,128)(2,1)S(1)} %get-tuple-element.16), channel_id=1, source_target_pairs={{0,257},{1,256},{2,259},{3,258},{4,261},{5,260},{6,263},{7,262},{8... | collective-permute-start | bytes 141320 | tf_op jit(solution)/shard_map/ppermute | solution.py:362
  51.6 2.1 %collective-permute-start.2 = (bf16[8,2944]{1,0:T(8,128)(2,1)S(1)}, bf16[8,2944]{1,0:T(8,128)(2,1)S(1)}, u32[]{:S(2)}, u32[]{:S(2)}) collective-permute-start(bf16[8,2944]{1,0:T(8,128)(2,1)S(1)} %get-tuple-element.16), channel_id=1, source_target_pairs={{0,1},{1,0},{2,3},{3,2},{4,5},{5,4},{6,7},{7,6},{8,9},{9,8},{10,11... | collective-permute-start | bytes 141320 | tf_op jit(solution)/shard_map/ppermute | solution.py:361
  53.7 10.1 %collective-permute-done.1.c_y = bf16[8,2944]{1,0:T(8,128)(2,1)S(1)} collective-permute-done((bf16[8,2944]{1,0:T(8,128)(2,1)S(1)}, bf16[8,2944]{1,0:T(8,128)(2,1)S(1)}, u32[]{:S(2)}, u32[]{:S(2)}) %collective-permute-start.1) | collective-permute-done | bytes 47136 | tf_op jit(solution)/shard_map/ppermute | solution.py:360
  63.8 2.2 %collective-permute-done.3.c_diag = bf16[8,2944]{1,0:T(8,128)(2,1)S(1)} collective-permute-done((bf16[8,2944]{1,0:T(8,128)(2,1)S(1)}, bf16[8,2944]{1,0:T(8,128)(2,1)S(1)}, u32[]{:S(2)}, u32[]{:S(2)}) %collective-permute-start.3) | collective-permute-done | bytes 47136 | tf_op jit(solution)/shard_map/ppermute | solution.py:362
  66.0 0.0 collective-permute-done.2.c_core
  66.0 0.5 all-to-all-done.1.vale
  66.5 0.0 collective-permute-done.w_mate
  66.5 0.0 copy-done
  66.5 8.0 %shard_map.57 = (f32[32,16,128]{2,1,0:T(8,128)S(1)}, s32[17,8,128]{2,1,0:T(8,128)S(1)}) custom-call(s32[32,32]{1,0:T(8,128)S(1)} %copy-done, s32[2]{0:T(128)S(1)} %pad_add_fusion.place, bf16[256,4096]{1,0:T(8,128)(2,1)} %bitcast.5, bf16[256,4096]{1,0:T(8,128)(2,1)} %collective-permute-done.w_mate, bf16[32,8,2944]{2,1,0:T(8,128)(2,1)S(1)} %all-to-all-done.1.vale, ...), custom_call_target="tpu_custom_call" | custom-call | tf_op jit(solution)/shard_map/pallas_call | solution.py:169
  74.6 14.5 %all_to_all.21.shares = f32[32,16,128]{2,1,0:T(8,128)S(1)} all-to-all(f32[32,16,128]{2,1,0:T(8,128)S(1)} %get-tuple-element.18), channel_id=1, replica_groups={{0,1,2,3,4,5,6,7,8,9,10,11,12,13,14,15,256,257,258,259,260,261,262,263,..., dimensions={0} | all-to-all | bytes 524288 | tf_op jit(solution)/shard_map/all_to_all | solution.py:366
  89.1 15.4 %all_to_all.22.rows = f32[16,8,128]{2,1,0:T(8,128)S(1)} all-to-all(f32[16,8,128]{2,1,0:T(8,128)S(1)} %shard_map.58), channel_id=1, replica_groups={{0,16,32,48,64,80,96,112,128,144,160,176,192,208,224,240},{256,272,288,..., dimensions={0} | all-to-all | bytes 131072 | tf_op jit(solution)/shard_map/all_to_all | solution.py:367
  104.5 0.7 shard_map.59
  (1 shorter events, 0.0 us)
Async XLA Ops:
  0.0 66.5 %copy-start = (s32[32,32]{1,0:T(8,128)S(1)}, s32[32,32]{1,0:T(8,128)}, u32[]{:S(2)}) copy-start(s32[32,32]{1,0:T(8,128)} %table.1) | copy-start | bytes 12292
  29.1 37.4 %collective-permute-start = (bf16[256,4096]{1,0:T(8,128)(2,1)}, bf16[256,4096]{1,0:T(8,128)(2,1)}, u32[]{:S(2)}, u32[]{:S(2)}) collective-permute-start(bf16[256,4096]{1,0:T(8,128)(2,1)} %bitcast.4), channel_id=1, source_target_pairs={{0,1},{1,0},{2,3},{3,2},{4,5},{5,4},{6,7},{7,6},{8,9},{9,8},{10,11... | collective-permute-start | bytes 6291464 | tf_op jit(solution)/shard_map/ppermute | solution.py:357
  37.2 29.3 %all-to-all-start.1 = ((bf16[32,8,2944]{2,1,0:T(8,128)(2,1)}), bf16[32,8,2944]{2,1,0:T(8,128)(2,1)S(1)}, u32[]{:S(2)}, u32[]{:S(2)}) async-start(bf16[32,8,2944]{2,1,0:T(8,128)(2,1)} %get-tuple-element.14), calls=%async_computation.1 | async-start | bytes 3014656 | tf_op jit(solution)/shard_map/all_to_all | solution.py:363
  44.4 19.4 %collective-permute-start.1 = (bf16[8,2944]{1,0:T(8,128)(2,1)S(1)}, bf16[8,2944]{1,0:T(8,128)(2,1)S(1)}, u32[]{:S(2)}, u32[]{:S(2)}) collective-permute-start(bf16[8,2944]{1,0:T(8,128)(2,1)S(1)} %get-tuple-element.15.c_keep), channel_id=1, source_target_pairs={{0,256},{16,272},{32,288},{48,304},{64,320},{80,336},{96,352},{112... | collective-permute-start | bytes 141320 | tf_op jit(solution)/shard_map/ppermute | solution.py:360
  49.2 16.8 %collective-permute-start.3 = (bf16[8,2944]{1,0:T(8,128)(2,1)S(1)}, bf16[8,2944]{1,0:T(8,128)(2,1)S(1)}, u32[]{:S(2)}, u32[]{:S(2)}) collective-permute-start(bf16[8,2944]{1,0:T(8,128)(2,1)S(1)} %get-tuple-element.16), channel_id=1, source_target_pairs={{0,257},{1,256},{2,259},{3,258},{4,261},{5,260},{6,263},{7,262},{8... | collective-permute-start | bytes 141320 | tf_op jit(solution)/shard_map/ppermute | solution.py:362
  51.6 14.4 %collective-permute-start.2 = (bf16[8,2944]{1,0:T(8,128)(2,1)S(1)}, bf16[8,2944]{1,0:T(8,128)(2,1)S(1)}, u32[]{:S(2)}, u32[]{:S(2)}) collective-permute-start(bf16[8,2944]{1,0:T(8,128)(2,1)S(1)} %get-tuple-element.16), channel_id=1, source_target_pairs={{0,1},{1,0},{2,3},{3,2},{4,5},{5,4},{6,7},{7,6},{8,9},{9,8},{10,11... | collective-permute-start | bytes 141320 | tf_op jit(solution)/shard_map/ppermute | solution.py:361

commit v5 on v4

--- a/solution.py
+++ b/solution.py
@@ -61,7 +61,7 @@
 
 def tile_kernel(
     table, place, w_own, w_mate, vale, c_keep, c_y, c_core, c_diag, out, plan,
-    slabs, far_v, far_c, c_all, pv, pc, image, arrived,
+    slabs, far_v, far_c, c_all, pv, pc, image, wide, arrived,
 ):
     n_blocks = vale.shape[0] // 2
     width = w_own.shape[0]
@@ -71,6 +71,8 @@
     my_ka, core = place[0], place[1] % 2
     my_y = my_ka // n_z
     shift = sum(jnp.where(table[by, 0] == my_ka, by, 0) for by in range(1, NSHIFT + 1))
+    chunks = n_blocks // CHUNK
+    spans = [pl.ds(chunk * CHUNK * width, CHUNK * width) for chunk in range(chunks)]
     fetches = [
         pltpu.make_async_copy(source, slabs.at[side], arrived.at[side])
         for side, source in enumerate((w_own, w_mate))
@@ -78,15 +80,14 @@
     for fetch in fetches:
         fetch.start()
 
-    upper = lax.broadcasted_iota(jnp.int32, (8, 128), 0) >= 4
+    upper = lax.broadcasted_iota(jnp.int32, (4, 128), 0) >= 2
     for z in range(n_z):
-        tile = jnp.full((8, 128), -1, jnp.int32)
+        tile = jnp.full((4, 128), -1, jnp.int32)
         for by in range(NSHIFT + 1):
             holder = table[by, 0]
             row = jnp.where(upper, holder - n_z, holder)
             tile = jnp.where(row == z, by, tile)
         plan[z] = tile
-    plan[n_z] = jnp.full((8, 128), my_ka % 2, jnp.int32)
 
     def partner(y, entry):
         other = entry - shift
@@ -132,7 +133,6 @@
                     rows = pl.ds(64 * (y * half_z + z), 64)
                     pc[rows, lanes] = density(own, far_c[partner(y, z + NSHIFT), :, lanes])
 
-    chunks = n_blocks // CHUNK
     form(0)
     for fetch in fetches:
         fetch.wait()
@@ -141,10 +141,9 @@
             form(chunk + 1)
         else:
             form_c()
-        span = pl.ds(chunk * CHUNK * width, CHUNK * width)
         for side in range(2):
             lanes = pl.ds(side * width, width)
-            term = last_dims(pv[chunk], slabs[side, :, span])
+            term = last_dims(pv[chunk], slabs[side, :, spans[chunk]])
             image[:, lanes] = term if chunk == 0 else image[:, lanes] + term
 
     low = lax.broadcasted_iota(jnp.int32, (64, 128), 1) < 64
@@ -156,7 +155,8 @@
                 base = 128 * pair
                 strip = full[:, base : base + 128]
                 tile = jnp.where(low, strip[base : base + 64], strip[base + 64 : base + 128])
-                out[pl.ds(16 * y, 16), pl.ds(8 * part + 4 * pair, 4), :] = tile.reshape(16, 4, 128)
+                wide[pl.ds(16 * y, 16), pl.ds(8 * part + 4 * pair, 4), :] = tile.reshape(16, 4, 128)
+    out[...] = wide[...].astype(jnp.bfloat16)
 
 
 def tiles(table, place, w_own, w_mate, vale, c_keep, c_y, c_core, c_diag):
@@ -171,8 +171,8 @@
         in_specs=[SMEM, SMEM, HBM, ANY] + [VMEM] * 5,
         out_specs=[VMEM, VMEM],
         out_shape=[
-            jax.ShapeDtypeStruct((sources, n_z, 128), jnp.float32),
-            jax.ShapeDtypeStruct((n_z + 1, 8, 128), jnp.int32),
+            jax.ShapeDtypeStruct((sources, n_z, 128), jnp.bfloat16),
+            jax.ShapeDtypeStruct((n_z, 4, 128), jnp.int32),
         ],
         scratch_shapes=[
             pltpu.VMEM((2,) + w_own.shape, jnp.bfloat16),
@@ -182,6 +182,7 @@
             pltpu.VMEM((chunks, rows, CHUNK * width), jnp.bfloat16),
             pltpu.VMEM((rows, 2 * width), jnp.bfloat16),
             pltpu.VMEM((rows, 2 * width), jnp.float32),
+            pltpu.VMEM((sources, n_z, 128), jnp.float32),
             pltpu.SemaphoreType.DMA((2,)),
         ],
         compiler_params=pltpu.CompilerParams(vmem_limit_bytes=36 * 1024 * 1024),
@@ -223,13 +224,14 @@
     )(place, *in_hbm(cond, vale, gmap))
 
 
-def pack_kernel(place, got, v_out, keep, give):
+def pack_kernel(place, got, v_out, keep, give, block, sent):
     n_z = got.shape[0]
     width = (got.shape[2] - 128) // 2
     half_z = n_z // 2
     count = half_z + NSHIFT
     core = place[1] % 2
     row_id = lax.broadcasted_iota(jnp.int32, (8, 128), 0)
+    started = []
     for half in range(2):
         spots = [(half * half_z + entry - NSHIFT) % n_z for entry in range(count)]
         maps = []
@@ -241,27 +243,29 @@
                 tile = jnp.where(row_id == 2 * (entry - first) + 1, pair[1:2], tile)
             maps.append(tile.astype(jnp.bfloat16))
 
-        def fill(write, column, spots=spots, maps=maps):
+        def fill(target, column, spots=spots, maps=maps):
             for entry, spot in enumerate(spots):
-                write(entry_lanes(entry, width), got[spot, :, column * width : (column + 1) * width])
+                lanes = pl.ds(column * width, width)
+                target[:, entry_lanes(entry, width)] = got[spot, :, lanes]
             for number, tile in enumerate(maps):
-                write(pl.ds(count * width + 128 * number, 128), tile)
-
+                target[:, pl.ds(count * width + 128 * number, 128)] = tile
+
+        fill(block.at[half], 0)
+        copies = [
+            pltpu.make_async_copy(block.at[half], v_out.at[dest], sent.at[dest])
+            for dest in range(half, v_out.shape[0], 2)
+        ]
+        for copy in copies:
+            copy.start()
+        started += copies
         for mine, c_out in ((True, keep), (False, give)):
 
             @pl.when((core == half) == mine)
             def _(c_out=c_out, fill=fill):
-                def write(lanes, value):
-                    c_out[:, lanes] = value
-
-                fill(write, 1)
-
-        for dest in range(half, v_out.shape[0], 2):
-
-            def write(lanes, value, dest=dest):
-                v_out[dest, :, lanes] = value
-
-            fill(write, 0)
+                fill(c_out, 1)
+
+    for copy in started:
+        copy.wait()
 
 
 def pack(place, got, dests):
@@ -272,29 +276,39 @@
     return pl.pallas_call(
         pack_kernel,
         in_specs=[SMEM, VMEM],
-        out_specs=[VMEM] * 3,
+        out_specs=[ANY, VMEM, VMEM],
         out_shape=[
             jax.ShapeDtypeStruct((dests,) + shape, jnp.bfloat16),
             jax.ShapeDtypeStruct(shape, jnp.bfloat16),
             jax.ShapeDtypeStruct(shape, jnp.bfloat16),
         ],
+        scratch_shapes=[
+            pltpu.VMEM((2,) + shape, jnp.bfloat16),
+            pltpu.SemaphoreType.DMA((dests,)),
+        ],
         compiler_params=pltpu.CompilerParams(vmem_limit_bytes=8 * 1024 * 1024),
     )(place, got)
 
 
 def total_kernel(shares, out):
     sources, rows, _ = shares.shape
-    for y in range(2):
-        for core in range(2):
+    low = lax.broadcasted_iota(jnp.int32, (1, 128), 1) < 64
+    for core in range(2):
+        sums = []
+        for y in range(2):
             first = y * (sources // 2) + core
-            total = shares[first]
+            total = shares[first].astype(jnp.float32)
             for source in range(first + 2, first + sources // 2, 2):
-                total = total + shares[source]
-            for pair in range(rows // 4):
-                strip = total[4 * pair : 4 * pair + 4]
-                for odd in range(2):
-                    z = core * (rows // 2) + 2 * pair + odd
-                    out[z, pl.ds(4 * y, 4), :] = strip
+                total = total + shares[source].astype(jnp.float32)
+            sums.append((total, pltpu.roll(total, 64, 1)))
+        for pair in range(rows // 4):
+            for odd in range(2):
+                lines = []
+                for strip, turned in sums:
+                    left, right = (turned, strip) if odd else (strip, turned)
+                    for row in (4 * pair, 4 * pair + 2):
+                        lines.append(jnp.where(low, left[row : row + 1], right[row + 1 : row + 2]))
+                out[core * (rows // 2) + 2 * pair + odd] = jnp.concatenate(lines, axis=0)
 
 
 def totals(shares):
@@ -303,26 +317,19 @@
         total_kernel,
         in_specs=[VMEM],
         out_specs=VMEM,
-        out_shape=jax.ShapeDtypeStruct((n_z, 8, 128), jnp.float32),
+        out_shape=jax.ShapeDtypeStruct((n_z, 4, 128), jnp.float32),
         compiler_params=pltpu.CompilerParams(vmem_limit_bytes=4 * 1024 * 1024),
     )(shares)
 
 
 def pick_kernel(plan, rows, out):
-    n_z = rows.shape[0]
-    odd = plan[n_z, 0:4] == 1
-    low = lax.broadcasted_iota(jnp.int32, (1, 128), 1) < 64
     for by in range(NSHIFT + 1):
-        both = jnp.zeros((8, 128), jnp.float32)
-        for z in range(n_z):
+        both = jnp.zeros((4, 128), jnp.float32)
+        for z in range(rows.shape[0]):
             both = jnp.where(plan[z] == by, rows[z], both)
-        strip = both[:4] + both[4:]
-        turned = pltpu.roll(strip, 64, 1)
-        left = jnp.where(odd, turned, strip)
-        right = jnp.where(odd, strip, turned)
+        pair = both[:2] + both[2:]
         for side in range(2):
-            line = jnp.where(low, left[2 * side : 2 * side + 1], right[2 * side + 1 : 2 * side + 2])
-            out[by, :, pl.ds(128 * side, 128)] = line
+            out[by, :, pl.ds(128 * side, 128)] = pair[side : side + 1]
 
 
 def pick(plan, rows):
@@ -350,11 +357,11 @@
         [(y * n_z + z) * n_ga + g for y in range(2) for g in range(n_ga)] for z in range(n_z)
     ]
 
+    slab = screen[0]
+    slab_mate = lax.ppermute(slab, "ga", swap_core)
+
     sent = spread(place, cond, vale, gmap, n_z)
     got = lax.all_to_all(sent, "ka", 0, 0, axis_index_groups=along_z)
-
-    got, slab = lax.optimization_barrier((got, screen[0]))
-    slab_mate = lax.ppermute(slab, "ga", swap_core)
 
     v_sent, c_keep, c_give = pack(place, got, 2 * n_ga)
     c_y = lax.ppermute(c_keep, "ka", swap_y)

time: 106 us -> 105 us (level)
  blocking collectives: 57.7 us -> 52.4 us
  starting transfers between devices: 22.7 us -> 27.4 us
    all_to_all x1, blocking collectives: 27.8 us -> 22.2 us  [per_device(): got = lax.all_to_all(sent, 'ka', 0, 0, axis_index_groups=along_z)]
    ppermute x1, starting transfers between devices: 6.27 us -> 8.91 us  [per_device(): slab_mate = lax.ppermute(slab, 'ga', swap_core)]
    all_to_all x1, starting transfers between devices: 7.2 us -> 9.2 us  [per_device(): v_all = lax.all_to_all(v_sent, ('ka', 'ga'), 0, 0, axis_index_groups=planes)]
    all_to_all x1, blocking collectives: 15.4 us -> 16.9 us  [per_device(): rows = lax.all_to_all(totals(shares), 'ka', 0, 0, axis_index_groups=along_z)]
    all_to_all x1, blocking collectives: 14.5 us -> 13.2 us  [per_device(): shares = lax.all_to_all(part, ('ka', 'ga'), 0, 0, axis_index_groups=planes)]
  transfers between devices with their start and end apart: 5 -> 5, of which waited for: 3 -> 3; matrix products, arithmetic and copies ran while one was open for 0% -> 0% of each run, Pallas kernels for 2% -> 3%
where the time goes in v5:
time: 105 us
  blocking collectives  52.4 us (50%)
  starting transfers between devices  27.4 us (26%)
  waiting for transfers between devices  12.8 us (12%)
  Pallas kernels  11.9 us (11%)
    all_to_all x1, blocking collectives, per_device(): got = lax.all_to_all(sent, 'ka', 0, 0, axis_index_groups=along_z)  22.2 us
    all_to_all x1, blocking collectives, per_device(): rows = lax.all_to_all(totals(shares), 'ka', 0, 0, axis_index_groups=along_z)  16.9 us
    all_to_all x1, blocking collectives, per_device(): shares = lax.all_to_all(part, ('ka', 'ga'), 0, 0, axis_index_groups=planes)  13.2 us
    ppermute x1, waiting for transfers between devices, per_device(): c_y = lax.ppermute(c_keep, 'ka', swap_y)  10.1 us
    all_to_all x1, starting transfers between devices, per_device(): v_all = lax.all_to_all(v_sent, ('ka', 'ga'), 0, 0, axis_index_groups=planes)  9.2 us
    ppermute x1, starting transfers between devices, per_device(): slab_mate = lax.ppermute(slab, 'ga', swap_core)  8.91 us
    pallas_call x1, Pallas kernels, tiles(): pl.pallas_call(tile_kernel, in_specs=[SMEM, SMEM, HBM, ANY] + [VMEM] * 5,...  7.92 us
    ppermute x1, starting transfers between devices, per_device(): c_y = lax.ppermute(c_keep, 'ka', swap_y)  4.81 us
  transfers between devices with their start and end apart: 5, of which 3 were waited for; matrix products, arithmetic and copies ran while one was open for 0% of the time, Pallas kernels for 3%

profile of v5, /device:TPU:1, one launch (start us, length us, event | category | flops | bytes accessed | tf_op | source)
XLA Modules:
  0.0 104.6 jit_solution(8920795905378894840)
XLA Ops:
  0.0 0.0 copy-start
  0.0 8.9 %collective-permute-start = (bf16[256,4096]{1,0:T(8,128)(2,1)}, bf16[256,4096]{1,0:T(8,128)(2,1)}, u32[]{:S(2)}, u32[]{:S(2)}) collective-permute-start(bf16[256,4096]{1,0:T(8,128)(2,1)} %bitcast.4), channel_id=1, source_target_pairs={{0,1},{1,0},{2,3},{3,2},{4,5},{5,4},{6,7},{7,6},{8,9},{9,8},{10,11... | collective-permute-start | bytes 6291464 | tf_op jit(solution)/shard_map/ppermute | solution.py:361
  8.9 0.1 pad_add_fusion.place
  9.0 1.3 %shard_map.55 = bf16[16,8,640]{2,1,0:T(8,128)(2,1)S(1)} custom-call(s32[2]{0:T(128)S(1)} %pad_add_fusion.place, bf16[1,8,256]{2,1,0:T(8,128)(2,1)} %cond_in.1, bf16[1,8,256]{2,1,0:T(8,128)(2,1)} %vale_in.1, s32[1,256]{1,0:T(1,128)} %gmap_in.1), custom_call_target="tpu_custom_call" | custom-call | tf_op jit(solution)/shard_map/pallas_call | solution.py:212
  10.3 22.2 %all_to_all.20.got = bf16[16,8,640]{2,1,0:T(8,128)(2,1)S(1)} all-to-all(bf16[16,8,640]{2,1,0:T(8,128)(2,1)S(1)} %shard_map.55), channel_id=1, replica_groups={{0,16,32,48,64,80,96,112,128,144,160,176,192,208,224,240},{256,272,288,..., dimensions={0} | all-to-all | bytes 327680 | tf_op jit(solution)/shard_map/all_to_all | solution.py:364
  32.5 2.0 %shard_map.56 = (bf16[32,8,2944]{2,1,0:T(8,128)(2,1)}, bf16[8,2944]{1,0:T(8,128)(2,1)S(1)}, bf16[8,2944]{1,0:T(8,128)(2,1)S(1)}) custom-call(s32[2]{0:T(128)S(1)} %pad_add_fusion.place, bf16[16,8,640]{2,1,0:T(8,128)(2,1)S(1)} %all_to_all.20.got), custom_call_target="tpu_custom_call" | custom-call | tf_op jit(solution)/shard_map/pallas_call | solution.py:276
  34.5 9.2 %all-to-all-start.1 = ((bf16[32,8,2944]{2,1,0:T(8,128)(2,1)}), bf16[32,8,2944]{2,1,0:T(8,128)(2,1)S(1)}, u32[]{:S(2)}, u32[]{:S(2)}) async-start(bf16[32,8,2944]{2,1,0:T(8,128)(2,1)} %get-tuple-element.10), calls=%async_computation.1 | async-start | bytes 3014656 | tf_op jit(solution)/shard_map/all_to_all | solution.py:370
  43.7 4.8 %collective-permute-start.1 = (bf16[8,2944]{1,0:T(8,128)(2,1)S(1)}, bf16[8,2944]{1,0:T(8,128)(2,1)S(1)}, u32[]{:S(2)}, u32[]{:S(2)}) collective-permute-start(bf16[8,2944]{1,0:T(8,128)(2,1)S(1)} %get-tuple-element.11.c_keep), channel_id=1, source_target_pairs={{0,256},{16,272},{32,288},{48,304},{64,320},{80,336},{96,352},{112... | collective-permute-start | bytes 141320 | tf_op jit(solution)/shard_map/ppermute | solution.py:367
  48.5 2.4 %collective-permute-start.3 = (bf16[8,2944]{1,0:T(8,128)(2,1)S(1)}, bf16[8,2944]{1,0:T(8,128)(2,1)S(1)}, u32[]{:S(2)}, u32[]{:S(2)}) collective-permute-start(bf16[8,2944]{1,0:T(8,128)(2,1)S(1)} %get-tuple-element.12), channel_id=1, source_target_pairs={{0,257},{1,256},{2,259},{3,258},{4,261},{5,260},{6,263},{7,262},{8... | collective-permute-start | bytes 141320 | tf_op jit(solution)/shard_map/ppermute | solution.py:369
  50.9 2.1 %collective-permute-start.2 = (bf16[8,2944]{1,0:T(8,128)(2,1)S(1)}, bf16[8,2944]{1,0:T(8,128)(2,1)S(1)}, u32[]{:S(2)}, u32[]{:S(2)}) collective-permute-start(bf16[8,2944]{1,0:T(8,128)(2,1)S(1)} %get-tuple-element.12), channel_id=1, source_target_pairs={{0,1},{1,0},{2,3},{3,2},{4,5},{5,4},{6,7},{7,6},{8,9},{9,8},{10,11... | collective-permute-start | bytes 141320 | tf_op jit(solution)/shard_map/ppermute | solution.py:368
  53.0 10.1 %collective-permute-done.1.c_y = bf16[8,2944]{1,0:T(8,128)(2,1)S(1)} collective-permute-done((bf16[8,2944]{1,0:T(8,128)(2,1)S(1)}, bf16[8,2944]{1,0:T(8,128)(2,1)S(1)}, u32[]{:S(2)}, u32[]{:S(2)}) %collective-permute-start.1) | collective-permute-done | bytes 47136 | tf_op jit(solution)/shard_map/ppermute | solution.py:367
  63.1 2.2 %collective-permute-done.3.c_diag = bf16[8,2944]{1,0:T(8,128)(2,1)S(1)} collective-permute-done((bf16[8,2944]{1,0:T(8,128)(2,1)S(1)}, bf16[8,2944]{1,0:T(8,128)(2,1)S(1)}, u32[]{:S(2)}, u32[]{:S(2)}) %collective-permute-start.3) | collective-permute-done | bytes 47136 | tf_op jit(solution)/shard_map/ppermute | solution.py:369
  65.3 0.0 collective-permute-done.2.c_core
  65.3 0.5 all-to-all-done.1.vale
  65.8 0.0 collective-permute-done.w_mate
  65.8 0.0 copy-done
  65.8 7.9 %shard_map.57 = (bf16[32,16,128]{2,1,0:T(8,128)(2,1)S(1)}, s32[16,4,128]{2,1,0:T(4,128)S(1)}) custom-call(s32[32,32]{1,0:T(8,128)S(1)} %copy-done, s32[2]{0:T(128)S(1)} %pad_add_fusion.place, bf16[256,4096]{1,0:T(8,128)(2,1)} %bitcast.5, bf16[256,4096]{1,0:T(8,128)(2,1)} %collective-permute-done.w_mate, bf16[32,8,2944]{2,1,0:T(8,128)(2,1)S(1)} %all-to-all-done.1.vale, ...), custom_call_target="tpu_custom_call" | custom-call | tf_op jit(solution)/shard_map/pallas_call | solution.py:169
  73.8 13.2 %all_to_all.21.shares = bf16[32,16,128]{2,1,0:T(8,128)(2,1)S(1)} all-to-all(bf16[32,16,128]{2,1,0:T(8,128)(2,1)S(1)} %get-tuple-element.14), channel_id=1, replica_groups={{0,1,2,3,4,5,6,7,8,9,10,11,12,13,14,15,256,257,258,259,260,261,262,263,..., dimensions={0} | all-to-all | bytes 262144 | tf_op jit(solution)/shard_map/all_to_all | solution.py:373
  87.0 0.1 shard_map.58
  87.1 16.9 %all_to_all.22.rows = f32[16,4,128]{2,1,0:T(4,128)S(1)} all-to-all(f32[16,4,128]{2,1,0:T(4,128)S(1)} %shard_map.58), channel_id=1, replica_groups={{0,16,32,48,64,80,96,112,128,144,160,176,192,208,224,240},{256,272,288,..., dimensions={0} | all-to-all | bytes 65536 | tf_op jit(solution)/shard_map/all_to_all | solution.py:374
  104.0 0.6 shard_map.59
Async XLA Ops:
  0.0 65.8 %copy-start = (s32[32,32]{1,0:T(8,128)S(1)}, s32[32,32]{1,0:T(8,128)}, u32[]{:S(2)}) copy-start(s32[32,32]{1,0:T(8,128)} %table.1) | copy-start | bytes 12292
  0.0 65.8 %collective-permute-start = (bf16[256,4096]{1,0:T(8,128)(2,1)}, bf16[256,4096]{1,0:T(8,128)(2,1)}, u32[]{:S(2)}, u32[]{:S(2)}) collective-permute-start(bf16[256,4096]{1,0:T(8,128)(2,1)} %bitcast.4), channel_id=1, source_target_pairs={{0,1},{1,0},{2,3},{3,2},{4,5},{5,4},{6,7},{7,6},{8,9},{9,8},{10,11... | collective-permute-start | bytes 6291464 | tf_op jit(solution)/shard_map/ppermute | solution.py:361
  34.5 31.3 %all-to-all-start.1 = ((bf16[32,8,2944]{2,1,0:T(8,128)(2,1)}), bf16[32,8,2944]{2,1,0:T(8,128)(2,1)S(1)}, u32[]{:S(2)}, u32[]{:S(2)}) async-start(bf16[32,8,2944]{2,1,0:T(8,128)(2,1)} %get-tuple-element.10), calls=%async_computation.1 | async-start | bytes 3014656 | tf_op jit(solution)/shard_map/all_to_all | solution.py:370
  43.7 19.4 %collective-permute-start.1 = (bf16[8,2944]{1,0:T(8,128)(2,1)S(1)}, bf16[8,2944]{1,0:T(8,128)(2,1)S(1)}, u32[]{:S(2)}, u32[]{:S(2)}) collective-permute-start(bf16[8,2944]{1,0:T(8,128)(2,1)S(1)} %get-tuple-element.11.c_keep), channel_id=1, source_target_pairs={{0,256},{16,272},{32,288},{48,304},{64,320},{80,336},{96,352},{112... | collective-permute-start | bytes 141320 | tf_op jit(solution)/shard_map/ppermute | solution.py:367
  48.5 16.8 %collective-permute-start.3 = (bf16[8,2944]{1,0:T(8,128)(2,1)S(1)}, bf16[8,2944]{1,0:T(8,128)(2,1)S(1)}, u32[]{:S(2)}, u32[]{:S(2)}) collective-permute-start(bf16[8,2944]{1,0:T(8,128)(2,1)S(1)} %get-tuple-element.12), channel_id=1, source_target_pairs={{0,257},{1,256},{2,259},{3,258},{4,261},{5,260},{6,263},{7,262},{8... | collective-permute-start | bytes 141320 | tf_op jit(solution)/shard_map/ppermute | solution.py:369
  50.9 14.4 %collective-permute-start.2 = (bf16[8,2944]{1,0:T(8,128)(2,1)S(1)}, bf16[8,2944]{1,0:T(8,128)(2,1)S(1)}, u32[]{:S(2)}, u32[]{:S(2)}) collective-permute-start(bf16[8,2944]{1,0:T(8,128)(2,1)S(1)} %get-tuple-element.12), channel_id=1, source_target_pairs={{0,1},{1,0},{2,3},{3,2},{4,5},{5,4},{6,7},{7,6},{8,9},{9,8},{10,11... | collective-permute-start | bytes 141320 | tf_op jit(solution)/shard_map/ppermute | solution.py:368

commit v6 on v5

v6 whole, which is shorter than its diff:
```python
import jax
import jax.numpy as jnp
from jax import lax
from jax.experimental import pallas as pl
from jax.experimental.pallas import tpu as pltpu
from jax.sharding import PartitionSpec as P

NSHIFT = 2
STEP_K = 4
CHUNK = 2
VMEM = pl.BlockSpec(memory_space=pltpu.VMEM)
SMEM = pl.BlockSpec(memory_space=pltpu.SMEM)
HBM = pl.BlockSpec(memory_space=pltpu.HBM)
ANY = pl.BlockSpec(memory_space=pl.ANY)


def in_hbm(*arrays):
    return [pltpu.with_memory_space_constraint(array, pltpu.HBM) for array in arrays]


def last_dims(a, b):
    return lax.dot_general(a, b, (((1,), (1,)), ((), ())), preferred_element_type=jnp.float32)


def density(own, far):
    product = own[:, None, :] * far[None, :, :]
    return product.reshape(64, own.shape[-1]).astype(jnp.bfloat16)


def lane_gather(source, places):
    return jnp.take_along_axis(source, places, axis=1, mode="promise_in_bounds")


def mapped(source, places):
    low, high = source[:, :128], source[:, 128:]
    sides = []
    for part in (places[:, :128], places[:, 128:]):
        inner = part & 127
        sides.append(jnp.where(part < 128, lane_gather(low, inner), lane_gather(high, inner)))
    return jnp.concatenate(sides, axis=1)


def entry_lanes(entry, width):
    return pl.ds(entry * width, width)


def map_entries(packed, count, width, store):
    maps = []
    for first in range(0, 2 * count, 8):
        lanes = pl.ds(count * width + 16 * first, 128)
        maps.append(packed[:, lanes].astype(jnp.float32).astype(jnp.int32))
    for entry in range(count):
        sides = []
        for side in range(2):
            row = 2 * entry + side
            places = maps[row // 8][row % 8 : row % 8 + 1]
            sides.append(jnp.broadcast_to(places, (8, 128)))
        source = packed[:, entry_lanes(entry, width)].astype(jnp.float32)
        store(entry, mapped(source, jnp.concatenate(sides, axis=1)))


def tile_kernel(
    table, place, w_own, w_mate, vale, c_keep, c_y, c_core, c_diag, out, plan,
    slabs, far_v, far_c, c_all, pv, pc, image, wide, arrived,
):
    blocks = vale.shape[0] // 2
    width = w_own.shape[0]
    n_z = plan.shape[0]
    my_ka, core = place[0], place[1] % 2
    my_y = my_ka // n_z
    shift = sum(jnp.where(table[by, 0] == my_ka, by, 0) for by in range(1, NSHIFT + 1))
    fetches = [
        pltpu.make_async_copy(
            source.at[:, pl.ds(pl.multiple_of((2 * block + core) * width, width), width)],
            slabs.at[side, :, pl.ds(block * width, width)],
            arrived.at[side, block],
        )
        for block in range(blocks)
        for side, source in enumerate((w_own, w_mate))
    ]
    for fetch in fetches:
        fetch.start()

    upper = lax.broadcasted_iota(jnp.int32, (4, 128), 0) >= 2
    for z in range(n_z):
        tile = jnp.full((4, 128), -1, jnp.int32)
        for by in range(NSHIFT + 1):
            holder = table[by, 0]
            row = jnp.where(upper, holder - n_z, holder)
            tile = jnp.where(row == z, by, tile)
        plan[z] = tile

    def partner(k):
        return jnp.where(k < shift, k - shift + 2 * n_z, k - shift)

    def form(chunk):
        slot = chunk % far_v.shape[0]
        for y in range(2):
            for inner in range(CHUNK):
                source = y * blocks + chunk * CHUNK + inner

                def store(z, value):
                    far_v[slot, y * n_z + z, :, pl.ds(inner * width, width)] = value

                map_entries(vale.at[source], n_z, width, store)
        for k in range(2 * n_z):
            for inner in range(CHUNK):
                source = k // n_z * blocks + chunk * CHUNK + inner
                lanes = pl.ds(inner * width, width)
                own = vale[source, :, entry_lanes(k % n_z, width)].astype(jnp.float32)
                pv[chunk, pl.ds(64 * k, 64), lanes] = density(own, far_v[slot, partner(k), :, lanes])

    def form_c():
        for side, (mine, other) in enumerate(((c_keep, c_y), (c_core, c_diag))):
            c_all[side, my_y] = mine[...]
            c_all[side, 1 - my_y] = other[...]
        for side in range(2):
            lanes = pl.ds(side * width, width)
            for y in range(2):

                def store(z, value):
                    far_c[y * n_z + z, :, lanes] = value

                map_entries(c_all.at[side, y], n_z, width, store)
            for k in range(2 * n_z):
                own = c_all[side, k // n_z, :, entry_lanes(k % n_z, width)].astype(jnp.float32)
                pc[pl.ds(64 * k, 64), lanes] = density(own, far_c[partner(k), :, lanes])

    chunks = blocks // CHUNK
    form(0)
    for fetch in fetches:
        fetch.wait()
    for chunk in range(chunks):
        if chunk + 1 < chunks:
            form(chunk + 1)
        else:
            form_c()
        for side in range(2):
            lanes = pl.ds(side * width, width)
            term = last_dims(pv[chunk], slabs[side, :, pl.ds(chunk * CHUNK * width, CHUNK * width)])
            image[:, lanes] = term if chunk == 0 else image[:, lanes] + term

    low = lax.broadcasted_iota(jnp.int32, (64, 128), 1) < 64
    for y in range(2):
        for part in range(n_z // STEP_K):
            rows = pl.ds(64 * (y * n_z + part * STEP_K), 64 * STEP_K)
            full = last_dims(pc[rows, :], image[rows, :].astype(jnp.bfloat16))
            for pair in range(STEP_K // 2):
                base = 128 * pair
                strip = full[:, base : base + 128]
                tile = jnp.where(low, strip[base : base + 64], strip[base + 64 : base + 128])
                wide[pl.ds(16 * y, 16), pl.ds(8 * part + 4 * pair, 4), :] = tile.reshape(16, 4, 128)
    out[...] = wide[...].astype(jnp.bfloat16)


def tiles(table, place, w_own, w_mate, vale, c_keep, c_y, c_core, c_diag):
    sources = vale.shape[0]
    width = w_own.shape[0]
    n_z = table.shape[0] // 2
    rows = 2 * n_z * 64
    blocks = sources // 2
    chunks = blocks // CHUNK
    return pl.pallas_call(
        tile_kernel,
        in_specs=[SMEM, SMEM, HBM, ANY] + [VMEM] * 5,
        out_specs=[VMEM, VMEM],
        out_shape=[
            jax.ShapeDtypeStruct((2 * sources, 2 * n_z, 128), jnp.bfloat16),
            jax.ShapeDtypeStruct((n_z, 4, 128), jnp.int32),
        ],
        scratch_shapes=[
            pltpu.VMEM((2, width, blocks * width), jnp.bfloat16),
            pltpu.VMEM((2, 2 * n_z, 8, CHUNK * width), jnp.float32),
            pltpu.VMEM((2 * n_z, 8, 2 * width), jnp.float32),
            pltpu.VMEM((2, 2) + c_keep.shape, jnp.bfloat16),
            pltpu.VMEM((chunks, rows, CHUNK * width), jnp.bfloat16),
            pltpu.VMEM((rows, 2 * width), jnp.bfloat16),
            pltpu.VMEM((rows, 2 * width), jnp.float32),
            pltpu.VMEM((2 * sources, 2 * n_z, 128), jnp.float32),
            pltpu.SemaphoreType.DMA((2, blocks)),
        ],
        compiler_params=pltpu.CompilerParams(vmem_limit_bytes=36 * 1024 * 1024),
    )(table, place, *in_hbm(w_own), w_mate, vale, c_keep, c_y, c_core, c_diag)


def spread_kernel(place, cond_in, vale_in, gmap_in, out, cond, vale, gmap, arrived):
    width = cond.shape[2]
    fetches = [
        pltpu.make_async_copy(source, target, arrived.at[number])
        for number, (source, target) in enumerate(((cond_in, cond), (vale_in, vale), (gmap_in, gmap)))
    ]
    for fetch in fetches:
        fetch.start()
    for fetch in fetches:
        fetch.wait()
    places = (gmap[...] - place[1] * width).astype(jnp.float32)
    top = lax.broadcasted_iota(jnp.int32, (8, 128), 0) == 0
    places = jnp.where(top, places[:, :128], places[:, 128:]).astype(jnp.bfloat16)
    for dest in range(out.shape[0]):
        out[dest, :, :width] = vale[0]
        out[dest, :, width : 2 * width] = cond[0]
        out[dest, :, 2 * width :] = places


def spread(place, cond, vale, gmap, dests):
    return pl.pallas_call(
        spread_kernel,
        in_specs=[SMEM] + [HBM] * 3,
        out_specs=VMEM,
        out_shape=jax.ShapeDtypeStruct((dests, 8, 2 * cond.shape[2] + 128), jnp.bfloat16),
        scratch_shapes=[
            pltpu.VMEM(cond.shape, jnp.bfloat16),
            pltpu.VMEM(vale.shape, jnp.bfloat16),
            pltpu.VMEM(gmap.shape, jnp.int32),
            pltpu.SemaphoreType.DMA((3,)),
        ],
        compiler_params=pltpu.CompilerParams(vmem_limit_bytes=4 * 1024 * 1024),
    )(place, *in_hbm(cond, vale, gmap))


def pack_kernel(got, v_out, c_out, block, sent):
    n_z = got.shape[0]
    width = (got.shape[2] - 128) // 2
    row_id = lax.broadcasted_iota(jnp.int32, (8, 128), 0)
    maps = []
    for first in range(0, n_z, 4):
        tile = jnp.zeros((8, 128), jnp.float32)
        for z in range(first, first + 4):
            pair = got[z, :, 2 * width :].astype(jnp.float32)
            tile = jnp.where(row_id == 2 * (z - first), pair[0:1], tile)
            tile = jnp.where(row_id == 2 * (z - first) + 1, pair[1:2], tile)
        maps.append(tile.astype(jnp.bfloat16))

    def fill(target, column):
        for z in range(n_z):
            target[:, entry_lanes(z, width)] = got[z, :, pl.ds(column * width, width)]
        for number, tile in enumerate(maps):
            target[:, pl.ds(n_z * width + 128 * number, 128)] = tile

    fill(block, 0)
    copies = [
        pltpu.make_async_copy(block, v_out.at[dest], sent.at[dest])
        for dest in range(v_out.shape[0])
    ]
    for copy in copies:
        copy.start()
    fill(c_out, 1)
    for copy in copies:
        copy.wait()


def pack(got, dests):
    n_z = got.shape[0]
    width = (got.shape[2] - 128) // 2
    shape = (8, n_z * width + 128 * (n_z // 4))
    return pl.pallas_call(
        pack_kernel,
        in_specs=[VMEM],
        out_specs=[ANY, VMEM],
        out_shape=[
            jax.ShapeDtypeStruct((dests,) + shape, jnp.bfloat16),
            jax.ShapeDtypeStruct(shape, jnp.bfloat16),
        ],
        scratch_shapes=[
            pltpu.VMEM(shape, jnp.bfloat16),
            pltpu.SemaphoreType.DMA((dests,)),
        ],
        compiler_params=pltpu.CompilerParams(vmem_limit_bytes=8 * 1024 * 1024),
    )(got)


def total_kernel(shares, out):
    sources, rows, _ = shares.shape
    low = lax.broadcasted_iota(jnp.int32, (1, 128), 1) < 64
    sums = []
    for y in range(2):
        first = y * (sources // 2)
        total = shares[first].astype(jnp.float32)
        for source in range(first + 1, first + sources // 2):
            total = total + shares[source].astype(jnp.float32)
        sums.append((total, pltpu.roll(total, 64, 1)))
    for z in range(rows // 2):
        lines = []
        for strip, turned in sums:
            left, right = (turned, strip) if z % 2 else (strip, turned)
            for row in (4 * (z // 2), 4 * (z // 2) + 2):
                lines.append(jnp.where(low, left[row : row + 1], right[row + 1 : row + 2]))
        out[z] = jnp.concatenate(lines, axis=0)


def totals(shares):
    n_z = shares.shape[1] // 2
    return pl.pallas_call(
        total_kernel,
        in_specs=[VMEM],
        out_specs=VMEM,
        out_shape=jax.ShapeDtypeStruct((n_z, 4, 128), jnp.float32),
        compiler_params=pltpu.CompilerParams(vmem_limit_bytes=4 * 1024 * 1024),
    )(shares)


def pick_kernel(plan, rows, out):
    for by in range(NSHIFT + 1):
        both = jnp.zeros((4, 128), jnp.float32)
        for z in range(rows.shape[0]):
            both = jnp.where(plan[z] == by, rows[z], both)
        pair = both[:2] + both[2:]
        for side in range(2):
            out[by, :, pl.ds(128 * side, 128)] = pair[side : side + 1]


def pick(plan, rows):
    return pl.pallas_call(
        pick_kernel,
        in_specs=[VMEM, VMEM],
        out_specs=VMEM,
        out_shape=jax.ShapeDtypeStruct((NSHIFT + 1, 1, 256), jnp.float32),
        compiler_params=pltpu.CompilerParams(vmem_limit_bytes=4 * 1024 * 1024),
    )(plan, rows)


def per_device(cond, vale, screen, qtable, gmap):
    n_ka = lax.axis_size("ka")
    n_ga = lax.axis_size("ga")
    n_z = n_ka // 2
    my_ka = lax.axis_index("ka")
    my_ga = lax.axis_index("ga")
    place = jnp.stack([my_ka, my_ga]).astype(jnp.int32)
    swap_core = [(i, i ^ 1) for i in range(n_ga)]
    swap_y = [(i, i ^ n_z) for i in range(n_ka)]
    swap_both = [(k * n_ga + g, (k ^ n_z) * n_ga + (g ^ 1)) for k in range(n_ka) for g in range(n_ga)]
    along_z = [list(range(n_z)), list(range(n_z, n_ka))]
    planes = [
        [(y * n_z + z) * n_ga + g for y in range(2) for g in range(n_ga)] for z in range(n_z)
    ]
    same_core = [plane[core::2] for plane in planes for core in range(2)]

    sent = spread(place, cond, vale, gmap, n_z)
    sent, slab = lax.optimization_barrier((sent, screen[0]))
    slab_mate = lax.ppermute(slab, "ga", swap_core)
    got = lax.all_to_all(sent, "ka", 0, 0, axis_index_groups=along_z)

    v_sent, c_keep = pack(got, n_ga)
    c_y = lax.ppermute(c_keep, "ka", swap_y)
    c_core = lax.ppermute(c_keep, "ga", swap_core)
    c_diag = lax.ppermute(c_keep, ("ka", "ga"), swap_both)
    v_all = lax.all_to_all(v_sent, ("ka", "ga"), 0, 0, axis_index_groups=same_core)

    part, plan = tiles(qtable, place, slab, slab_mate, v_all, c_keep, c_y, c_core, c_diag)
    shares = lax.all_to_all(part, ("ka", "ga"), 0, 0, axis_index_groups=planes)
    rows = lax.all_to_all(totals(shares), "ka", 0, 0, axis_index_groups=along_z)
    return jnp.transpose(pick(plan, rows), (1, 0, 2))


def solution(mesh):
    in_specs = (P("ka", None, "ga"), P("ka", None, "ga"), P("ka", "ga", None), P(), P("ka", "ga"))
    out_specs = P("ka", None, "ga")
    return jax.shard_map(
        per_device, mesh=mesh, in_specs=in_specs, out_specs=out_specs, check_vma=False
    )
```

time: 105 us -> 105 us (level)
  waiting for transfers between devices: 12.8 us -> 8.38 us
  blocking collectives: 52.4 us -> 55.3 us
  local copies, waits for them, and re-layouts: 0.01 us -> 2.51 us
    ppermute x1, waiting for transfers between devices: 10.1 us -> 0.01 us  [per_device(): c_y = lax.ppermute(c_keep, 'ka', swap_y)]
    ppermute x2, waiting for transfers between devices: 2.2 us -> 8.37 us  [the longest x1 8.37 us: per_device(): c_diag = lax.ppermute(c_keep, ('ka', 'ga'), swap_both)]
    ppermute x2, starting transfers between devices: 4.47 us -> 9.24 us  [the longest x1 7.32 us: per_device(): c_diag = lax.ppermute(c_keep, ('ka', 'ga'), swap_both)]
    ppermute x1, starting transfers between devices: 4.81 us -> 2.02 us  [per_device(): c_y = lax.ppermute(c_keep, 'ka', swap_y)]
    unnamed x2 -> x8, local copies, waits for them, and re-layouts: 0.01 us -> 2.51 us
    all_to_all x1, starting transfers between devices: 9.2 us -> 6.75 us  [per_device(): lax.all_to_all(v_sent, ('ka', 'ga'), 0, 0, axis_index_groups=same_core)]
    all_to_all x1, blocking collectives: 13.2 us -> 14.9 us  [per_device(): shares = lax.all_to_all(part, ('ka', 'ga'), 0, 0, axis_index_groups=planes)]
    all_to_all x1, blocking collectives: 16.9 us -> 18.1 us  [per_device(): rows = lax.all_to_all(totals(shares), 'ka', 0, 0, axis_index_groups=along_z)]
  transfers between devices with their start and end apart: 5 -> 5, of which waited for: 3 -> 1; matrix products, arithmetic and copies ran while one was open for 0% -> 0% of each run, Pallas kernels for 3% -> 2%
where the time goes in v6:
time: 105 us
  blocking collectives  55.3 us (53%)
  starting transfers between devices  26.8 us (26%)
  Pallas kernels  11.7 us (11%)
  waiting for transfers between devices  8.38 us (8%)
  local copies, waits for them, and re-layouts  2.51 us (2%)
    all_to_all x1, blocking collectives, per_device(): got = lax.all_to_all(sent, 'ka', 0, 0, axis_index_groups=along_z)  22.2 us
    all_to_all x1, blocking collectives, per_device(): rows = lax.all_to_all(totals(shares), 'ka', 0, 0, axis_index_groups=along_z)  18.1 us
    all_to_all x1, blocking collectives, per_device(): shares = lax.all_to_all(part, ('ka', 'ga'), 0, 0, axis_index_groups=planes)  14.9 us
    ppermute x1, starting transfers between devices, per_device(): slab_mate = lax.ppermute(slab, 'ga', swap_core)  8.79 us
    ppermute x1, waiting for transfers between devices, per_device(): c_diag = lax.ppermute(c_keep, ('ka', 'ga'), swap_both)  8.37 us
    pallas_call x1, Pallas kernels, tiles(): pl.pallas_call(tile_kernel, in_specs=[SMEM, SMEM, HBM, ANY] + [VMEM] * 5,...  8.03 us
    ppermute x1, starting transfers between devices, per_device(): c_diag = lax.ppermute(c_keep, ('ka', 'ga'), swap_both)  7.32 us
    all_to_all x1, starting transfers between devices, per_device(): lax.all_to_all(v_sent, ('ka', 'ga'), 0, 0, axis_index_groups=same_core)  6.75 us
  transfers between devices with their start and end apart: 5, of which 1 were waited for; matrix products, arithmetic and copies ran while one was open for 0% of the time, Pallas kernels for 2%

profile of v6, /device:TPU:1, one launch (start us, length us, event | category | flops | bytes accessed | tf_op | source)
XLA Modules:
  0.0 104.9 jit_solution(15190396195777471800)
XLA Ops:
  0.0 0.0 copy-start.3
  0.0 0.1 pad_add_fusion.place
  0.1 1.3 %shard_map.55 = bf16[16,8,640]{2,1,0:T(8,128)(2,1)S(1)} custom-call(s32[2]{0:T(128)S(1)} %pad_add_fusion.place, bf16[1,8,256]{2,1,0:T(8,128)(2,1)} %cond_in.1, bf16[1,8,256]{2,1,0:T(8,128)(2,1)} %vale_in.1, s32[1,256]{1,0:T(1,128)} %gmap_in.1), custom_call_target="tpu_custom_call" | custom-call | tf_op jit(solution)/shard_map/pallas_call | solution.py:206
  1.4 8.8 %collective-permute-start = (bf16[256,4096]{1,0:T(8,128)(2,1)}, bf16[256,4096]{1,0:T(8,128)(2,1)S(1)}, u32[]{:S(2)}, u32[]{:S(2)}) collective-permute-start(bf16[256,4096]{1,0:T(8,128)(2,1)} %bitcast.4), channel_id=1, source_target_pairs={{0,1},{1,0},{2,3},{3,2},{4,5},{5,4},{6,7},{7,6},{8,9},{9,8},{10,11... | collective-permute-start | bytes 6291464 | tf_op jit(solution)/shard_map/ppermute | solution.py:340
  10.2 22.2 %all_to_all.20.got = bf16[16,8,640]{2,1,0:T(8,128)(2,1)S(1)} all-to-all(bf16[16,8,640]{2,1,0:T(8,128)(2,1)S(1)} %shard_map.55), channel_id=1, replica_groups={{0,16,32,48,64,80,96,112,128,144,160,176,192,208,224,240},{256,272,288,..., dimensions={0} | all-to-all | bytes 327680 | tf_op jit(solution)/shard_map/all_to_all | solution.py:341
  32.4 1.7 %shard_map.56 = (bf16[16,8,4608]{2,1,0:T(8,128)(2,1)S(1)}, bf16[8,4608]{1,0:T(8,128)(2,1)S(1)}) custom-call(bf16[16,8,640]{2,1,0:T(8,128)(2,1)S(1)} %all_to_all.20.got), custom_call_target="tpu_custom_call" | custom-call | tf_op jit(solution)/shard_map/pallas_call | solution.py:256
  34.1 0.0 copy-start
  34.1 1.0 copy-done
  35.1 6.8 %all-to-all-start.1 = ((bf16[16,8,4608]{2,1,0:T(8,128)(2,1)}), bf16[16,8,4608]{2,1,0:T(8,128)(2,1)S(1)}, u32[]{:S(2)}, u32[]{:S(2)}) async-start(bf16[16,8,4608]{2,1,0:T(8,128)(2,1)} %copy-done), calls=%async_computation.1 | async-start | bytes 2359296 | tf_op jit(solution)/shard_map/all_to_all | solution.py:347
  41.9 7.3 %collective-permute-start.3 = (bf16[8,4608]{1,0:T(8,128)(2,1)S(1)}, bf16[8,4608]{1,0:T(8,128)(2,1)S(1)}, u32[]{:S(2)}, u32[]{:S(2)}) collective-permute-start(bf16[8,4608]{1,0:T(8,128)(2,1)S(1)} %get-tuple-element.14.c_keep), channel_id=1, source_target_pairs={{0,257},{1,256},{2,259},{3,258},{4,261},{5,260},{6,263},{7,262},{8... | collective-permute-start | bytes 221192 | tf_op jit(solution)/shard_map/ppermute | solution.py:346
  49.2 1.9 %collective-permute-start.2 = (bf16[8,4608]{1,0:T(8,128)(2,1)S(1)}, bf16[8,4608]{1,0:T(8,128)(2,1)S(1)}, u32[]{:S(2)}, u32[]{:S(2)}) collective-permute-start(bf16[8,4608]{1,0:T(8,128)(2,1)S(1)} %get-tuple-element.14.c_keep), channel_id=1, source_target_pairs={{0,1},{1,0},{2,3},{3,2},{4,5},{5,4},{6,7},{7,6},{8,9},{9,8},{10,11... | collective-permute-start | bytes 221192 | tf_op jit(solution)/shard_map/ppermute | solution.py:345
  51.2 2.0 %collective-permute-start.1 = (bf16[8,4608]{1,0:T(8,128)(2,1)S(1)}, bf16[8,4608]{1,0:T(8,128)(2,1)S(1)}, u32[]{:S(2)}, u32[]{:S(2)}) collective-permute-start(bf16[8,4608]{1,0:T(8,128)(2,1)S(1)} %get-tuple-element.14.c_keep), channel_id=1, source_target_pairs={{0,256},{16,272},{32,288},{48,304},{64,320},{80,336},{96,352},{112... | collective-permute-start | bytes 221192 | tf_op jit(solution)/shard_map/ppermute | solution.py:344
  53.2 8.4 %collective-permute-done.3.c_diag = bf16[8,4608]{1,0:T(8,128)(2,1)S(1)} collective-permute-done((bf16[8,4608]{1,0:T(8,128)(2,1)S(1)}, bf16[8,4608]{1,0:T(8,128)(2,1)S(1)}, u32[]{:S(2)}, u32[]{:S(2)}) %collective-permute-start.3) | collective-permute-done | bytes 73760 | tf_op jit(solution)/shard_map/ppermute | solution.py:346
  61.6 0.0 collective-permute-done.2.c_core
  61.6 0.0 collective-permute-done.1.c_y
  61.6 0.0 copy-start.1
  61.6 0.6 copy-done.1
  62.2 0.0 all-to-all-done.1.vale
  62.2 0.0 collective-permute-done.w_mate
  62.2 0.0 copy-done.3
  62.2 0.0 copy-start.2
  62.2 0.9 copy-done.2
  63.1 8.0 %shard_map.57 = (bf16[32,32,128]{2,1,0:T(8,128)(2,1)S(1)}, s32[16,4,128]{2,1,0:T(4,128)S(1)}) custom-call(s32[32,32]{1,0:T(8,128)S(1)} %copy-done.3, s32[2]{0:T(128)S(1)} %pad_add_fusion.place, bf16[256,4096]{1,0:T(8,128)(2,1)} %bitcast.5, bf16[256,4096]{1,0:T(8,128)(2,1)S(1)} %collective-permute-done.w_mate, bf16[16,8,4608]{2,1,0:T(8,128)(2,1)S(1)} %all-to-all-done.1.vale, ...), custom_call_target="tpu_custom_call" | custom-call | tf_op jit(solution)/shard_map/pallas_call | solution.py:163
  71.1 14.9 %all_to_all.21.shares = bf16[32,32,128]{2,1,0:T(8,128)(2,1)S(1)} all-to-all(bf16[32,32,128]{2,1,0:T(8,128)(2,1)S(1)} %get-tuple-element.16), channel_id=1, replica_groups={{0,1,2,3,4,5,6,7,8,9,10,11,12,13,14,15,256,257,258,259,260,261,262,263,..., dimensions={0} | all-to-all | bytes 524288 | tf_op jit(solution)/shard_map/all_to_all | solution.py:350
  86.0 0.1 shard_map.58
  86.1 18.1 %all_to_all.22.rows = f32[16,4,128]{2,1,0:T(4,128)S(1)} all-to-all(f32[16,4,128]{2,1,0:T(4,128)S(1)} %shard_map.58), channel_id=1, replica_groups={{0,16,32,48,64,80,96,112,128,144,160,176,192,208,224,240},{256,272,288,..., dimensions={0} | all-to-all | bytes 65536 | tf_op jit(solution)/shard_map/all_to_all | solution.py:351
  104.3 0.6 shard_map.59
Async XLA Ops:
  0.0 62.2 %copy-start.3 = (s32[32,32]{1,0:T(8,128)S(1)}, s32[32,32]{1,0:T(8,128)}, u32[]{:S(2)}) copy-start(s32[32,32]{1,0:T(8,128)} %table.1) | copy-start | bytes 12292
  1.4 60.8 %collective-permute-start = (bf16[256,4096]{1,0:T(8,128)(2,1)}, bf16[256,4096]{1,0:T(8,128)(2,1)S(1)}, u32[]{:S(2)}, u32[]{:S(2)}) collective-permute-start(bf16[256,4096]{1,0:T(8,128)(2,1)} %bitcast.4), channel_id=1, source_target_pairs={{0,1},{1,0},{2,3},{3,2},{4,5},{5,4},{6,7},{7,6},{8,9},{9,8},{10,11... | collective-permute-start | bytes 6291464 | tf_op jit(solution)/shard_map/ppermute | solution.py:340
  34.1 1.0 copy-start
  35.1 27.1 %all-to-all-start.1 = ((bf16[16,8,4608]{2,1,0:T(8,128)(2,1)}), bf16[16,8,4608]{2,1,0:T(8,128)(2,1)S(1)}, u32[]{:S(2)}, u32[]{:S(2)}) async-start(bf16[16,8,4608]{2,1,0:T(8,128)(2,1)} %copy-done), calls=%async_computation.1 | async-start | bytes 2359296 | tf_op jit(solution)/shard_map/all_to_all | solution.py:347
  41.9 19.7 %collective-permute-start.3 = (bf16[8,4608]{1,0:T(8,128)(2,1)S(1)}, bf16[8,4608]{1,0:T(8,128)(2,1)S(1)}, u32[]{:S(2)}, u32[]{:S(2)}) collective-permute-start(bf16[8,4608]{1,0:T(8,128)(2,1)S(1)} %get-tuple-element.14.c_keep), channel_id=1, source_target_pairs={{0,257},{1,256},{2,259},{3,258},{4,261},{5,260},{6,263},{7,262},{8... | collective-permute-start | bytes 221192 | tf_op jit(solution)/shard_map/ppermute | solution.py:346
  49.2 12.3 %collective-permute-start.2 = (bf16[8,4608]{1,0:T(8,128)(2,1)S(1)}, bf16[8,4608]{1,0:T(8,128)(2,1)S(1)}, u32[]{:S(2)}, u32[]{:S(2)}) collective-permute-start(bf16[8,4608]{1,0:T(8,128)(2,1)S(1)} %get-tuple-element.14.c_keep), channel_id=1, source_target_pairs={{0,1},{1,0},{2,3},{3,2},{4,5},{5,4},{6,7},{7,6},{8,9},{9,8},{10,11... | collective-permute-start | bytes 221192 | tf_op jit(solution)/shard_map/ppermute | solution.py:345
  51.2 10.4 %collective-permute-start.1 = (bf16[8,4608]{1,0:T(8,128)(2,1)S(1)}, bf16[8,4608]{1,0:T(8,128)(2,1)S(1)}, u32[]{:S(2)}, u32[]{:S(2)}) collective-permute-start(bf16[8,4608]{1,0:T(8,128)(2,1)S(1)} %get-tuple-element.14.c_keep), channel_id=1, source_target_pairs={{0,256},{16,272},{32,288},{48,304},{64,320},{80,336},{96,352},{112... | collective-permute-start | bytes 221192 | tf_op jit(solution)/shard_map/ppermute | solution.py:344
  61.6 0.6 copy-start.1
  62.2 0.9 copy-start.2

commit v7 on v6

--- a/solution.py
+++ b/solution.py
@@ -7,7 +7,8 @@
 
 NSHIFT = 2
 STEP_K = 4
-CHUNK = 2
+BAND_K = 16
+CHUNKS = ((0,), (1,2,3), (4,5,6,7))
 VMEM = pl.BlockSpec(memory_space=pltpu.VMEM)
 SMEM = pl.BlockSpec(memory_space=pltpu.SMEM)
 HBM = pl.BlockSpec(memory_space=pltpu.HBM)
@@ -61,7 +62,7 @@
 
 def tile_kernel(
     table, place, w_own, w_mate, vale, c_keep, c_y, c_core, c_diag, out, plan,
-    slabs, far_v, far_c, c_all, pv, pc, image, wide, arrived,
+    slabs, far_v, far_c, c_all, pv, pc, image, wide, arrived, joined,
 ):
     blocks = vale.shape[0] // 2
     width = w_own.shape[0]
@@ -78,6 +79,11 @@
         for block in range(blocks)
         for side, source in enumerate((w_own, w_mate))
     ]
+    fetches += [
+        pltpu.make_async_copy(source, c_all.at[side, y], joined.at[side, other])
+        for side, pair in enumerate(((c_keep, c_y), (c_core, c_diag)))
+        for other, (source, y) in enumerate(zip(pair, (my_y, 1 - my_y)))
+    ]
     for fetch in fetches:
         fetch.start()
 
@@ -93,27 +99,23 @@
     def partner(k):
         return jnp.where(k < shift, k - shift + 2 * n_z, k - shift)
 
-    def form(chunk):
-        slot = chunk % far_v.shape[0]
+    def form(number):
+        slot = number % far_v.shape[0]
         for y in range(2):
-            for inner in range(CHUNK):
-                source = y * blocks + chunk * CHUNK + inner
+            for inner, block in enumerate(CHUNKS[number]):
 
                 def store(z, value):
                     far_v[slot, y * n_z + z, :, pl.ds(inner * width, width)] = value
 
-                map_entries(vale.at[source], n_z, width, store)
+                map_entries(vale.at[y * blocks + block], n_z, width, store)
         for k in range(2 * n_z):
-            for inner in range(CHUNK):
-                source = k // n_z * blocks + chunk * CHUNK + inner
-                lanes = pl.ds(inner * width, width)
-                own = vale[source, :, entry_lanes(k % n_z, width)].astype(jnp.float32)
-                pv[chunk, pl.ds(64 * k, 64), lanes] = density(own, far_v[slot, partner(k), :, lanes])
+            for inner, block in enumerate(CHUNKS[number]):
+                far = far_v[slot, partner(k), :, pl.ds(inner * width, width)]
+                own = vale[k // n_z * blocks + block, :, entry_lanes(k % n_z, width)]
+                own = own.astype(jnp.float32)
+                pv[pl.ds(64 * k, 64), pl.ds(block * width, width)] = density(own, far)
 
     def form_c():
-        for side, (mine, other) in enumerate(((c_keep, c_y), (c_core, c_diag))):
-            c_all[side, my_y] = mine[...]
-            c_all[side, 1 - my_y] = other[...]
         for side in range(2):
             lanes = pl.ds(side * width, width)
             for y in range(2):
@@ -126,30 +128,43 @@
                 own = c_all[side, k // n_z, :, entry_lanes(k % n_z, width)].astype(jnp.float32)
                 pc[pl.ds(64 * k, 64), lanes] = density(own, far_c[partner(k), :, lanes])
 
-    chunks = blocks // CHUNK
+    def term(rows, number, side):
+        span = pl.ds(CHUNKS[number][0] * width, len(CHUNKS[number]) * width)
+        return last_dims(pv[rows, span], slabs[side, :, span])
+
+    sides = [pl.ds(side * width, width) for side in range(2)]
+    last = len(CHUNKS) - 1
     form(0)
     for fetch in fetches:
         fetch.wait()
-    for chunk in range(chunks):
-        if chunk + 1 < chunks:
-            form(chunk + 1)
-        else:
+    for number in range(last):
+        form(number + 1)
+        if number + 1 == last:
             form_c()
-        for side in range(2):
-            lanes = pl.ds(side * width, width)
-            term = last_dims(pv[chunk], slabs[side, :, pl.ds(chunk * CHUNK * width, CHUNK * width)])
-            image[:, lanes] = term if chunk == 0 else image[:, lanes] + term
+        for side, lanes in enumerate(sides):
+            part = term(pl.ds(0, pv.shape[0]), number, side)
+            image[:, lanes] = part if number == 0 else image[:, lanes] + part
 
     low = lax.broadcasted_iota(jnp.int32, (64, 128), 1) < 64
-    for y in range(2):
-        for part in range(n_z // STEP_K):
-            rows = pl.ds(64 * (y * n_z + part * STEP_K), 64 * STEP_K)
-            full = last_dims(pc[rows, :], image[rows, :].astype(jnp.bfloat16))
+    for first in range(0, 2 * n_z, BAND_K):
+        rows = pl.ds(64 * first, 64 * BAND_K)
+        bands = [
+            (image[rows, lanes] + term(rows, last, side)).astype(jnp.bfloat16)
+            for side, lanes in enumerate(sides)
+        ]
+        for step in range(0, BAND_K, STEP_K):
+            full = None
+            for lanes, band in zip(sides, bands):
+                band = band[64 * step : 64 * (step + STEP_K)]
+                part = last_dims(pc[pl.ds(64 * (first + step), 64 * STEP_K), lanes], band)
+                full = part if full is None else full + part
             for pair in range(STEP_K // 2):
                 base = 128 * pair
                 strip = full[:, base : base + 128]
                 tile = jnp.where(low, strip[base : base + 64], strip[base + 64 : base + 128])
-                wide[pl.ds(16 * y, 16), pl.ds(8 * part + 4 * pair, 4), :] = tile.reshape(16, 4, 128)
+                k = first + step + 2 * pair
+                dests = pl.ds(16 * (k // n_z), 16)
+                wide[dests, pl.ds(2 * (k % n_z), 4), :] = tile.reshape(16, 4, 128)
     out[...] = wide[...].astype(jnp.bfloat16)
 
 
@@ -159,10 +174,10 @@
     n_z = table.shape[0] // 2
     rows = 2 * n_z * 64
     blocks = sources // 2
-    chunks = blocks // CHUNK
+    wide = max(len(chunk) for chunk in CHUNKS) * width
     return pl.pallas_call(
         tile_kernel,
-        in_specs=[SMEM, SMEM, HBM, ANY] + [VMEM] * 5,
+        in_specs=[SMEM, SMEM, HBM, ANY, VMEM] + [ANY] * 4,
         out_specs=[VMEM, VMEM],
         out_shape=[
             jax.ShapeDtypeStruct((2 * sources, 2 * n_z, 128), jnp.bfloat16),
@@ -170,16 +185,17 @@
         ],
         scratch_shapes=[
             pltpu.VMEM((2, width, blocks * width), jnp.bfloat16),
-            pltpu.VMEM((2, 2 * n_z, 8, CHUNK * width), jnp.float32),
+            pltpu.VMEM((2, 2 * n_z, 8, wide), jnp.float32),
             pltpu.VMEM((2 * n_z, 8, 2 * width), jnp.float32),
             pltpu.VMEM((2, 2) + c_keep.shape, jnp.bfloat16),
-            pltpu.VMEM((chunks, rows, CHUNK * width), jnp.bfloat16),
+            pltpu.VMEM((rows, blocks * width), jnp.bfloat16),
             pltpu.VMEM((rows, 2 * width), jnp.bfloat16),
             pltpu.VMEM((rows, 2 * width), jnp.float32),
             pltpu.VMEM((2 * sources, 2 * n_z, 128), jnp.float32),
             pltpu.SemaphoreType.DMA((2, blocks)),
-        ],
-        compiler_params=pltpu.CompilerParams(vmem_limit_bytes=36 * 1024 * 1024),
+            pltpu.SemaphoreType.DMA((2, 2)),
+        ],
+        compiler_params=pltpu.CompilerParams(vmem_limit_bytes=28 * 1024 * 1024),
     )(table, place, *in_hbm(w_own), w_mate, vale, c_keep, c_y, c_core, c_diag)
 
 
@@ -256,9 +272,9 @@
     return pl.pallas_call(
         pack_kernel,
         in_specs=[VMEM],
-        out_specs=[ANY, VMEM],
+        out_specs=[HBM, VMEM],
         out_shape=[
-            jax.ShapeDtypeStruct((dests,) + shape, jnp.bfloat16),
+            pltpu.HBM((dests,) + shape, jnp.bfloat16),
             jax.ShapeDtypeStruct(shape, jnp.bfloat16),
         ],
         scratch_shapes=[
@@ -336,14 +352,14 @@
     same_core = [plane[core::2] for plane in planes for core in range(2)]
 
     sent = spread(place, cond, vale, gmap, n_z)
-    sent, slab = lax.optimization_barrier((sent, screen[0]))
-    slab_mate = lax.ppermute(slab, "ga", swap_core)
     got = lax.all_to_all(sent, "ka", 0, 0, axis_index_groups=along_z)
 
     v_sent, c_keep = pack(got, n_ga)
+    v_sent, c_keep, slab = lax.optimization_barrier((v_sent, c_keep, screen[0]))
     c_y = lax.ppermute(c_keep, "ka", swap_y)
     c_core = lax.ppermute(c_keep, "ga", swap_core)
     c_diag = lax.ppermute(c_keep, ("ka", "ga"), swap_both)
+    slab_mate = lax.ppermute(slab, "ga", swap_core)
     v_all = lax.all_to_all(v_sent, ("ka", "ga"), 0, 0, axis_index_groups=same_core)
 
     part, plan = tiles(qtable, place, slab, slab_mate, v_all, c_keep, c_y, c_core, c_diag)

time: 105 us -> 103 us (0.981)
  starting transfers between devices: 26.8 us -> 22.2 us
  blocking collectives: 55.3 us -> 58 us
  waiting for transfers between devices: 8.38 us -> 10.1 us
    all_to_all x1, blocking collectives: 22.2 us -> 27.8 us  [per_device(): got = lax.all_to_all(sent, 'ka', 0, 0, axis_index_groups=along_z)]
    all_to_all x1, blocking collectives: 18.1 us -> 15.3 us  [per_device(): rows = lax.all_to_all(totals(shares), 'ka', 0, 0, axis_index_groups=along_z)]
    ppermute x1, starting transfers between devices: 8.79 us -> 6.28 us  [per_device(): slab_mate = lax.ppermute(slab, 'ga', swap_core)]
    ppermute x1, starting transfers between devices: 7.32 us -> 5.23 us  [per_device(): c_diag = lax.ppermute(c_keep, ('ka', 'ga'), swap_both)]
    all_to_all x1, waiting for transfers between devices: 0.01 us -> 1.52 us  [per_device(): lax.all_to_all(v_sent, ('ka', 'ga'), 0, 0, axis_index_groups=same_core)]
    unnamed x8 -> x6, local copies, waits for them, and re-layouts: 2.51 us -> 1.52 us
  transfers between devices with their start and end apart: 5 -> 5, of which waited for: 1 -> 3; matrix products, arithmetic and copies ran while one was open for 0% -> 0% of each run, Pallas kernels for 2% -> 0%
where the time goes in v7:
time: 103 us
  blocking collectives  58 us (56%)
  starting transfers between devices  22.2 us (22%)
  Pallas kernels  10.8 us (10%)
  waiting for transfers between devices  10.1 us (10%)
  local copies, waits for them, and re-layouts  1.52 us (1%)
    all_to_all x1, blocking collectives, per_device(): got = lax.all_to_all(sent, 'ka', 0, 0, axis_index_groups=along_z)  27.8 us
    all_to_all x1, blocking collectives, per_device(): rows = lax.all_to_all(totals(shares), 'ka', 0, 0, axis_index_groups=along_z)  15.3 us
    all_to_all x1, blocking collectives, per_device(): shares = lax.all_to_all(part, ('ka', 'ga'), 0, 0, axis_index_groups=planes)  14.9 us
    ppermute x1, waiting for transfers between devices, per_device(): c_diag = lax.ppermute(c_keep, ('ka', 'ga'), swap_both)  8.18 us
    pallas_call x1, Pallas kernels, tiles(): pl.pallas_call(tile_kernel, in_specs=[SMEM, SMEM, HBM, ANY, VMEM] + [ANY]...  7.66 us
    all_to_all x1, starting transfers between devices, per_device(): lax.all_to_all(v_sent, ('ka', 'ga'), 0, 0, axis_index_groups=same_core)  6.77 us
    ppermute x1, starting transfers between devices, per_device(): slab_mate = lax.ppermute(slab, 'ga', swap_core)  6.28 us
    ppermute x1, starting transfers between devices, per_device(): c_diag = lax.ppermute(c_keep, ('ka', 'ga'), swap_both)  5.23 us
  transfers between devices with their start and end apart: 5, of which 3 were waited for; matrix products, arithmetic and copies ran while one was open for 0% of the time, Pallas kernels for 0%

profile of v7, /device:TPU:1, one launch (start us, length us, event | category | flops | bytes accessed | tf_op | source)
XLA Modules:
  0.0 102.9 jit_solution(3669436679828881357)
XLA Ops:
  0.0 0.0 copy-start.2
  0.0 0.1 pad_add_fusion.place
  0.1 1.3 %shard_map.55 = bf16[16,8,640]{2,1,0:T(8,128)(2,1)S(1)} custom-call(s32[2]{0:T(128)S(1)} %pad_add_fusion.place, bf16[1,8,256]{2,1,0:T(8,128)(2,1)} %cond_in.1, bf16[1,8,256]{2,1,0:T(8,128)(2,1)} %vale_in.1, s32[1,256]{1,0:T(1,128)} %gmap_in.1), custom_call_target="tpu_custom_call" | custom-call | tf_op jit(solution)/shard_map/pallas_call | solution.py:222
  1.4 27.8 %all_to_all.20.got = bf16[16,8,640]{2,1,0:T(8,128)(2,1)S(1)} all-to-all(bf16[16,8,640]{2,1,0:T(8,128)(2,1)S(1)} %shard_map.55), channel_id=1, replica_groups={{0,16,32,48,64,80,96,112,128,144,160,176,192,208,224,240},{256,272,288,..., dimensions={0} | all-to-all | bytes 327680 | tf_op jit(solution)/shard_map/all_to_all | solution.py:355
  29.1 1.2 %shard_map.56 = (bf16[16,8,4608]{2,1,0:T(8,128)(2,1)}, bf16[8,4608]{1,0:T(8,128)(2,1)S(1)}) custom-call(bf16[16,8,640]{2,1,0:T(8,128)(2,1)S(1)} %all_to_all.20.got), custom_call_target="tpu_custom_call" | custom-call | tf_op jit(solution)/shard_map/pallas_call | solution.py:272
  30.3 6.3 %collective-permute-start = (bf16[256,4096]{1,0:T(8,128)(2,1)}, bf16[256,4096]{1,0:T(8,128)(2,1)S(1)}, u32[]{:S(2)}, u32[]{:S(2)}) collective-permute-start(bf16[256,4096]{1,0:T(8,128)(2,1)} %bitcast.4), channel_id=1, source_target_pairs={{0,1},{1,0},{2,3},{3,2},{4,5},{5,4},{6,7},{7,6},{8,9},{9,8},{10,11... | collective-permute-start | bytes 6291464 | tf_op jit(solution)/shard_map/ppermute | solution.py:362
  36.6 6.8 %all-to-all-start.1 = ((bf16[16,8,4608]{2,1,0:T(8,128)(2,1)}), bf16[16,8,4608]{2,1,0:T(8,128)(2,1)S(1)}, u32[]{:S(2)}, u32[]{:S(2)}) async-start(bf16[16,8,4608]{2,1,0:T(8,128)(2,1)} %get-tuple-element.15), calls=%async_computation.1 | async-start | bytes 2359296 | tf_op jit(solution)/shard_map/all_to_all | solution.py:363
  43.4 5.2 %collective-permute-start.3 = (bf16[8,4608]{1,0:T(8,128)(2,1)S(1)}, bf16[8,4608]{1,0:T(8,128)(2,1)S(1)}, u32[]{:S(2)}, u32[]{:S(2)}) collective-permute-start(bf16[8,4608]{1,0:T(8,128)(2,1)S(1)} %get-tuple-element.16.c_keep), channel_id=1, source_target_pairs={{0,257},{1,256},{2,259},{3,258},{4,261},{5,260},{6,263},{7,262},{8... | collective-permute-start | bytes 221192 | tf_op jit(solution)/shard_map/ppermute | solution.py:361
  48.6 1.9 %collective-permute-start.2 = (bf16[8,4608]{1,0:T(8,128)(2,1)S(1)}, bf16[8,4608]{1,0:T(8,128)(2,1)S(1)}, u32[]{:S(2)}, u32[]{:S(2)}) collective-permute-start(bf16[8,4608]{1,0:T(8,128)(2,1)S(1)} %get-tuple-element.16.c_keep), channel_id=1, source_target_pairs={{0,1},{1,0},{2,3},{3,2},{4,5},{5,4},{6,7},{7,6},{8,9},{9,8},{10,11... | collective-permute-start | bytes 221192 | tf_op jit(solution)/shard_map/ppermute | solution.py:360
  50.6 2.0 %collective-permute-start.1 = (bf16[8,4608]{1,0:T(8,128)(2,1)S(1)}, bf16[8,4608]{1,0:T(8,128)(2,1)S(1)}, u32[]{:S(2)}, u32[]{:S(2)}) collective-permute-start(bf16[8,4608]{1,0:T(8,128)(2,1)S(1)} %get-tuple-element.16.c_keep), channel_id=1, source_target_pairs={{0,256},{16,272},{32,288},{48,304},{64,320},{80,336},{96,352},{112... | collective-permute-start | bytes 221192 | tf_op jit(solution)/shard_map/ppermute | solution.py:359
  52.6 8.2 %collective-permute-done.3.c_diag = bf16[8,4608]{1,0:T(8,128)(2,1)S(1)} collective-permute-done((bf16[8,4608]{1,0:T(8,128)(2,1)S(1)}, bf16[8,4608]{1,0:T(8,128)(2,1)S(1)}, u32[]{:S(2)}, u32[]{:S(2)}) %collective-permute-start.3) | collective-permute-done | bytes 73760 | tf_op jit(solution)/shard_map/ppermute | solution.py:361
  60.8 0.0 collective-permute-done.2.c_core
  60.8 0.4 collective-permute-done.1.c_y
  61.2 0.0 copy-start
  61.2 0.6 copy-done
  61.8 1.5 %all-to-all-done.1.vale = bf16[16,8,4608]{2,1,0:T(8,128)(2,1)S(1)} async-done(((bf16[16,8,4608]{2,1,0:T(8,128)(2,1)}), bf16[16,8,4608]{2,1,0:T(8,128)(2,1)S(1)}, u32[]{:S(2)}, u32[]{:S(2)}) %all-to-all-start.1) | async-done | bytes 1179680 | tf_op jit(solution)/shard_map/all_to_all | solution.py:363
  63.4 0.0 collective-permute-done.w_mate
  63.4 0.0 copy-done.2
  63.4 0.0 copy-start.1
  63.4 0.9 copy-done.1
  64.3 7.7 %shard_map.57 = (bf16[32,32,128]{2,1,0:T(8,128)(2,1)S(1)}, s32[16,4,128]{2,1,0:T(4,128)S(1)}) custom-call(s32[32,32]{1,0:T(8,128)S(1)} %copy-done.2, s32[2]{0:T(128)S(1)} %pad_add_fusion.place, bf16[256,4096]{1,0:T(8,128)(2,1)} %bitcast.5, bf16[256,4096]{1,0:T(8,128)(2,1)S(1)} %collective-permute-done.w_mate, bf16[16,8,4608]{2,1,0:T(8,128)(2,1)S(1)} %all-to-all-done.1.vale, ...), custom_call_target="tpu_custom_call" | custom-call | tf_op jit(solution)/shard_map/pallas_call | solution.py:178
  71.9 14.9 %all_to_all.21.shares = bf16[32,32,128]{2,1,0:T(8,128)(2,1)S(1)} all-to-all(bf16[32,32,128]{2,1,0:T(8,128)(2,1)S(1)} %get-tuple-element.18), channel_id=1, replica_groups={{0,1,2,3,4,5,6,7,8,9,10,11,12,13,14,15,256,257,258,259,260,261,262,263,..., dimensions={0} | all-to-all | bytes 524288 | tf_op jit(solution)/shard_map/all_to_all | solution.py:366
  86.9 0.1 shard_map.58
  87.0 15.3 %all_to_all.22.rows = f32[16,4,128]{2,1,0:T(4,128)S(1)} all-to-all(f32[16,4,128]{2,1,0:T(4,128)S(1)} %shard_map.58), channel_id=1, replica_groups={{0,16,32,48,64,80,96,112,128,144,160,176,192,208,224,240},{256,272,288,..., dimensions={0} | all-to-all | bytes 65536 | tf_op jit(solution)/shard_map/all_to_all | solution.py:367
  102.3 0.6 shard_map.59
Async XLA Ops:
  0.0 63.4 %copy-start.2 = (s32[32,32]{1,0:T(8,128)S(1)}, s32[32,32]{1,0:T(8,128)}, u32[]{:S(2)}) copy-start(s32[32,32]{1,0:T(8,128)} %table.1) | copy-start | bytes 12292
  30.3 33.0 %collective-permute-start = (bf16[256,4096]{1,0:T(8,128)(2,1)}, bf16[256,4096]{1,0:T(8,128)(2,1)S(1)}, u32[]{:S(2)}, u32[]{:S(2)}) collective-permute-start(bf16[256,4096]{1,0:T(8,128)(2,1)} %bitcast.4), channel_id=1, source_target_pairs={{0,1},{1,0},{2,3},{3,2},{4,5},{5,4},{6,7},{7,6},{8,9},{9,8},{10,11... | collective-permute-start | bytes 6291464 | tf_op jit(solution)/shard_map/ppermute | solution.py:362
  36.6 26.7 %all-to-all-start.1 = ((bf16[16,8,4608]{2,1,0:T(8,128)(2,1)}), bf16[16,8,4608]{2,1,0:T(8,128)(2,1)S(1)}, u32[]{:S(2)}, u32[]{:S(2)}) async-start(bf16[16,8,4608]{2,1,0:T(8,128)(2,1)} %get-tuple-element.15), calls=%async_computation.1 | async-start | bytes 2359296 | tf_op jit(solution)/shard_map/all_to_all | solution.py:363
  43.4 17.4 %collective-permute-start.3 = (bf16[8,4608]{1,0:T(8,128)(2,1)S(1)}, bf16[8,4608]{1,0:T(8,128)(2,1)S(1)}, u32[]{:S(2)}, u32[]{:S(2)}) collective-permute-start(bf16[8,4608]{1,0:T(8,128)(2,1)S(1)} %get-tuple-element.16.c_keep), channel_id=1, source_target_pairs={{0,257},{1,256},{2,259},{3,258},{4,261},{5,260},{6,263},{7,262},{8... | collective-permute-start | bytes 221192 | tf_op jit(solution)/shard_map/ppermute | solution.py:361
  48.6 12.1 %collective-permute-start.2 = (bf16[8,4608]{1,0:T(8,128)(2,1)S(1)}, bf16[8,4608]{1,0:T(8,128)(2,1)S(1)}, u32[]{:S(2)}, u32[]{:S(2)}) collective-permute-start(bf16[8,4608]{1,0:T(8,128)(2,1)S(1)} %get-tuple-element.16.c_keep), channel_id=1, source_target_pairs={{0,1},{1,0},{2,3},{3,2},{4,5},{5,4},{6,7},{7,6},{8,9},{9,8},{10,11... | collective-permute-start | bytes 221192 | tf_op jit(solution)/shard_map/ppermute | solution.py:360
  50.6 10.7 %collective-permute-start.1 = (bf16[8,4608]{1,0:T(8,128)(2,1)S(1)}, bf16[8,4608]{1,0:T(8,128)(2,1)S(1)}, u32[]{:S(2)}, u32[]{:S(2)}) collective-permute-start(bf16[8,4608]{1,0:T(8,128)(2,1)S(1)} %get-tuple-element.16.c_keep), channel_id=1, source_target_pairs={{0,256},{16,272},{32,288},{48,304},{64,320},{80,336},{96,352},{112... | collective-permute-start | bytes 221192 | tf_op jit(solution)/shard_map/ppermute | solution.py:359
  61.2 0.6 copy-start
  63.4 0.9 copy-start.1

commit v8 on v7

--- a/solution.py
+++ b/solution.py
@@ -61,7 +61,7 @@
 
 
 def tile_kernel(
-    table, place, w_own, w_mate, vale, c_keep, c_y, c_core, c_diag, out, plan,
+    table, place, w_own, w_low, w_high, vale, c_keep, c_y, c_core, c_diag, out, plan,
     slabs, far_v, far_c, c_all, pv, pc, image, wide, arrived, joined,
 ):
     blocks = vale.shape[0] // 2
@@ -72,12 +72,18 @@
     shift = sum(jnp.where(table[by, 0] == my_ka, by, 0) for by in range(1, NSHIFT + 1))
     fetches = [
         pltpu.make_async_copy(
-            source.at[:, pl.ds(pl.multiple_of((2 * block + core) * width, width), width)],
-            slabs.at[side, :, pl.ds(block * width, width)],
-            arrived.at[side, block],
+            w_own.at[:, pl.ds(pl.multiple_of((2 * block + core) * width, width), width)],
+            slabs.at[0, :, pl.ds(block * width, width)],
+            arrived.at[block],
         )
         for block in range(blocks)
-        for side, source in enumerate((w_own, w_mate))
+    ]
+    half = w_low.shape[1]
+    fetches += [
+        pltpu.make_async_copy(
+            source, slabs.at[1, :, pl.ds(number * half, half)], arrived.at[blocks + number]
+        )
+        for number, source in enumerate((w_low, w_high))
     ]
     fetches += [
         pltpu.make_async_copy(source, c_all.at[side, y], joined.at[side, other])
@@ -168,7 +174,7 @@
     out[...] = wide[...].astype(jnp.bfloat16)
 
 
-def tiles(table, place, w_own, w_mate, vale, c_keep, c_y, c_core, c_diag):
+def tiles(table, place, w_own, w_low, w_high, vale, c_keep, c_y, c_core, c_diag):
     sources = vale.shape[0]
     width = w_own.shape[0]
     n_z = table.shape[0] // 2
@@ -177,7 +183,7 @@
     wide = max(len(chunk) for chunk in CHUNKS) * width
     return pl.pallas_call(
         tile_kernel,
-        in_specs=[SMEM, SMEM, HBM, ANY, VMEM] + [ANY] * 4,
+        in_specs=[SMEM, SMEM, HBM, ANY, ANY, VMEM] + [ANY] * 4,
         out_specs=[VMEM, VMEM],
         out_shape=[
             jax.ShapeDtypeStruct((2 * sources, 2 * n_z, 128), jnp.bfloat16),
@@ -192,11 +198,11 @@
             pltpu.VMEM((rows, 2 * width), jnp.bfloat16),
             pltpu.VMEM((rows, 2 * width), jnp.float32),
             pltpu.VMEM((2 * sources, 2 * n_z, 128), jnp.float32),
-            pltpu.SemaphoreType.DMA((2, blocks)),
+            pltpu.SemaphoreType.DMA((blocks + 2,)),
             pltpu.SemaphoreType.DMA((2, 2)),
         ],
         compiler_params=pltpu.CompilerParams(vmem_limit_bytes=28 * 1024 * 1024),
-    )(table, place, *in_hbm(w_own), w_mate, vale, c_keep, c_y, c_core, c_diag)
+    )(table, place, *in_hbm(w_own), w_low, w_high, vale, c_keep, c_y, c_core, c_diag)
 
 
 def spread_kernel(place, cond_in, vale_in, gmap_in, out, cond, vale, gmap, arrived):
@@ -234,9 +240,24 @@
     )(place, *in_hbm(cond, vale, gmap))
 
 
-def pack_kernel(got, v_out, c_out, block, sent):
+def pack_kernel(place, got, slab, v_out, c_out, w_low, w_high, block, sent, cut):
     n_z = got.shape[0]
     width = (got.shape[2] - 128) // 2
+    mate = 1 - place[1] % 2
+    half = w_low.shape[1] // width
+    slices = []
+    for number in range(2 * half):
+        lanes = pl.ds(pl.multiple_of((2 * number + mate) * width, width), width)
+        target = (w_low, w_high)[number // half]
+        slices.append(
+            pltpu.make_async_copy(
+                slab.at[:, lanes],
+                target.at[:, pl.ds(number % half * width, width)],
+                cut.at[number],
+            )
+        )
+    for copy in slices:
+        copy.start()
     row_id = lax.broadcasted_iota(jnp.int32, (8, 128), 0)
     maps = []
     for first in range(0, n_z, 4):
@@ -261,28 +282,32 @@
     for copy in copies:
         copy.start()
     fill(c_out, 1)
-    for copy in copies:
+    for copy in copies + slices:
         copy.wait()
 
 
-def pack(got, dests):
+def pack(place, got, slab, dests):
     n_z = got.shape[0]
-    width = (got.shape[2] - 128) // 2
+    width, grid_h = slab.shape
     shape = (8, n_z * width + 128 * (n_z // 4))
+    quarter = (width, grid_h // 4)
     return pl.pallas_call(
         pack_kernel,
-        in_specs=[VMEM],
-        out_specs=[HBM, VMEM],
+        in_specs=[SMEM, VMEM, HBM],
+        out_specs=[HBM, VMEM, HBM, HBM],
         out_shape=[
             pltpu.HBM((dests,) + shape, jnp.bfloat16),
             jax.ShapeDtypeStruct(shape, jnp.bfloat16),
+            pltpu.HBM(quarter, jnp.bfloat16),
+            pltpu.HBM(quarter, jnp.bfloat16),
         ],
         scratch_shapes=[
             pltpu.VMEM(shape, jnp.bfloat16),
             pltpu.SemaphoreType.DMA((dests,)),
+            pltpu.SemaphoreType.DMA((dests // 2,)),
         ],
         compiler_params=pltpu.CompilerParams(vmem_limit_bytes=8 * 1024 * 1024),
-    )(got)
+    )(place, got, *in_hbm(slab))
 
 
 def total_kernel(shares, out):
@@ -354,15 +379,16 @@
     sent = spread(place, cond, vale, gmap, n_z)
     got = lax.all_to_all(sent, "ka", 0, 0, axis_index_groups=along_z)
 
-    v_sent, c_keep = pack(got, n_ga)
-    v_sent, c_keep, slab = lax.optimization_barrier((v_sent, c_keep, screen[0]))
+    slab = screen[0]
+    v_sent, c_keep, w_low, w_high = pack(place, got, slab, n_ga)
     c_y = lax.ppermute(c_keep, "ka", swap_y)
     c_core = lax.ppermute(c_keep, "ga", swap_core)
     c_diag = lax.ppermute(c_keep, ("ka", "ga"), swap_both)
-    slab_mate = lax.ppermute(slab, "ga", swap_core)
+    w_low = lax.ppermute(w_low, "ga", swap_core)
+    w_high = lax.ppermute(w_high, "ga", swap_core)
     v_all = lax.all_to_all(v_sent, ("ka", "ga"), 0, 0, axis_index_groups=same_core)
 
-    part, plan = tiles(qtable, place, slab, slab_mate, v_all, c_keep, c_y, c_core, c_diag)
+    part, plan = tiles(qtable, place, slab, w_low, w_high, v_all, c_keep, c_y, c_core, c_diag)
     shares = lax.all_to_all(part, ("ka", "ga"), 0, 0, axis_index_groups=planes)
     rows = lax.all_to_all(totals(shares), "ka", 0, 0, axis_index_groups=along_z)
     return jnp.transpose(pick(plan, rows), (1, 0, 2))

time: 103 us -> 132 us (1.28)
  Pallas kernels: 10.8 us -> 43.3 us
  waiting for transfers between devices: 10.1 us -> 4.58 us
  starting transfers between devices: 22.2 us -> 24.8 us
  local copies, waits for them, and re-layouts: 1.52 us -> 0.01 us
    pallas_call x2, Pallas kernels: 8.84 us -> 41.2 us  [the longest x1 33.6 us: pack(): pl.pallas_call(pack_kernel, in_specs=[SMEM, VMEM, HBM], out_specs=[HBM, V...]
    ppermute x1, waiting for transfers between devices: 8.18 us -> 0.55 us  [per_device(): c_diag = lax.ppermute(c_keep, ('ka', 'ga'), swap_both)]
    ppermute x1, waiting for transfers between devices: 0.44 us -> 4.02 us  [per_device(): c_y = lax.ppermute(c_keep, 'ka', swap_y)]
    ppermute x1 -> x2, starting transfers between devices: 6.28 us -> 8.48 us  [the longest x1 6.56 us: per_device(): w_low = lax.ppermute(w_low, 'ga', swap_core)]
    all_to_all x1, waiting for transfers between devices: 1.52 us -> 0.01 us  [per_device(): lax.all_to_all(v_sent, ('ka', 'ga'), 0, 0, axis_index_groups=same_core)]
    unnamed x6 -> x4, local copies, waits for them, and re-layouts: 1.52 us -> 0.01 us
  transfers between devices with their start and end apart: 5 -> 6, of which waited for: 3 -> 2; matrix products, arithmetic and copies ran while one was open for 0% -> 0% of each run, Pallas kernels for 0% -> 0%
where the time goes in v8:
time: 132 us
  blocking collectives  59 us (45%)
  Pallas kernels  43.3 us (33%)
  starting transfers between devices  24.8 us (19%)
  waiting for transfers between devices  4.58 us (3%)
    pallas_call x1, Pallas kernels, pack(): pl.pallas_call(pack_kernel, in_specs=[SMEM, VMEM, HBM], out_specs=[HBM, V...  33.6 us
    all_to_all x1, blocking collectives, per_device(): got = lax.all_to_all(sent, 'ka', 0, 0, axis_index_groups=along_z)  27.8 us
    all_to_all x1, blocking collectives, per_device(): rows = lax.all_to_all(totals(shares), 'ka', 0, 0, axis_index_groups=along_z)  15.9 us
    all_to_all x1, blocking collectives, per_device(): shares = lax.all_to_all(part, ('ka', 'ga'), 0, 0, axis_index_groups=planes)  15.3 us
    pallas_call x1, Pallas kernels, tiles(): pl.pallas_call(tile_kernel, in_specs=[SMEM, SMEM, HBM, ANY, ANY, VMEM] +...  7.62 us
    all_to_all x1, starting transfers between devices, per_device(): lax.all_to_all(v_sent, ('ka', 'ga'), 0, 0, axis_index_groups=same_core)  6.9 us
    ppermute x1, starting transfers between devices, per_device(): w_low = lax.ppermute(w_low, 'ga', swap_core)  6.56 us
    ppermute x1, starting transfers between devices, per_device(): c_diag = lax.ppermute(c_keep, ('ka', 'ga'), swap_both)  5.43 us
  transfers between devices with their start and end apart: 6, of which 2 were waited for; matrix products, arithmetic and copies ran while one was open for 0% of the time, Pallas kernels for 0%

profile of v8, /device:TPU:1, one launch (start us, length us, event | category | flops | bytes accessed | tf_op | source)
XLA Modules:
  0.0 131.8 jit_solution(3849632536120969281)
XLA Ops:
  0.0 0.1 pad_add_fusion.place
  0.1 1.3 shard_map.55
  1.4 27.8 %all_to_all.20.got = bf16[16,8,640]{2,1,0:T(8,128)(2,1)S(1)} all-to-all(bf16[16,8,640]{2,1,0:T(8,128)(2,1)S(1)} %shard_map.55), channel_id=1, replica_groups={{0,16,32,48,64,80,96,112,128,144,160,176,192,208,224,240},{256,272,288,..., dimensions={0} | all-to-all | bytes 327680 | tf_op jit(solution)/shard_map/all_to_all | solution.py:380
  29.1 33.6 %shard_map.56 = (bf16[16,8,4608]{2,1,0:T(8,128)(2,1)}, bf16[8,4608]{1,0:T(8,128)(2,1)S(1)}, bf16[256,1024]{1,0:T(8,128)(2,1)}, bf16[256,1024]{1,0:T(8,128)(2,1)}) custom-call(s32[2]{0:T(128)S(1)} %pad_add_fusion.place, bf16[16,8,640]{2,1,0:T(8,128)(2,1)S(1)} %all_to_all.20.got, bf16[256,4096]{1,0:T(8,128)(2,1)} %bitcast.4), custom_call_target="tpu_custom_call" | custom-call | tf_op jit(solution)/shard_map/pallas_call | solution.py:294
  62.8 0.0 copy-start.1
  62.8 0.0 copy-start
  62.8 6.9 %all-to-all-start.1 = ((bf16[16,8,4608]{2,1,0:T(8,128)(2,1)}), bf16[16,8,4608]{2,1,0:T(8,128)(2,1)S(1)}, u32[]{:S(2)}, u32[]{:S(2)}) async-start(bf16[16,8,4608]{2,1,0:T(8,128)(2,1)} %get-tuple-element.13), calls=%async_computation.1 | async-start | bytes 2359296 | tf_op jit(solution)/shard_map/all_to_all | solution.py:389
  69.7 6.6 %collective-permute-start = (bf16[256,1024]{1,0:T(8,128)(2,1)}, bf16[256,1024]{1,0:T(8,128)(2,1)S(1)}, u32[]{:S(2)}, u32[]{:S(2)}) collective-permute-start(bf16[256,1024]{1,0:T(8,128)(2,1)} %get-tuple-element.11), channel_id=1, source_target_pairs={{0,1},{1,0},{2,3},{3,2},{4,5},{5,4},{6,7},{7,6},{8,9},{9,8},{10,11... | collective-permute-start | bytes 1572872 | tf_op jit(solution)/shard_map/ppermute | solution.py:387
  76.3 0.0 copy-done.1
  76.3 1.9 %collective-permute-start.1 = (bf16[256,1024]{1,0:T(8,128)(2,1)S(1)}, bf16[256,1024]{1,0:T(8,128)(2,1)S(1)}, u32[]{:S(2)}, u32[]{:S(2)}) collective-permute-start(bf16[256,1024]{1,0:T(8,128)(2,1)S(1)} %copy-done.1), channel_id=1, source_target_pairs={{0,1},{1,0},{2,3},{3,2},{4,5},{5,4},{6,7},{7,6},{8,9},{9,8},{10,11... | collective-permute-start | bytes 1572872 | tf_op jit(solution)/shard_map/ppermute | solution.py:388
  78.2 5.4 %collective-permute-start.4 = (bf16[8,4608]{1,0:T(8,128)(2,1)S(1)}, bf16[8,4608]{1,0:T(8,128)(2,1)S(1)}, u32[]{:S(2)}, u32[]{:S(2)}) collective-permute-start(bf16[8,4608]{1,0:T(8,128)(2,1)S(1)} %get-tuple-element.14.c_keep), channel_id=1, source_target_pairs={{0,257},{1,256},{2,259},{3,258},{4,261},{5,260},{6,263},{7,262},{8... | collective-permute-start | bytes 221192 | tf_op jit(solution)/shard_map/ppermute | solution.py:386
  83.6 1.9 %collective-permute-start.3 = (bf16[8,4608]{1,0:T(8,128)(2,1)S(1)}, bf16[8,4608]{1,0:T(8,128)(2,1)S(1)}, u32[]{:S(2)}, u32[]{:S(2)}) collective-permute-start(bf16[8,4608]{1,0:T(8,128)(2,1)S(1)} %get-tuple-element.14.c_keep), channel_id=1, source_target_pairs={{0,1},{1,0},{2,3},{3,2},{4,5},{5,4},{6,7},{7,6},{8,9},{9,8},{10,11... | collective-permute-start | bytes 221192 | tf_op jit(solution)/shard_map/ppermute | solution.py:385
  85.6 2.0 %collective-permute-start.2 = (bf16[8,4608]{1,0:T(8,128)(2,1)S(1)}, bf16[8,4608]{1,0:T(8,128)(2,1)S(1)}, u32[]{:S(2)}, u32[]{:S(2)}) collective-permute-start(bf16[8,4608]{1,0:T(8,128)(2,1)S(1)} %get-tuple-element.14.c_keep), channel_id=1, source_target_pairs={{0,256},{16,272},{32,288},{48,304},{64,320},{80,336},{96,352},{112... | collective-permute-start | bytes 221192 | tf_op jit(solution)/shard_map/ppermute | solution.py:384
  87.6 0.5 collective-permute-done.4.c_diag
  88.2 0.0 collective-permute-done.3.c_core
  88.2 4.0 %collective-permute-done.2.c_y = bf16[8,4608]{1,0:T(8,128)(2,1)S(1)} collective-permute-done((bf16[8,4608]{1,0:T(8,128)(2,1)S(1)}, bf16[8,4608]{1,0:T(8,128)(2,1)S(1)}, u32[]{:S(2)}, u32[]{:S(2)}) %collective-permute-start.2) | collective-permute-done | bytes 73760 | tf_op jit(solution)/shard_map/ppermute | solution.py:384
  92.2 0.0 collective-permute-done.w_low
  92.2 0.0 collective-permute-done.1.w_high
  92.2 0.0 all-to-all-done.1.vale
  92.2 0.0 copy-done
  92.2 7.6 %shard_map.57 = (bf16[32,32,128]{2,1,0:T(8,128)(2,1)S(1)}, s32[16,4,128]{2,1,0:T(4,128)S(1)}) custom-call(s32[32,32]{1,0:T(8,128)S(1)} %copy-done, s32[2]{0:T(128)S(1)} %pad_add_fusion.place, bf16[256,4096]{1,0:T(8,128)(2,1)} %bitcast.5, bf16[256,1024]{1,0:T(8,128)(2,1)S(1)} %collective-permute-done.w_low, ...), custom_call_target="tpu_custom_call" | custom-call | tf_op jit(solution)/shard_map/pallas_call | solution.py:184
  99.8 15.3 %all_to_all.21.shares = bf16[32,32,128]{2,1,0:T(8,128)(2,1)S(1)} all-to-all(bf16[32,32,128]{2,1,0:T(8,128)(2,1)S(1)} %get-tuple-element.16), channel_id=1, replica_groups={{0,1,2,3,4,5,6,7,8,9,10,11,12,13,14,15,256,257,258,259,260,261,262,263,..., dimensions={0} | all-to-all | bytes 524288 | tf_op jit(solution)/shard_map/all_to_all | solution.py:392
  115.2 0.1 shard_map.58
  115.3 15.9 %all_to_all.22.rows = f32[16,4,128]{2,1,0:T(4,128)S(1)} all-to-all(f32[16,4,128]{2,1,0:T(4,128)S(1)} %shard_map.58), channel_id=1, replica_groups={{0,16,32,48,64,80,96,112,128,144,160,176,192,208,224,240},{256,272,288,..., dimensions={0} | all-to-all | bytes 65536 | tf_op jit(solution)/shard_map/all_to_all | solution.py:393
  131.2 0.6 shard_map.59
Async XLA Ops:
  62.8 13.5 %copy-start.1 = (bf16[256,1024]{1,0:T(8,128)(2,1)S(1)}, bf16[256,1024]{1,0:T(8,128)(2,1)}, u32[]{:S(2)}) copy-start(bf16[256,1024]{1,0:T(8,128)(2,1)} %get-tuple-element.12) | copy-start | bytes 1572868
  62.8 29.4 %copy-start = (s32[32,32]{1,0:T(8,128)S(1)}, s32[32,32]{1,0:T(8,128)}, u32[]{:S(2)}) copy-start(s32[32,32]{1,0:T(8,128)} %table.1) | copy-start | bytes 12292
  62.8 29.4 %all-to-all-start.1 = ((bf16[16,8,4608]{2,1,0:T(8,128)(2,1)}), bf16[16,8,4608]{2,1,0:T(8,128)(2,1)S(1)}, u32[]{:S(2)}, u32[]{:S(2)}) async-start(bf16[16,8,4608]{2,1,0:T(8,128)(2,1)} %get-tuple-element.13), calls=%async_computation.1 | async-start | bytes 2359296 | tf_op jit(solution)/shard_map/all_to_all | solution.py:389
  69.7 22.5 %collective-permute-start = (bf16[256,1024]{1,0:T(8,128)(2,1)}, bf16[256,1024]{1,0:T(8,128)(2,1)S(1)}, u32[]{:S(2)}, u32[]{:S(2)}) collective-permute-start(bf16[256,1024]{1,0:T(8,128)(2,1)} %get-tuple-element.11), channel_id=1, source_target_pairs={{0,1},{1,0},{2,3},{3,2},{4,5},{5,4},{6,7},{7,6},{8,9},{9,8},{10,11... | collective-permute-start | bytes 1572872 | tf_op jit(solution)/shard_map/ppermute | solution.py:387
  76.3 15.9 %collective-permute-start.1 = (bf16[256,1024]{1,0:T(8,128)(2,1)S(1)}, bf16[256,1024]{1,0:T(8,128)(2,1)S(1)}, u32[]{:S(2)}, u32[]{:S(2)}) collective-permute-start(bf16[256,1024]{1,0:T(8,128)(2,1)S(1)} %copy-done.1), channel_id=1, source_target_pairs={{0,1},{1,0},{2,3},{3,2},{4,5},{5,4},{6,7},{7,6},{8,9},{9,8},{10,11... | collective-permute-start | bytes 1572872 | tf_op jit(solution)/shard_map/ppermute | solution.py:388
  78.2 9.9 %collective-permute-start.4 = (bf16[8,4608]{1,0:T(8,128)(2,1)S(1)}, bf16[8,4608]{1,0:T(8,128)(2,1)S(1)}, u32[]{:S(2)}, u32[]{:S(2)}) collective-permute-start(bf16[8,4608]{1,0:T(8,128)(2,1)S(1)} %get-tuple-element.14.c_keep), channel_id=1, source_target_pairs={{0,257},{1,256},{2,259},{3,258},{4,261},{5,260},{6,263},{7,262},{8... | collective-permute-start | bytes 221192 | tf_op jit(solution)/shard_map/ppermute | solution.py:386
  83.6 4.5 %collective-permute-start.3 = (bf16[8,4608]{1,0:T(8,128)(2,1)S(1)}, bf16[8,4608]{1,0:T(8,128)(2,1)S(1)}, u32[]{:S(2)}, u32[]{:S(2)}) collective-permute-start(bf16[8,4608]{1,0:T(8,128)(2,1)S(1)} %get-tuple-element.14.c_keep), channel_id=1, source_target_pairs={{0,1},{1,0},{2,3},{3,2},{4,5},{5,4},{6,7},{7,6},{8,9},{9,8},{10,11... | collective-permute-start | bytes 221192 | tf_op jit(solution)/shard_map/ppermute | solution.py:385
  85.6 6.6 %collective-permute-start.2 = (bf16[8,4608]{1,0:T(8,128)(2,1)S(1)}, bf16[8,4608]{1,0:T(8,128)(2,1)S(1)}, u32[]{:S(2)}, u32[]{:S(2)}) collective-permute-start(bf16[8,4608]{1,0:T(8,128)(2,1)S(1)} %get-tuple-element.14.c_keep), channel_id=1, source_target_pairs={{0,256},{16,272},{32,288},{48,304},{64,320},{80,336},{96,352},{112... | collective-permute-start | bytes 221192 | tf_op jit(solution)/shard_map/ppermute | solution.py:384

commit v9 on v7

--- a/solution.py
+++ b/solution.py
@@ -61,7 +61,7 @@
 
 
 def tile_kernel(
-    table, place, w_own, w_mate, vale, c_keep, c_y, c_core, c_diag, out, plan,
+    table, place, w_own, w_low, w_high, vale, c_keep, c_y, c_core, c_diag, out, plan,
     slabs, far_v, far_c, c_all, pv, pc, image, wide, arrived, joined,
 ):
     blocks = vale.shape[0] // 2
@@ -72,12 +72,18 @@
     shift = sum(jnp.where(table[by, 0] == my_ka, by, 0) for by in range(1, NSHIFT + 1))
     fetches = [
         pltpu.make_async_copy(
-            source.at[:, pl.ds(pl.multiple_of((2 * block + core) * width, width), width)],
-            slabs.at[side, :, pl.ds(block * width, width)],
-            arrived.at[side, block],
+            w_own.at[:, pl.ds(pl.multiple_of((2 * block + core) * width, width), width)],
+            slabs.at[0, :, pl.ds(block * width, width)],
+            arrived.at[block],
         )
         for block in range(blocks)
-        for side, source in enumerate((w_own, w_mate))
+    ]
+    half = w_low.shape[1]
+    fetches += [
+        pltpu.make_async_copy(
+            source, slabs.at[1, :, pl.ds(number * half, half)], arrived.at[blocks + number]
+        )
+        for number, source in enumerate((w_low, w_high))
     ]
     fetches += [
         pltpu.make_async_copy(source, c_all.at[side, y], joined.at[side, other])
@@ -168,7 +174,7 @@
     out[...] = wide[...].astype(jnp.bfloat16)
 
 
-def tiles(table, place, w_own, w_mate, vale, c_keep, c_y, c_core, c_diag):
+def tiles(table, place, w_own, w_low, w_high, vale, c_keep, c_y, c_core, c_diag):
     sources = vale.shape[0]
     width = w_own.shape[0]
     n_z = table.shape[0] // 2
@@ -177,7 +183,7 @@
     wide = max(len(chunk) for chunk in CHUNKS) * width
     return pl.pallas_call(
         tile_kernel,
-        in_specs=[SMEM, SMEM, HBM, ANY, VMEM] + [ANY] * 4,
+        in_specs=[SMEM, SMEM, HBM, ANY, ANY, VMEM] + [ANY] * 4,
         out_specs=[VMEM, VMEM],
         out_shape=[
             jax.ShapeDtypeStruct((2 * sources, 2 * n_z, 128), jnp.bfloat16),
@@ -192,11 +198,11 @@
             pltpu.VMEM((rows, 2 * width), jnp.bfloat16),
             pltpu.VMEM((rows, 2 * width), jnp.float32),
             pltpu.VMEM((2 * sources, 2 * n_z, 128), jnp.float32),
-            pltpu.SemaphoreType.DMA((2, blocks)),
+            pltpu.SemaphoreType.DMA((blocks + 2,)),
             pltpu.SemaphoreType.DMA((2, 2)),
         ],
         compiler_params=pltpu.CompilerParams(vmem_limit_bytes=28 * 1024 * 1024),
-    )(table, place, *in_hbm(w_own), w_mate, vale, c_keep, c_y, c_core, c_diag)
+    )(table, place, *in_hbm(w_own), w_low, w_high, vale, c_keep, c_y, c_core, c_diag)
 
 
 def spread_kernel(place, cond_in, vale_in, gmap_in, out, cond, vale, gmap, arrived):
@@ -354,15 +360,23 @@
     sent = spread(place, cond, vale, gmap, n_z)
     got = lax.all_to_all(sent, "ka", 0, 0, axis_index_groups=along_z)
 
+    slab = screen[0]
     v_sent, c_keep = pack(got, n_ga)
-    v_sent, c_keep, slab = lax.optimization_barrier((v_sent, c_keep, screen[0]))
+    width, grid_h = slab.shape
+    by_core = slab.reshape(width, 2, grid_h // (4 * width), 2, width)
+    other = 1 - my_ga % 2
+    w_low, w_high = (
+        lax.dynamic_index_in_dim(by_core[:, part], other, 2, keepdims=False).reshape(width, -1)
+        for part in range(2)
+    )
     c_y = lax.ppermute(c_keep, "ka", swap_y)
     c_core = lax.ppermute(c_keep, "ga", swap_core)
     c_diag = lax.ppermute(c_keep, ("ka", "ga"), swap_both)
-    slab_mate = lax.ppermute(slab, "ga", swap_core)
+    w_low = lax.ppermute(w_low, "ga", swap_core)
+    w_high = lax.ppermute(w_high, "ga", swap_core)
     v_all = lax.all_to_all(v_sent, ("ka", "ga"), 0, 0, axis_index_groups=same_core)
 
-    part, plan = tiles(qtable, place, slab, slab_mate, v_all, c_keep, c_y, c_core, c_diag)
+    part, plan = tiles(qtable, place, slab, w_low, w_high, v_all, c_keep, c_y, c_core, c_diag)
     shares = lax.all_to_all(part, ("ka", "ga"), 0, 0, axis_index_groups=planes)
     rows = lax.all_to_all(totals(shares), "ka", 0, 0, axis_index_groups=along_z)
     return jnp.transpose(pick(plan, rows), (1, 0, 2))

time: 103 us -> 111 us (1.078)
  local copies, waits for them, and re-layouts: 1.52 us -> 12.2 us
  waiting for transfers between devices: 10.1 us -> 5.15 us
  starting transfers between devices: 22.2 us -> 25.1 us
    dynamic_slice x0 -> x1, local copies, waits for them, and re-layouts: none -> 6.55 us  [per_device(): lax.dynamic_index_in_dim(by_core[:, part], other, 2, keepdims=False)]
    ppermute x1, starting transfers between devices: 5.23 us -> 2.1 us  [per_device(): c_diag = lax.ppermute(c_keep, ('ka', 'ga'), swap_both)]
    ppermute x1, waiting for transfers between devices: 8.18 us -> 5.14 us  [per_device(): c_diag = lax.ppermute(c_keep, ('ka', 'ga'), swap_both)]
    ppermute x1, starting transfers between devices: 2.02 us -> 5.05 us  [per_device(): c_y = lax.ppermute(c_keep, 'ka', swap_y)]
    another operation x0 -> x1, local copies, waits for them, and re-layouts: none -> 2.76 us  [per_device(): by_core = slab.reshape(width, 2, grid_h // (4 * width), 2, width)]
    slice x0 -> x1, local copies, waits for them, and re-layouts: none -> 2.69 us  [per_device(): by_core[:, part]]
    ppermute x1 -> x2, starting transfers between devices: 6.28 us -> 8.48 us  [the longest x1 6.56 us: per_device(): w_low = lax.ppermute(w_low, 'ga', swap_core)]
    all_to_all x1, waiting for transfers between devices: 1.52 us -> 0.01 us  [per_device(): lax.all_to_all(v_sent, ('ka', 'ga'), 0, 0, axis_index_groups=same_core)]
  transfers between devices with their start and end apart: 5 -> 6, of which waited for: 3 -> 1; matrix products, arithmetic and copies ran while one was open for 0% -> 11% of each run, Pallas kernels for 0% -> 0%
where the time goes in v9:
time: 111 us; the launch traced here: 110 us
  blocking collectives  56.9 us (51%)
  starting transfers between devices  25.1 us (23%)
  local copies, waits for them, and re-layouts  12.2 us (11%)
  Pallas kernels  10.8 us (10%)
  waiting for transfers between devices  5.15 us (5%)
    all_to_all x1, blocking collectives, per_device(): got = lax.all_to_all(sent, 'ka', 0, 0, axis_index_groups=along_z)  27.8 us
    all_to_all x1, blocking collectives, per_device(): rows = lax.all_to_all(totals(shares), 'ka', 0, 0, axis_index_groups=along_z)  15.3 us
    all_to_all x1, blocking collectives, per_device(): shares = lax.all_to_all(part, ('ka', 'ga'), 0, 0, axis_index_groups=planes)  13.8 us
    pallas_call x1, Pallas kernels, tiles(): pl.pallas_call(tile_kernel, in_specs=[SMEM, SMEM, HBM, ANY, ANY, VMEM] +...  7.62 us
    all_to_all x1, starting transfers between devices, per_device(): lax.all_to_all(v_sent, ('ka', 'ga'), 0, 0, axis_index_groups=same_core)  6.77 us
    ppermute x1, starting transfers between devices, per_device(): w_low = lax.ppermute(w_low, 'ga', swap_core)  6.56 us
    dynamic_slice x1, local copies, waits for them, and re-layouts, per_device(): lax.dynamic_index_in_dim(by_core[:, part], other, 2, keepdims=False)  6.55 us
    ppermute x1, waiting for transfers between devices, per_device(): c_diag = lax.ppermute(c_keep, ('ka', 'ga'), swap_both)  5.14 us
  transfers between devices with their start and end apart: 6, of which 1 were waited for; matrix products, arithmetic and copies ran while one was open for 11% of the time, Pallas kernels for 0%

profile of v9, /device:TPU:1, one launch (start us, length us, event | category | flops | bytes accessed | tf_op | source)
XLA Modules:
  0.0 110.4 jit_solution(9180812441998946971)
XLA Ops:
  0.0 0.0 copy-start.1
  0.0 0.1 pad_add_fusion.place
  0.1 1.3 %shard_map.55 = bf16[16,8,640]{2,1,0:T(8,128)(2,1)S(1)} custom-call(s32[2]{0:T(128)S(1)} %pad_add_fusion.place, bf16[1,8,256]{2,1,0:T(8,128)(2,1)} %cond_in.1, bf16[1,8,256]{2,1,0:T(8,128)(2,1)} %vale_in.1, s32[1,256]{1,0:T(1,128)} %gmap_in.1), custom_call_target="tpu_custom_call" | custom-call | tf_op jit(solution)/shard_map/pallas_call | solution.py:228
  1.4 27.8 %all_to_all.20.got = bf16[16,8,640]{2,1,0:T(8,128)(2,1)S(1)} all-to-all(bf16[16,8,640]{2,1,0:T(8,128)(2,1)S(1)} %shard_map.55), channel_id=1, replica_groups={{0,16,32,48,64,80,96,112,128,144,160,176,192,208,224,240},{256,272,288,..., dimensions={0} | all-to-all | bytes 327680 | tf_op jit(solution)/shard_map/all_to_all | solution.py:361
  29.2 1.2 %shard_map.56 = (bf16[16,8,4608]{2,1,0:T(8,128)(2,1)}, bf16[8,4608]{1,0:T(8,128)(2,1)S(1)}) custom-call(bf16[16,8,640]{2,1,0:T(8,128)(2,1)S(1)} %all_to_all.20.got), custom_call_target="tpu_custom_call" | custom-call | tf_op jit(solution)/shard_map/pallas_call | solution.py:278
  30.3 6.8 %all-to-all-start.1 = ((bf16[16,8,4608]{2,1,0:T(8,128)(2,1)}), bf16[16,8,4608]{2,1,0:T(8,128)(2,1)S(1)}, u32[]{:S(2)}, u32[]{:S(2)}) async-start(bf16[16,8,4608]{2,1,0:T(8,128)(2,1)} %get-tuple-element.9), calls=%async_computation.1 | async-start | bytes 2359296 | tf_op jit(solution)/shard_map/all_to_all | solution.py:377
  37.1 0.0 copy-done.1
  37.1 2.8 %reshape_squeeze.3 = bf16[256,2,4,2,256]{4,3,2,1,0:T(2,128)(2,1)} reshape(bf16[1,256,4096]{2,1,0:T(8,128)(2,1)S(1)} %copy-done.1) | data formatting | bytes 4194304 | tf_op jit(solution)/shard_map/reshape;squeeze | solution.py:366
  39.9 2.7 %fusion = (bf16[256,1,4,2,256]{4,3,2,1,0:T(2,128)(2,1)S(1)}, bf16[256,1,4,2,256]{4,3,2,1,0:T(2,128)(2,1)S(1)}) fusion(bf16[256,2,4,2,256]{4,3,2,1,0:T(2,128)(2,1)} %reshape_squeeze.3), kind=kLoop, calls=%fused_computation.3 | loop fusion | bytes 4194304 | tf_op jit(solution)/shard_map/slice | solution.py:369
  42.6 0.0 copy-start
  42.6 6.5 %dynamic-slice_reduce_fusion = (bf16[256,4,256]{2,1,0:T(4,128)(2,1)S(1)}, bf16[256,4,256]{2,1,0:T(4,128)(2,1)S(1)}) fusion(bf16[256,1,4,2,256]{4,3,2,1,0:T(2,128)(2,1)S(1)} %get-tuple-element.13, s32[]{:T(128)S(6)} %select_n.13, bf16[256,1,4,2,256]{4,3,2,1,0:T(2,128)(2,1)S(1)} %get-tuple-element.14), kind=kLoop, calls=%fused_computation | loop fusion | bytes 2097156 | tf_op jit(solution)/shard_map/jit(dynamic_index_in_dim)/dynamic_slice | solution.py:369
  49.2 0.1 copy.12
  49.3 6.6 %collective-permute-start = (bf16[256,1024]{1,0:T(8,128)(2,1)S(1)}, bf16[256,1024]{1,0:T(8,128)(2,1)S(1)}, u32[]{:S(2)}, u32[]{:S(2)}) collective-permute-start(bf16[256,1024]{1,0:T(8,128)(2,1)S(1)} %bitcast.11), channel_id=1, source_target_pairs={{0,1},{1,0},{2,3},{3,2},{4,5},{5,4},{6,7},{7,6},{8,9},{9,8},{10,11... | collective-permute-start | bytes 1572872 | tf_op jit(solution)/shard_map/ppermute | solution.py:375
  55.8 0.1 copy.13
  55.9 1.9 %collective-permute-start.1 = (bf16[256,1024]{1,0:T(8,128)(2,1)S(1)}, bf16[256,1024]{1,0:T(8,128)(2,1)S(1)}, u32[]{:S(2)}, u32[]{:S(2)}) collective-permute-start(bf16[256,1024]{1,0:T(8,128)(2,1)S(1)} %bitcast.12), channel_id=1, source_target_pairs={{0,1},{1,0},{2,3},{3,2},{4,5},{5,4},{6,7},{7,6},{8,9},{9,8},{10,11... | collective-permute-start | bytes 1572872 | tf_op jit(solution)/shard_map/ppermute | solution.py:376
  57.9 5.1 %collective-permute-start.2 = (bf16[8,4608]{1,0:T(8,128)(2,1)S(1)}, bf16[8,4608]{1,0:T(8,128)(2,1)S(1)}, u32[]{:S(2)}, u32[]{:S(2)}) collective-permute-start(bf16[8,4608]{1,0:T(8,128)(2,1)S(1)} %get-tuple-element.10.c_keep), channel_id=1, source_target_pairs={{0,256},{16,272},{32,288},{48,304},{64,320},{80,336},{96,352},{112... | collective-permute-start | bytes 221192 | tf_op jit(solution)/shard_map/ppermute | solution.py:372
  62.9 2.7 %collective-permute-start.3 = (bf16[8,4608]{1,0:T(8,128)(2,1)S(1)}, bf16[8,4608]{1,0:T(8,128)(2,1)S(1)}, u32[]{:S(2)}, u32[]{:S(2)}) collective-permute-start(bf16[8,4608]{1,0:T(8,128)(2,1)S(1)} %get-tuple-element.10.c_keep), channel_id=1, source_target_pairs={{0,1},{1,0},{2,3},{3,2},{4,5},{5,4},{6,7},{7,6},{8,9},{9,8},{10,11... | collective-permute-start | bytes 221192 | tf_op jit(solution)/shard_map/ppermute | solution.py:373
  65.6 2.1 %collective-permute-start.4 = (bf16[8,4608]{1,0:T(8,128)(2,1)S(1)}, bf16[8,4608]{1,0:T(8,128)(2,1)S(1)}, u32[]{:S(2)}, u32[]{:S(2)}) collective-permute-start(bf16[8,4608]{1,0:T(8,128)(2,1)S(1)} %get-tuple-element.10.c_keep), channel_id=1, source_target_pairs={{0,257},{1,256},{2,259},{3,258},{4,261},{5,260},{6,263},{7,262},{8... | collective-permute-start | bytes 221192 | tf_op jit(solution)/shard_map/ppermute | solution.py:374
  67.7 0.0 collective-permute-done.w_low
  67.7 0.0 collective-permute-done.1.w_high
  67.7 0.0 collective-permute-done.2.c_y
  67.8 0.0 collective-permute-done.3.c_core
  67.8 5.1 %collective-permute-done.4.c_diag = bf16[8,4608]{1,0:T(8,128)(2,1)S(1)} collective-permute-done((bf16[8,4608]{1,0:T(8,128)(2,1)S(1)}, bf16[8,4608]{1,0:T(8,128)(2,1)S(1)}, u32[]{:S(2)}, u32[]{:S(2)}) %collective-permute-start.4) | collective-permute-done | bytes 73760 | tf_op jit(solution)/shard_map/ppermute | solution.py:374
  72.9 0.0 all-to-all-done.1.vale
  72.9 0.0 copy-done
  72.9 7.6 %shard_map.57 = (bf16[32,32,128]{2,1,0:T(8,128)(2,1)S(1)}, s32[16,4,128]{2,1,0:T(4,128)S(1)}) custom-call(s32[32,32]{1,0:T(8,128)S(1)} %copy-done, s32[2]{0:T(128)S(1)} %pad_add_fusion.place, bf16[256,4096]{1,0:T(8,128)(2,1)} %bitcast.8, bf16[256,1024]{1,0:T(8,128)(2,1)S(1)} %collective-permute-done.w_low, ...), custom_call_target="tpu_custom_call" | custom-call | tf_op jit(solution)/shard_map/pallas_call | solution.py:184
  80.5 13.8 %all_to_all.21.shares = bf16[32,32,128]{2,1,0:T(8,128)(2,1)S(1)} all-to-all(bf16[32,32,128]{2,1,0:T(8,128)(2,1)S(1)} %get-tuple-element.12), channel_id=1, replica_groups={{0,1,2,3,4,5,6,7,8,9,10,11,12,13,14,15,256,257,258,259,260,261,262,263,..., dimensions={0} | all-to-all | bytes 524288 | tf_op jit(solution)/shard_map/all_to_all | solution.py:380
  94.3 0.1 shard_map.58
  94.5 15.3 %all_to_all.22.rows = f32[16,4,128]{2,1,0:T(4,128)S(1)} all-to-all(f32[16,4,128]{2,1,0:T(4,128)S(1)} %shard_map.58), channel_id=1, replica_groups={{0,16,32,48,64,80,96,112,128,144,160,176,192,208,224,240},{256,272,288,..., dimensions={0} | all-to-all | bytes 65536 | tf_op jit(solution)/shard_map/all_to_all | solution.py:381
  109.8 0.6 shard_map.59
Async XLA Ops:
  0.0 37.1 %copy-start.1 = (bf16[1,256,4096]{2,1,0:T(8,128)(2,1)S(1)}, bf16[1,256,4096]{2,1,0:T(8,128)(2,1)}, u32[]{:S(2)}) copy-start(bf16[1,256,4096]{2,1,0:T(8,128)(2,1)} %param.7) | copy-start | bytes 6291460
  30.3 42.6 %all-to-all-start.1 = ((bf16[16,8,4608]{2,1,0:T(8,128)(2,1)}), bf16[16,8,4608]{2,1,0:T(8,128)(2,1)S(1)}, u32[]{:S(2)}, u32[]{:S(2)}) async-start(bf16[16,8,4608]{2,1,0:T(8,128)(2,1)} %get-tuple-element.9), calls=%async_computation.1 | async-start | bytes 2359296 | tf_op jit(solution)/shard_map/all_to_all | solution.py:377
  42.6 30.3 %copy-start = (s32[32,32]{1,0:T(8,128)S(1)}, s32[32,32]{1,0:T(8,128)}, u32[]{:S(2)}) copy-start(s32[32,32]{1,0:T(8,128)} %table.1) | copy-start | bytes 12292
  49.3 18.5 %collective-permute-start = (bf16[256,1024]{1,0:T(8,128)(2,1)S(1)}, bf16[256,1024]{1,0:T(8,128)(2,1)S(1)}, u32[]{:S(2)}, u32[]{:S(2)}) collective-permute-start(bf16[256,1024]{1,0:T(8,128)(2,1)S(1)} %bitcast.11), channel_id=1, source_target_pairs={{0,1},{1,0},{2,3},{3,2},{4,5},{5,4},{6,7},{7,6},{8,9},{9,8},{10,11... | collective-permute-start | bytes 1572872 | tf_op jit(solution)/shard_map/ppermute | solution.py:375
  55.9 11.8 %collective-permute-start.1 = (bf16[256,1024]{1,0:T(8,128)(2,1)S(1)}, bf16[256,1024]{1,0:T(8,128)(2,1)S(1)}, u32[]{:S(2)}, u32[]{:S(2)}) collective-permute-start(bf16[256,1024]{1,0:T(8,128)(2,1)S(1)} %bitcast.12), channel_id=1, source_target_pairs={{0,1},{1,0},{2,3},{3,2},{4,5},{5,4},{6,7},{7,6},{8,9},{9,8},{10,11... | collective-permute-start | bytes 1572872 | tf_op jit(solution)/shard_map/ppermute | solution.py:376
  57.9 9.9 %collective-permute-start.2 = (bf16[8,4608]{1,0:T(8,128)(2,1)S(1)}, bf16[8,4608]{1,0:T(8,128)(2,1)S(1)}, u32[]{:S(2)}, u32[]{:S(2)}) collective-permute-start(bf16[8,4608]{1,0:T(8,128)(2,1)S(1)} %get-tuple-element.10.c_keep), channel_id=1, source_target_pairs={{0,256},{16,272},{32,288},{48,304},{64,320},{80,336},{96,352},{112... | collective-permute-start | bytes 221192 | tf_op jit(solution)/shard_map/ppermute | solution.py:372
  62.9 4.8 %collective-permute-start.3 = (bf16[8,4608]{1,0:T(8,128)(2,1)S(1)}, bf16[8,4608]{1,0:T(8,128)(2,1)S(1)}, u32[]{:S(2)}, u32[]{:S(2)}) collective-permute-start(bf16[8,4608]{1,0:T(8,128)(2,1)S(1)} %get-tuple-element.10.c_keep), channel_id=1, source_target_pairs={{0,1},{1,0},{2,3},{3,2},{4,5},{5,4},{6,7},{7,6},{8,9},{9,8},{10,11... | collective-permute-start | bytes 221192 | tf_op jit(solution)/shard_map/ppermute | solution.py:373
  65.6 7.3 %collective-permute-start.4 = (bf16[8,4608]{1,0:T(8,128)(2,1)S(1)}, bf16[8,4608]{1,0:T(8,128)(2,1)S(1)}, u32[]{:S(2)}, u32[]{:S(2)}) collective-permute-start(bf16[8,4608]{1,0:T(8,128)(2,1)S(1)} %get-tuple-element.10.c_keep), channel_id=1, source_target_pairs={{0,257},{1,256},{2,259},{3,258},{4,261},{5,260},{6,263},{7,262},{8... | collective-permute-start | bytes 221192 | tf_op jit(solution)/shard_map/ppermute | solution.py:374

commit v10 on v9

--- a/solution.py
+++ b/solution.py
@@ -291,6 +291,35 @@
     )(got)
 
 
+def cut_kernel(place, slab, w_low, w_high, whole, arrived):
+    width = slab.shape[0]
+    fetch = pltpu.make_async_copy(slab, whole, arrived)
+    fetch.start()
+    fetch.wait()
+    half = w_low.shape[1] // width
+    for number in range(2 * half):
+        block = 2 * number + 1 - place[1] % 2
+        lanes = pl.ds(pl.multiple_of(block * width, width), width)
+        target = (w_low, w_high)[number // half]
+        target[:, pl.ds(number % half * width, width)] = whole[:, lanes]
+
+
+def cut(place, slab):
+    width, grid_h = slab.shape
+    quarter = jax.ShapeDtypeStruct((width, grid_h // 4), jnp.bfloat16)
+    return pl.pallas_call(
+        cut_kernel,
+        in_specs=[SMEM, HBM],
+        out_specs=[VMEM, VMEM],
+        out_shape=[quarter, quarter],
+        scratch_shapes=[pltpu.VMEM(slab.shape, jnp.bfloat16), pltpu.SemaphoreType.DMA(())],
+        compiler_params=pltpu.CompilerParams(vmem_limit_bytes=6 * 1024 * 1024),
+        cost_estimate=pl.CostEstimate(
+            flops=0, bytes_accessed=3 * width * grid_h, transcendentals=0
+        ),
+    )(place, *in_hbm(slab))
+
+
 def total_kernel(shares, out):
     sources, rows, _ = shares.shape
     low = lax.broadcasted_iota(jnp.int32, (1, 128), 1) < 64
@@ -362,13 +391,7 @@
 
     slab = screen[0]
     v_sent, c_keep = pack(got, n_ga)
-    width, grid_h = slab.shape
-    by_core = slab.reshape(width, 2, grid_h // (4 * width), 2, width)
-    other = 1 - my_ga % 2
-    w_low, w_high = (
-        lax.dynamic_index_in_dim(by_core[:, part], other, 2, keepdims=False).reshape(width, -1)
-        for part in range(2)
-    )
+    w_low, w_high = cut(place, slab)
     c_y = lax.ppermute(c_keep, "ka", swap_y)
     c_core = lax.ppermute(c_keep, "ga", swap_core)
     c_diag = lax.ppermute(c_keep, ("ka", "ga"), swap_both)

time: 111 us -> 101 us (0.910)
  local copies, waits for them, and re-layouts: 12.2 us -> 0.01 us
  Pallas kernels: 10.8 us -> 13 us
  blocking collectives: 56.9 us -> 58.4 us
    dynamic_slice x1 -> x0, local copies, waits for them, and re-layouts: 6.55 us -> none  [per_device(): lax.dynamic_index_in_dim(by_core[:, part], other, 2, keepdims=False)]
    ppermute x1, waiting for transfers between devices: 5.14 us -> 0.01 us  [per_device(): c_diag = lax.ppermute(c_keep, ('ka', 'ga'), swap_both)]
    ppermute x1, waiting for transfers between devices: 0.01 us -> 4.53 us  [per_device(): c_y = lax.ppermute(c_keep, 'ka', swap_y)]
    ppermute x1, starting transfers between devices: 2.1 us -> 5.44 us  [per_device(): c_diag = lax.ppermute(c_keep, ('ka', 'ga'), swap_both)]
    ppermute x1, starting transfers between devices: 5.05 us -> 2.02 us  [per_device(): c_y = lax.ppermute(c_keep, 'ka', swap_y)]
    another operation x1 -> x0, local copies, waits for them, and re-layouts: 2.76 us -> none  [per_device(): by_core = slab.reshape(width, 2, grid_h // (4 * width), 2, width)]
    slice x1 -> x0, local copies, waits for them, and re-layouts: 2.69 us -> none  [per_device(): by_core[:, part]]
    pallas_call x0 -> x1, Pallas kernels: none -> 2.29 us  [cut(): pl.pallas_call(cut_kernel, in_specs=[SMEM, HBM], out_specs=[VMEM, VMEM],...]
  transfers between devices with their start and end apart: 6 -> 6, of which waited for: 1 -> 1; matrix products, arithmetic and copies ran while one was open for 11% -> 0% of each run, Pallas kernels for 0% -> 2%
where the time goes in v10:
time: 101 us
  blocking collectives  58.4 us (58%)
  starting transfers between devices  24.6 us (24%)
  Pallas kernels  13 us (13%)
  waiting for transfers between devices  4.54 us (4%)
    all_to_all x1, blocking collectives, per_device(): got = lax.all_to_all(sent, 'ka', 0, 0, axis_index_groups=along_z)  27.8 us
    all_to_all x1, blocking collectives, per_device(): shares = lax.all_to_all(part, ('ka', 'ga'), 0, 0, axis_index_groups=planes)  15.3 us
    all_to_all x1, blocking collectives, per_device(): rows = lax.all_to_all(totals(shares), 'ka', 0, 0, axis_index_groups=along_z)  15.3 us
    pallas_call x1, Pallas kernels, tiles(): pl.pallas_call(tile_kernel, in_specs=[SMEM, SMEM, HBM, ANY, ANY, VMEM] +...  7.57 us
    all_to_all x1, starting transfers between devices, per_device(): lax.all_to_all(v_sent, ('ka', 'ga'), 0, 0, axis_index_groups=same_core)  6.77 us
    ppermute x1, starting transfers between devices, per_device(): w_low = lax.ppermute(w_low, 'ga', swap_core)  6.56 us
    ppermute x1, starting transfers between devices, per_device(): c_diag = lax.ppermute(c_keep, ('ka', 'ga'), swap_both)  5.44 us
    ppermute x1, waiting for transfers between devices, per_device(): c_y = lax.ppermute(c_keep, 'ka', swap_y)  4.53 us
  transfers between devices with their start and end apart: 6, of which 1 were waited for; matrix products, arithmetic and copies ran while one was open for 0% of the time, Pallas kernels for 2%

profile of v10, /device:TPU:1, one launch (start us, length us, event | category | flops | bytes accessed | tf_op | source)
XLA Modules:
  0.0 100.9 jit_solution(2193942362781454483)
XLA Ops:
  0.0 0.1 pad_add_fusion.place
  0.1 1.3 %shard_map.56 = bf16[16,8,640]{2,1,0:T(8,128)(2,1)S(1)} custom-call(s32[2]{0:T(128)S(1)} %pad_add_fusion.place, bf16[1,8,256]{2,1,0:T(8,128)(2,1)} %cond_in.1, bf16[1,8,256]{2,1,0:T(8,128)(2,1)} %vale_in.1, s32[1,256]{1,0:T(1,128)} %gmap_in.1), custom_call_target="tpu_custom_call" | custom-call | tf_op jit(solution)/shard_map/pallas_call | solution.py:228
  1.4 27.8 %all_to_all.20.got = bf16[16,8,640]{2,1,0:T(8,128)(2,1)S(1)} all-to-all(bf16[16,8,640]{2,1,0:T(8,128)(2,1)S(1)} %shard_map.56), channel_id=1, replica_groups={{0,16,32,48,64,80,96,112,128,144,160,176,192,208,224,240},{256,272,288,..., dimensions={0} | all-to-all | bytes 327680 | tf_op jit(solution)/shard_map/all_to_all | solution.py:390
  29.1 1.2 %shard_map.57 = (bf16[16,8,4608]{2,1,0:T(8,128)(2,1)}, bf16[8,4608]{1,0:T(8,128)(2,1)S(1)}) custom-call(bf16[16,8,640]{2,1,0:T(8,128)(2,1)S(1)} %all_to_all.20.got), custom_call_target="tpu_custom_call" | custom-call | tf_op jit(solution)/shard_map/pallas_call | solution.py:278
  30.3 6.8 %all-to-all-start.1 = ((bf16[16,8,4608]{2,1,0:T(8,128)(2,1)}), bf16[16,8,4608]{2,1,0:T(8,128)(2,1)S(1)}, u32[]{:S(2)}, u32[]{:S(2)}) async-start(bf16[16,8,4608]{2,1,0:T(8,128)(2,1)} %get-tuple-element.13), calls=%async_computation.1 | async-start | bytes 2359296 | tf_op jit(solution)/shard_map/all_to_all | solution.py:400
  37.1 0.0 copy-start
  37.1 2.3 %shard_map.55 = (bf16[256,1024]{1,0:T(8,128)(2,1)S(1)}, bf16[256,1024]{1,0:T(8,128)(2,1)S(1)}) custom-call(s32[2]{0:T(128)S(1)} %pad_add_fusion.place, bf16[256,4096]{1,0:T(8,128)(2,1)} %bitcast.4), custom_call_target="tpu_custom_call" | custom-call | bytes 3145728 | tf_op jit(solution)/shard_map/pallas_call | solution.py:310
  39.4 6.6 %collective-permute-start = (bf16[256,1024]{1,0:T(8,128)(2,1)S(1)}, bf16[256,1024]{1,0:T(8,128)(2,1)S(1)}, u32[]{:S(2)}, u32[]{:S(2)}) collective-permute-start(bf16[256,1024]{1,0:T(8,128)(2,1)S(1)} %get-tuple-element.11), channel_id=1, source_target_pairs={{0,1},{1,0},{2,3},{3,2},{4,5},{5,4},{6,7},{7,6},{8,9},{9,8},{10,11... | collective-permute-start | bytes 1572872 | tf_op jit(solution)/shard_map/ppermute | solution.py:398
  46.0 1.9 %collective-permute-start.1 = (bf16[256,1024]{1,0:T(8,128)(2,1)S(1)}, bf16[256,1024]{1,0:T(8,128)(2,1)S(1)}, u32[]{:S(2)}, u32[]{:S(2)}) collective-permute-start(bf16[256,1024]{1,0:T(8,128)(2,1)S(1)} %get-tuple-element.12), channel_id=1, source_target_pairs={{0,1},{1,0},{2,3},{3,2},{4,5},{5,4},{6,7},{7,6},{8,9},{9,8},{10,11... | collective-permute-start | bytes 1572872 | tf_op jit(solution)/shard_map/ppermute | solution.py:399
  47.9 5.4 %collective-permute-start.4 = (bf16[8,4608]{1,0:T(8,128)(2,1)S(1)}, bf16[8,4608]{1,0:T(8,128)(2,1)S(1)}, u32[]{:S(2)}, u32[]{:S(2)}) collective-permute-start(bf16[8,4608]{1,0:T(8,128)(2,1)S(1)} %get-tuple-element.14.c_keep), channel_id=1, source_target_pairs={{0,257},{1,256},{2,259},{3,258},{4,261},{5,260},{6,263},{7,262},{8... | collective-permute-start | bytes 221192 | tf_op jit(solution)/shard_map/ppermute | solution.py:397
  53.4 1.9 %collective-permute-start.3 = (bf16[8,4608]{1,0:T(8,128)(2,1)S(1)}, bf16[8,4608]{1,0:T(8,128)(2,1)S(1)}, u32[]{:S(2)}, u32[]{:S(2)}) collective-permute-start(bf16[8,4608]{1,0:T(8,128)(2,1)S(1)} %get-tuple-element.14.c_keep), channel_id=1, source_target_pairs={{0,1},{1,0},{2,3},{3,2},{4,5},{5,4},{6,7},{7,6},{8,9},{9,8},{10,11... | collective-permute-start | bytes 221192 | tf_op jit(solution)/shard_map/ppermute | solution.py:396
  55.3 2.0 %collective-permute-start.2 = (bf16[8,4608]{1,0:T(8,128)(2,1)S(1)}, bf16[8,4608]{1,0:T(8,128)(2,1)S(1)}, u32[]{:S(2)}, u32[]{:S(2)}) collective-permute-start(bf16[8,4608]{1,0:T(8,128)(2,1)S(1)} %get-tuple-element.14.c_keep), channel_id=1, source_target_pairs={{0,256},{16,272},{32,288},{48,304},{64,320},{80,336},{96,352},{112... | collective-permute-start | bytes 221192 | tf_op jit(solution)/shard_map/ppermute | solution.py:395
  57.3 0.0 collective-permute-done.w_low
  57.3 0.0 collective-permute-done.1.w_high
  57.3 0.0 collective-permute-done.4.c_diag
  57.3 0.0 collective-permute-done.3.c_core
  57.4 4.5 %collective-permute-done.2.c_y = bf16[8,4608]{1,0:T(8,128)(2,1)S(1)} collective-permute-done((bf16[8,4608]{1,0:T(8,128)(2,1)S(1)}, bf16[8,4608]{1,0:T(8,128)(2,1)S(1)}, u32[]{:S(2)}, u32[]{:S(2)}) %collective-permute-start.2) | collective-permute-done | bytes 73760 | tf_op jit(solution)/shard_map/ppermute | solution.py:395
  61.9 0.0 all-to-all-done.1.vale
  61.9 0.0 copy-done
  61.9 7.6 %shard_map.58 = (bf16[32,32,128]{2,1,0:T(8,128)(2,1)S(1)}, s32[16,4,128]{2,1,0:T(4,128)S(1)}) custom-call(s32[32,32]{1,0:T(8,128)S(1)} %copy-done, s32[2]{0:T(128)S(1)} %pad_add_fusion.place, bf16[256,4096]{1,0:T(8,128)(2,1)} %bitcast.5, bf16[256,1024]{1,0:T(8,128)(2,1)S(1)} %collective-permute-done.w_low, ...), custom_call_target="tpu_custom_call" | custom-call | tf_op jit(solution)/shard_map/pallas_call | solution.py:184
  69.5 15.3 %all_to_all.21.shares = bf16[32,32,128]{2,1,0:T(8,128)(2,1)S(1)} all-to-all(bf16[32,32,128]{2,1,0:T(8,128)(2,1)S(1)} %get-tuple-element.16), channel_id=1, replica_groups={{0,1,2,3,4,5,6,7,8,9,10,11,12,13,14,15,256,257,258,259,260,261,262,263,..., dimensions={0} | all-to-all | bytes 524288 | tf_op jit(solution)/shard_map/all_to_all | solution.py:403
  84.8 0.1 shard_map.59
  84.9 15.3 %all_to_all.22.rows = f32[16,4,128]{2,1,0:T(4,128)S(1)} all-to-all(f32[16,4,128]{2,1,0:T(4,128)S(1)} %shard_map.59), channel_id=1, replica_groups={{0,16,32,48,64,80,96,112,128,144,160,176,192,208,224,240},{256,272,288,..., dimensions={0} | all-to-all | bytes 65536 | tf_op jit(solution)/shard_map/all_to_all | solution.py:404
  100.3 0.6 shard_map.60
Async XLA Ops:
  30.3 31.6 %all-to-all-start.1 = ((bf16[16,8,4608]{2,1,0:T(8,128)(2,1)}), bf16[16,8,4608]{2,1,0:T(8,128)(2,1)S(1)}, u32[]{:S(2)}, u32[]{:S(2)}) async-start(bf16[16,8,4608]{2,1,0:T(8,128)(2,1)} %get-tuple-element.13), calls=%async_computation.1 | async-start | bytes 2359296 | tf_op jit(solution)/shard_map/all_to_all | solution.py:400
  37.1 24.8 %copy-start = (s32[32,32]{1,0:T(8,128)S(1)}, s32[32,32]{1,0:T(8,128)}, u32[]{:S(2)}) copy-start(s32[32,32]{1,0:T(8,128)} %table.1) | copy-start | bytes 12292
  39.4 17.9 %collective-permute-start = (bf16[256,1024]{1,0:T(8,128)(2,1)S(1)}, bf16[256,1024]{1,0:T(8,128)(2,1)S(1)}, u32[]{:S(2)}, u32[]{:S(2)}) collective-permute-start(bf16[256,1024]{1,0:T(8,128)(2,1)S(1)} %get-tuple-element.11), channel_id=1, source_target_pairs={{0,1},{1,0},{2,3},{3,2},{4,5},{5,4},{6,7},{7,6},{8,9},{9,8},{10,11... | collective-permute-start | bytes 1572872 | tf_op jit(solution)/shard_map/ppermute | solution.py:398
  46.0 11.3 %collective-permute-start.1 = (bf16[256,1024]{1,0:T(8,128)(2,1)S(1)}, bf16[256,1024]{1,0:T(8,128)(2,1)S(1)}, u32[]{:S(2)}, u32[]{:S(2)}) collective-permute-start(bf16[256,1024]{1,0:T(8,128)(2,1)S(1)} %get-tuple-element.12), channel_id=1, source_target_pairs={{0,1},{1,0},{2,3},{3,2},{4,5},{5,4},{6,7},{7,6},{8,9},{9,8},{10,11... | collective-permute-start | bytes 1572872 | tf_op jit(solution)/shard_map/ppermute | solution.py:399
  47.9 9.4 %collective-permute-start.4 = (bf16[8,4608]{1,0:T(8,128)(2,1)S(1)}, bf16[8,4608]{1,0:T(8,128)(2,1)S(1)}, u32[]{:S(2)}, u32[]{:S(2)}) collective-permute-start(bf16[8,4608]{1,0:T(8,128)(2,1)S(1)} %get-tuple-element.14.c_keep), channel_id=1, source_target_pairs={{0,257},{1,256},{2,259},{3,258},{4,261},{5,260},{6,263},{7,262},{8... | collective-permute-start | bytes 221192 | tf_op jit(solution)/shard_map/ppermute | solution.py:397
  53.4 4.0 %collective-permute-start.3 = (bf16[8,4608]{1,0:T(8,128)(2,1)S(1)}, bf16[8,4608]{1,0:T(8,128)(2,1)S(1)}, u32[]{:S(2)}, u32[]{:S(2)}) collective-permute-start(bf16[8,4608]{1,0:T(8,128)(2,1)S(1)} %get-tuple-element.14.c_keep), channel_id=1, source_target_pairs={{0,1},{1,0},{2,3},{3,2},{4,5},{5,4},{6,7},{7,6},{8,9},{9,8},{10,11... | collective-permute-start | bytes 221192 | tf_op jit(solution)/shard_map/ppermute | solution.py:396
  55.3 6.6 %collective-permute-start.2 = (bf16[8,4608]{1,0:T(8,128)(2,1)S(1)}, bf16[8,4608]{1,0:T(8,128)(2,1)S(1)}, u32[]{:S(2)}, u32[]{:S(2)}) collective-permute-start(bf16[8,4608]{1,0:T(8,128)(2,1)S(1)} %get-tuple-element.14.c_keep), channel_id=1, source_target_pairs={{0,256},{16,272},{32,288},{48,304},{64,320},{80,336},{96,352},{112... | collective-permute-start | bytes 221192 | tf_op jit(solution)/shard_map/ppermute | solution.py:395

commit v11 on v10

--- a/solution.py
+++ b/solution.py
@@ -61,7 +61,7 @@
 
 
 def tile_kernel(
-    table, place, w_own, w_low, w_high, vale, c_keep, c_y, c_core, c_diag, out, plan,
+    table, place, w_own, w_mate, vale, c_keep, c_y, c_core, c_diag, out, plan,
     slabs, far_v, far_c, c_all, pv, pc, image, wide, arrived, joined,
 ):
     blocks = vale.shape[0] // 2
@@ -78,13 +78,7 @@
         )
         for block in range(blocks)
     ]
-    half = w_low.shape[1]
-    fetches += [
-        pltpu.make_async_copy(
-            source, slabs.at[1, :, pl.ds(number * half, half)], arrived.at[blocks + number]
-        )
-        for number, source in enumerate((w_low, w_high))
-    ]
+    fetches.append(pltpu.make_async_copy(w_mate, slabs.at[1], arrived.at[blocks]))
     fetches += [
         pltpu.make_async_copy(source, c_all.at[side, y], joined.at[side, other])
         for side, pair in enumerate(((c_keep, c_y), (c_core, c_diag)))
@@ -174,7 +168,7 @@
     out[...] = wide[...].astype(jnp.bfloat16)
 
 
-def tiles(table, place, w_own, w_low, w_high, vale, c_keep, c_y, c_core, c_diag):
+def tiles(table, place, w_own, w_mate, vale, c_keep, c_y, c_core, c_diag):
     sources = vale.shape[0]
     width = w_own.shape[0]
     n_z = table.shape[0] // 2
@@ -183,7 +177,7 @@
     wide = max(len(chunk) for chunk in CHUNKS) * width
     return pl.pallas_call(
         tile_kernel,
-        in_specs=[SMEM, SMEM, HBM, ANY, ANY, VMEM] + [ANY] * 4,
+        in_specs=[SMEM, SMEM, HBM, ANY, VMEM] + [ANY] * 4,
         out_specs=[VMEM, VMEM],
         out_shape=[
             jax.ShapeDtypeStruct((2 * sources, 2 * n_z, 128), jnp.bfloat16),
@@ -198,11 +192,11 @@
             pltpu.VMEM((rows, 2 * width), jnp.bfloat16),
             pltpu.VMEM((rows, 2 * width), jnp.float32),
             pltpu.VMEM((2 * sources, 2 * n_z, 128), jnp.float32),
-            pltpu.SemaphoreType.DMA((blocks + 2,)),
+            pltpu.SemaphoreType.DMA((blocks + 1,)),
             pltpu.SemaphoreType.DMA((2, 2)),
         ],
         compiler_params=pltpu.CompilerParams(vmem_limit_bytes=28 * 1024 * 1024),
-    )(table, place, *in_hbm(w_own), w_low, w_high, vale, c_keep, c_y, c_core, c_diag)
+    )(table, place, *in_hbm(w_own), w_mate, vale, c_keep, c_y, c_core, c_diag)
 
 
 def spread_kernel(place, cond_in, vale_in, gmap_in, out, cond, vale, gmap, arrived):
@@ -291,27 +285,24 @@
     )(got)
 
 
-def cut_kernel(place, slab, w_low, w_high, whole, arrived):
+def cut_kernel(place, slab, w_half, whole, arrived):
     width = slab.shape[0]
     fetch = pltpu.make_async_copy(slab, whole, arrived)
     fetch.start()
     fetch.wait()
-    half = w_low.shape[1] // width
-    for number in range(2 * half):
+    for number in range(w_half.shape[1] // width):
         block = 2 * number + 1 - place[1] % 2
         lanes = pl.ds(pl.multiple_of(block * width, width), width)
-        target = (w_low, w_high)[number // half]
-        target[:, pl.ds(number % half * width, width)] = whole[:, lanes]
+        w_half[:, pl.ds(number * width, width)] = whole[:, lanes]
 
 
 def cut(place, slab):
     width, grid_h = slab.shape
-    quarter = jax.ShapeDtypeStruct((width, grid_h // 4), jnp.bfloat16)
     return pl.pallas_call(
         cut_kernel,
         in_specs=[SMEM, HBM],
-        out_specs=[VMEM, VMEM],
-        out_shape=[quarter, quarter],
+        out_specs=VMEM,
+        out_shape=jax.ShapeDtypeStruct((width, grid_h // 2), jnp.bfloat16),
         scratch_shapes=[pltpu.VMEM(slab.shape, jnp.bfloat16), pltpu.SemaphoreType.DMA(())],
         compiler_params=pltpu.CompilerParams(vmem_limit_bytes=6 * 1024 * 1024),
         cost_estimate=pl.CostEstimate(
@@ -391,15 +382,14 @@
 
     slab = screen[0]
     v_sent, c_keep = pack(got, n_ga)
-    w_low, w_high = cut(place, slab)
+    w_mate = cut(place, slab)
     c_y = lax.ppermute(c_keep, "ka", swap_y)
     c_core = lax.ppermute(c_keep, "ga", swap_core)
     c_diag = lax.ppermute(c_keep, ("ka", "ga"), swap_both)
-    w_low = lax.ppermute(w_low, "ga", swap_core)
-    w_high = lax.ppermute(w_high, "ga", swap_core)
+    w_mate = lax.ppermute(w_mate, "ga", swap_core)
     v_all = lax.all_to_all(v_sent, ("ka", "ga"), 0, 0, axis_index_groups=same_core)
 
-    part, plan = tiles(qtable, place, slab, w_low, w_high, v_all, c_keep, c_y, c_core, c_diag)
+    part, plan = tiles(qtable, place, slab, w_mate, v_all, c_keep, c_y, c_core, c_diag)
     shares = lax.all_to_all(part, ("ka", "ga"), 0, 0, axis_index_groups=planes)
     rows = lax.all_to_all(totals(shares), "ka", 0, 0, axis_index_groups=along_z)
     return jnp.transpose(pick(plan, rows), (1, 0, 2))

time: 101 us -> 99.6 us (0.986)
  starting transfers between devices: 24.6 us -> 22.6 us
    ppermute x2 -> x1, starting transfers between devices: 8.48 us -> 6.56 us  [per_device(): w_mate = lax.ppermute(w_mate, 'ga', swap_core)]
  transfers between devices with their start and end apart: 6 -> 5, of which waited for: 1 -> 2; matrix products, arithmetic and copies ran while one was open for 0% -> 0% of each run, Pallas kernels for 2% -> 2%
where the time goes in v11:
time: 99.6 us; the launch traced here: 99.1 us
  blocking collectives  57.9 us (58%)
  starting transfers between devices  22.6 us (23%)
  Pallas kernels  13.1 us (13%)
  waiting for transfers between devices  5.36 us (5%)
    all_to_all x1, blocking collectives, per_device(): got = lax.all_to_all(sent, 'ka', 0, 0, axis_index_groups=along_z)  27.8 us
    all_to_all x1, blocking collectives, per_device(): rows = lax.all_to_all(totals(shares), 'ka', 0, 0, axis_index_groups=along_z)  15.7 us
    all_to_all x1, blocking collectives, per_device(): shares = lax.all_to_all(part, ('ka', 'ga'), 0, 0, axis_index_groups=planes)  14.5 us
    pallas_call x1, Pallas kernels, tiles(): pl.pallas_call(tile_kernel, in_specs=[SMEM, SMEM, HBM, ANY, VMEM] + [ANY]...  7.57 us
    all_to_all x1, starting transfers between devices, per_device(): lax.all_to_all(v_sent, ('ka', 'ga'), 0, 0, axis_index_groups=same_core)  6.77 us
    ppermute x1, starting transfers between devices, per_device(): w_mate = lax.ppermute(w_mate, 'ga', swap_core)  6.56 us
    ppermute x1, waiting for transfers between devices, per_device(): c_y = lax.ppermute(c_keep, 'ka', swap_y)  5.08 us
    ppermute x1, starting transfers between devices, per_device(): c_diag = lax.ppermute(c_keep, ('ka', 'ga'), swap_both)  4.95 us
  transfers between devices with their start and end apart: 5, of which 2 were waited for; matrix products, arithmetic and copies ran while one was open for 0% of the time, Pallas kernels for 2%

profile of v11, /device:TPU:1, one launch (start us, length us, event | category | flops | bytes accessed | tf_op | source)
XLA Modules:
  0.0 99.1 jit_solution(1617634291562167631)
XLA Ops:
  0.0 0.1 pad_add_fusion.place
  0.1 1.3 %shard_map.56 = bf16[16,8,640]{2,1,0:T(8,128)(2,1)S(1)} custom-call(s32[2]{0:T(128)S(1)} %pad_add_fusion.place, bf16[1,8,256]{2,1,0:T(8,128)(2,1)} %cond_in.1, bf16[1,8,256]{2,1,0:T(8,128)(2,1)} %vale_in.1, s32[1,256]{1,0:T(1,128)} %gmap_in.1), custom_call_target="tpu_custom_call" | custom-call | tf_op jit(solution)/shard_map/pallas_call | solution.py:222
  1.4 27.8 %all_to_all.20.got = bf16[16,8,640]{2,1,0:T(8,128)(2,1)S(1)} all-to-all(bf16[16,8,640]{2,1,0:T(8,128)(2,1)S(1)} %shard_map.56), channel_id=1, replica_groups={{0,16,32,48,64,80,96,112,128,144,160,176,192,208,224,240},{256,272,288,..., dimensions={0} | all-to-all | bytes 327680 | tf_op jit(solution)/shard_map/all_to_all | solution.py:381
  29.1 1.2 %shard_map.57 = (bf16[16,8,4608]{2,1,0:T(8,128)(2,1)}, bf16[8,4608]{1,0:T(8,128)(2,1)S(1)}) custom-call(bf16[16,8,640]{2,1,0:T(8,128)(2,1)S(1)} %all_to_all.20.got), custom_call_target="tpu_custom_call" | custom-call | tf_op jit(solution)/shard_map/pallas_call | solution.py:272
  30.3 6.8 %all-to-all-start.1 = ((bf16[16,8,4608]{2,1,0:T(8,128)(2,1)}), bf16[16,8,4608]{2,1,0:T(8,128)(2,1)S(1)}, u32[]{:S(2)}, u32[]{:S(2)}) async-start(bf16[16,8,4608]{2,1,0:T(8,128)(2,1)} %get-tuple-element.9), calls=%async_computation.1 | async-start | bytes 2359296 | tf_op jit(solution)/shard_map/all_to_all | solution.py:390
  37.1 0.0 copy-start
  37.1 2.3 %shard_map.55 = bf16[256,2048]{1,0:T(8,128)(2,1)S(1)} custom-call(s32[2]{0:T(128)S(1)} %pad_add_fusion.place, bf16[256,4096]{1,0:T(8,128)(2,1)} %bitcast.4), custom_call_target="tpu_custom_call" | custom-call | bytes 3145728 | tf_op jit(solution)/shard_map/pallas_call | solution.py:301
  39.4 6.6 %collective-permute-start = (bf16[256,2048]{1,0:T(8,128)(2,1)S(1)}, bf16[256,2048]{1,0:T(8,128)(2,1)S(1)}, u32[]{:S(2)}, u32[]{:S(2)}) collective-permute-start(bf16[256,2048]{1,0:T(8,128)(2,1)S(1)} %shard_map.55), channel_id=1, source_target_pairs={{0,1},{1,0},{2,3},{3,2},{4,5},{5,4},{6,7},{7,6},{8,9},{9,8},{10,11... | collective-permute-start | bytes 3145736 | tf_op jit(solution)/shard_map/ppermute | solution.py:389
  46.0 5.0 %collective-permute-start.3 = (bf16[8,4608]{1,0:T(8,128)(2,1)S(1)}, bf16[8,4608]{1,0:T(8,128)(2,1)S(1)}, u32[]{:S(2)}, u32[]{:S(2)}) collective-permute-start(bf16[8,4608]{1,0:T(8,128)(2,1)S(1)} %get-tuple-element.10.c_keep), channel_id=1, source_target_pairs={{0,257},{1,256},{2,259},{3,258},{4,261},{5,260},{6,263},{7,262},{8... | collective-permute-start | bytes 221192 | tf_op jit(solution)/shard_map/ppermute | solution.py:388
  51.0 2.4 %collective-permute-start.2 = (bf16[8,4608]{1,0:T(8,128)(2,1)S(1)}, bf16[8,4608]{1,0:T(8,128)(2,1)S(1)}, u32[]{:S(2)}, u32[]{:S(2)}) collective-permute-start(bf16[8,4608]{1,0:T(8,128)(2,1)S(1)} %get-tuple-element.10.c_keep), channel_id=1, source_target_pairs={{0,1},{1,0},{2,3},{3,2},{4,5},{5,4},{6,7},{7,6},{8,9},{9,8},{10,11... | collective-permute-start | bytes 221192 | tf_op jit(solution)/shard_map/ppermute | solution.py:387
  53.4 1.9 %collective-permute-start.1 = (bf16[8,4608]{1,0:T(8,128)(2,1)S(1)}, bf16[8,4608]{1,0:T(8,128)(2,1)S(1)}, u32[]{:S(2)}, u32[]{:S(2)}) collective-permute-start(bf16[8,4608]{1,0:T(8,128)(2,1)S(1)} %get-tuple-element.10.c_keep), channel_id=1, source_target_pairs={{0,256},{16,272},{32,288},{48,304},{64,320},{80,336},{96,352},{112... | collective-permute-start | bytes 221192 | tf_op jit(solution)/shard_map/ppermute | solution.py:386
  55.3 0.3 collective-permute-done.3.c_diag
  55.6 0.0 collective-permute-done.2.c_core
  55.6 5.1 %collective-permute-done.1.c_y = bf16[8,4608]{1,0:T(8,128)(2,1)S(1)} collective-permute-done((bf16[8,4608]{1,0:T(8,128)(2,1)S(1)}, bf16[8,4608]{1,0:T(8,128)(2,1)S(1)}, u32[]{:S(2)}, u32[]{:S(2)}) %collective-permute-start.1) | collective-permute-done | bytes 73760 | tf_op jit(solution)/shard_map/ppermute | solution.py:386
  60.7 0.0 collective-permute-done.w_mate
  60.7 0.0 all-to-all-done.1.vale
  60.7 0.0 copy-done
  60.7 7.6 %shard_map.58 = (bf16[32,32,128]{2,1,0:T(8,128)(2,1)S(1)}, s32[16,4,128]{2,1,0:T(4,128)S(1)}) custom-call(s32[32,32]{1,0:T(8,128)S(1)} %copy-done, s32[2]{0:T(128)S(1)} %pad_add_fusion.place, bf16[256,4096]{1,0:T(8,128)(2,1)} %bitcast.5, bf16[256,2048]{1,0:T(8,128)(2,1)S(1)} %collective-permute-done.w_mate, bf16[16,8,4608]{2,1,0:T(8,128)(2,1)S(1)} %all-to-all-done.1.vale, ...), custom_call_target="tpu_custom_call" | custom-call | tf_op jit(solution)/shard_map/pallas_call | solution.py:178
  68.2 14.5 %all_to_all.21.shares = bf16[32,32,128]{2,1,0:T(8,128)(2,1)S(1)} all-to-all(bf16[32,32,128]{2,1,0:T(8,128)(2,1)S(1)} %get-tuple-element.12), channel_id=1, replica_groups={{0,1,2,3,4,5,6,7,8,9,10,11,12,13,14,15,256,257,258,259,260,261,262,263,..., dimensions={0} | all-to-all | bytes 524288 | tf_op jit(solution)/shard_map/all_to_all | solution.py:393
  82.7 0.1 shard_map.59
  82.9 15.7 %all_to_all.22.rows = f32[16,4,128]{2,1,0:T(4,128)S(1)} all-to-all(f32[16,4,128]{2,1,0:T(4,128)S(1)} %shard_map.59), channel_id=1, replica_groups={{0,16,32,48,64,80,96,112,128,144,160,176,192,208,224,240},{256,272,288,..., dimensions={0} | all-to-all | bytes 65536 | tf_op jit(solution)/shard_map/all_to_all | solution.py:394
  98.5 0.6 shard_map.60
Async XLA Ops:
  30.3 30.3 %all-to-all-start.1 = ((bf16[16,8,4608]{2,1,0:T(8,128)(2,1)}), bf16[16,8,4608]{2,1,0:T(8,128)(2,1)S(1)}, u32[]{:S(2)}, u32[]{:S(2)}) async-start(bf16[16,8,4608]{2,1,0:T(8,128)(2,1)} %get-tuple-element.9), calls=%async_computation.1 | async-start | bytes 2359296 | tf_op jit(solution)/shard_map/all_to_all | solution.py:390
  37.1 23.5 %copy-start = (s32[32,32]{1,0:T(8,128)S(1)}, s32[32,32]{1,0:T(8,128)}, u32[]{:S(2)}) copy-start(s32[32,32]{1,0:T(8,128)} %table.1) | copy-start | bytes 12292
  39.4 21.2 %collective-permute-start = (bf16[256,2048]{1,0:T(8,128)(2,1)S(1)}, bf16[256,2048]{1,0:T(8,128)(2,1)S(1)}, u32[]{:S(2)}, u32[]{:S(2)}) collective-permute-start(bf16[256,2048]{1,0:T(8,128)(2,1)S(1)} %shard_map.55), channel_id=1, source_target_pairs={{0,1},{1,0},{2,3},{3,2},{4,5},{5,4},{6,7},{7,6},{8,9},{9,8},{10,11... | collective-permute-start | bytes 3145736 | tf_op jit(solution)/shard_map/ppermute | solution.py:389
  46.0 9.6 %collective-permute-start.3 = (bf16[8,4608]{1,0:T(8,128)(2,1)S(1)}, bf16[8,4608]{1,0:T(8,128)(2,1)S(1)}, u32[]{:S(2)}, u32[]{:S(2)}) collective-permute-start(bf16[8,4608]{1,0:T(8,128)(2,1)S(1)} %get-tuple-element.10.c_keep), channel_id=1, source_target_pairs={{0,257},{1,256},{2,259},{3,258},{4,261},{5,260},{6,263},{7,262},{8... | collective-permute-start | bytes 221192 | tf_op jit(solution)/shard_map/ppermute | solution.py:388
  51.0 4.6 %collective-permute-start.2 = (bf16[8,4608]{1,0:T(8,128)(2,1)S(1)}, bf16[8,4608]{1,0:T(8,128)(2,1)S(1)}, u32[]{:S(2)}, u32[]{:S(2)}) collective-permute-start(bf16[8,4608]{1,0:T(8,128)(2,1)S(1)} %get-tuple-element.10.c_keep), channel_id=1, source_target_pairs={{0,1},{1,0},{2,3},{3,2},{4,5},{5,4},{6,7},{7,6},{8,9},{9,8},{10,11... | collective-permute-start | bytes 221192 | tf_op jit(solution)/shard_map/ppermute | solution.py:387
  53.4 7.3 %collective-permute-start.1 = (bf16[8,4608]{1,0:T(8,128)(2,1)S(1)}, bf16[8,4608]{1,0:T(8,128)(2,1)S(1)}, u32[]{:S(2)}, u32[]{:S(2)}) collective-permute-start(bf16[8,4608]{1,0:T(8,128)(2,1)S(1)} %get-tuple-element.10.c_keep), channel_id=1, source_target_pairs={{0,256},{16,272},{32,288},{48,304},{64,320},{80,336},{96,352},{112... | collective-permute-start | bytes 221192 | tf_op jit(solution)/shard_map/ppermute | solution.py:386

commit v12 on v11

--- a/solution.py
+++ b/solution.py
@@ -383,8 +383,8 @@
     slab = screen[0]
     v_sent, c_keep = pack(got, n_ga)
     w_mate = cut(place, slab)
+    c_core = lax.ppermute(c_keep, "ga", swap_core)
     c_y = lax.ppermute(c_keep, "ka", swap_y)
-    c_core = lax.ppermute(c_keep, "ga", swap_core)
     c_diag = lax.ppermute(c_keep, ("ka", "ga"), swap_both)
     w_mate = lax.ppermute(w_mate, "ga", swap_core)
     v_all = lax.all_to_all(v_sent, ("ka", "ga"), 0, 0, axis_index_groups=same_core)

time: 99.6 us -> 99.6 us (level)
  no operation moved by 1% of the time
where the time goes in v12:
time: 99.6 us; the launch traced here: 99.1 us
  blocking collectives  57.9 us (58%)
  starting transfers between devices  22.6 us (23%)
  Pallas kernels  13.1 us (13%)
  waiting for transfers between devices  5.36 us (5%)
    all_to_all x1, blocking collectives, per_device(): got = lax.all_to_all(sent, 'ka', 0, 0, axis_index_groups=along_z)  27.8 us
    all_to_all x1, blocking collectives, per_device(): rows = lax.all_to_all(totals(shares), 'ka', 0, 0, axis_index_groups=along_z)  15.7 us
    all_to_all x1, blocking collectives, per_device(): shares = lax.all_to_all(part, ('ka', 'ga'), 0, 0, axis_index_groups=planes)  14.5 us
    pallas_call x1, Pallas kernels, tiles(): pl.pallas_call(tile_kernel, in_specs=[SMEM, SMEM, HBM, ANY, VMEM] + [ANY]...  7.57 us
    all_to_all x1, starting transfers between devices, per_device(): lax.all_to_all(v_sent, ('ka', 'ga'), 0, 0, axis_index_groups=same_core)  6.77 us
    ppermute x1, starting transfers between devices, per_device(): w_mate = lax.ppermute(w_mate, 'ga', swap_core)  6.56 us
    ppermute x1, waiting for transfers between devices, per_device(): c_y = lax.ppermute(c_keep, 'ka', swap_y)  5.08 us
    ppermute x1, starting transfers between devices, per_device(): c_diag = lax.ppermute(c_keep, ('ka', 'ga'), swap_both)  4.95 us
  transfers between devices with their start and end apart: 5, of which 2 were waited for; matrix products, arithmetic and copies ran while one was open for 0% of the time, Pallas kernels for 2%

profile of v12, /device:TPU:1, one launch (start us, length us, event | category | flops | bytes accessed | tf_op | source)
XLA Modules:
  0.0 99.1 jit_solution(1617634291562167631)
XLA Ops:
  0.0 0.1 pad_add_fusion.place
  0.1 1.3 %shard_map.56 = bf16[16,8,640]{2,1,0:T(8,128)(2,1)S(1)} custom-call(s32[2]{0:T(128)S(1)} %pad_add_fusion.place, bf16[1,8,256]{2,1,0:T(8,128)(2,1)} %cond_in.1, bf16[1,8,256]{2,1,0:T(8,128)(2,1)} %vale_in.1, s32[1,256]{1,0:T(1,128)} %gmap_in.1), custom_call_target="tpu_custom_call" | custom-call | tf_op jit(solution)/shard_map/pallas_call | solution.py:222
  1.4 27.8 %all_to_all.20.got = bf16[16,8,640]{2,1,0:T(8,128)(2,1)S(1)} all-to-all(bf16[16,8,640]{2,1,0:T(8,128)(2,1)S(1)} %shard_map.56), channel_id=1, replica_groups={{0,16,32,48,64,80,96,112,128,144,160,176,192,208,224,240},{256,272,288,..., dimensions={0} | all-to-all | bytes 327680 | tf_op jit(solution)/shard_map/all_to_all | solution.py:381
  29.1 1.2 %shard_map.57 = (bf16[16,8,4608]{2,1,0:T(8,128)(2,1)}, bf16[8,4608]{1,0:T(8,128)(2,1)S(1)}) custom-call(bf16[16,8,640]{2,1,0:T(8,128)(2,1)S(1)} %all_to_all.20.got), custom_call_target="tpu_custom_call" | custom-call | tf_op jit(solution)/shard_map/pallas_call | solution.py:272
  30.3 6.8 %all-to-all-start.1 = ((bf16[16,8,4608]{2,1,0:T(8,128)(2,1)}), bf16[16,8,4608]{2,1,0:T(8,128)(2,1)S(1)}, u32[]{:S(2)}, u32[]{:S(2)}) async-start(bf16[16,8,4608]{2,1,0:T(8,128)(2,1)} %get-tuple-element.9), calls=%async_computation.1 | async-start | bytes 2359296 | tf_op jit(solution)/shard_map/all_to_all | solution.py:390
  37.1 0.0 copy-start
  37.1 2.3 %shard_map.55 = bf16[256,2048]{1,0:T(8,128)(2,1)S(1)} custom-call(s32[2]{0:T(128)S(1)} %pad_add_fusion.place, bf16[256,4096]{1,0:T(8,128)(2,1)} %bitcast.4), custom_call_target="tpu_custom_call" | custom-call | bytes 3145728 | tf_op jit(solution)/shard_map/pallas_call | solution.py:301
  39.4 6.6 %collective-permute-start = (bf16[256,2048]{1,0:T(8,128)(2,1)S(1)}, bf16[256,2048]{1,0:T(8,128)(2,1)S(1)}, u32[]{:S(2)}, u32[]{:S(2)}) collective-permute-start(bf16[256,2048]{1,0:T(8,128)(2,1)S(1)} %shard_map.55), channel_id=1, source_target_pairs={{0,1},{1,0},{2,3},{3,2},{4,5},{5,4},{6,7},{7,6},{8,9},{9,8},{10,11... | collective-permute-start | bytes 3145736 | tf_op jit(solution)/shard_map/ppermute | solution.py:389
  46.0 5.0 %collective-permute-start.3 = (bf16[8,4608]{1,0:T(8,128)(2,1)S(1)}, bf16[8,4608]{1,0:T(8,128)(2,1)S(1)}, u32[]{:S(2)}, u32[]{:S(2)}) collective-permute-start(bf16[8,4608]{1,0:T(8,128)(2,1)S(1)} %get-tuple-element.10.c_keep), channel_id=1, source_target_pairs={{0,257},{1,256},{2,259},{3,258},{4,261},{5,260},{6,263},{7,262},{8... | collective-permute-start | bytes 221192 | tf_op jit(solution)/shard_map/ppermute | solution.py:388
  51.0 2.4 %collective-permute-start.2 = (bf16[8,4608]{1,0:T(8,128)(2,1)S(1)}, bf16[8,4608]{1,0:T(8,128)(2,1)S(1)}, u32[]{:S(2)}, u32[]{:S(2)}) collective-permute-start(bf16[8,4608]{1,0:T(8,128)(2,1)S(1)} %get-tuple-element.10.c_keep), channel_id=1, source_target_pairs={{0,1},{1,0},{2,3},{3,2},{4,5},{5,4},{6,7},{7,6},{8,9},{9,8},{10,11... | collective-permute-start | bytes 221192 | tf_op jit(solution)/shard_map/ppermute | solution.py:386
  53.4 1.9 %collective-permute-start.1 = (bf16[8,4608]{1,0:T(8,128)(2,1)S(1)}, bf16[8,4608]{1,0:T(8,128)(2,1)S(1)}, u32[]{:S(2)}, u32[]{:S(2)}) collective-permute-start(bf16[8,4608]{1,0:T(8,128)(2,1)S(1)} %get-tuple-element.10.c_keep), channel_id=1, source_target_pairs={{0,256},{16,272},{32,288},{48,304},{64,320},{80,336},{96,352},{112... | collective-permute-start | bytes 221192 | tf_op jit(solution)/shard_map/ppermute | solution.py:387
  55.3 0.3 collective-permute-done.3.c_diag
  55.6 0.0 collective-permute-done.2.c_core
  55.6 5.1 %collective-permute-done.1.c_y = bf16[8,4608]{1,0:T(8,128)(2,1)S(1)} collective-permute-done((bf16[8,4608]{1,0:T(8,128)(2,1)S(1)}, bf16[8,4608]{1,0:T(8,128)(2,1)S(1)}, u32[]{:S(2)}, u32[]{:S(2)}) %collective-permute-start.1) | collective-permute-done | bytes 73760 | tf_op jit(solution)/shard_map/ppermute | solution.py:387
  60.7 0.0 collective-permute-done.w_mate
  60.7 0.0 all-to-all-done.1.vale
  60.7 0.0 copy-done
  60.7 7.6 %shard_map.58 = (bf16[32,32,128]{2,1,0:T(8,128)(2,1)S(1)}, s32[16,4,128]{2,1,0:T(4,128)S(1)}) custom-call(s32[32,32]{1,0:T(8,128)S(1)} %copy-done, s32[2]{0:T(128)S(1)} %pad_add_fusion.place, bf16[256,4096]{1,0:T(8,128)(2,1)} %bitcast.5, bf16[256,2048]{1,0:T(8,128)(2,1)S(1)} %collective-permute-done.w_mate, bf16[16,8,4608]{2,1,0:T(8,128)(2,1)S(1)} %all-to-all-done.1.vale, ...), custom_call_target="tpu_custom_call" | custom-call | tf_op jit(solution)/shard_map/pallas_call | solution.py:178
  68.2 14.5 %all_to_all.21.shares = bf16[32,32,128]{2,1,0:T(8,128)(2,1)S(1)} all-to-all(bf16[32,32,128]{2,1,0:T(8,128)(2,1)S(1)} %get-tuple-element.12), channel_id=1, replica_groups={{0,1,2,3,4,5,6,7,8,9,10,11,12,13,14,15,256,257,258,259,260,261,262,263,..., dimensions={0} | all-to-all | bytes 524288 | tf_op jit(solution)/shard_map/all_to_all | solution.py:393
  82.7 0.1 shard_map.59
  82.9 15.7 %all_to_all.22.rows = f32[16,4,128]{2,1,0:T(4,128)S(1)} all-to-all(f32[16,4,128]{2,1,0:T(4,128)S(1)} %shard_map.59), channel_id=1, replica_groups={{0,16,32,48,64,80,96,112,128,144,160,176,192,208,224,240},{256,272,288,..., dimensions={0} | all-to-all | bytes 65536 | tf_op jit(solution)/shard_map/all_to_all | solution.py:394
  98.5 0.6 shard_map.60
Async XLA Ops:
  30.3 30.3 %all-to-all-start.1 = ((bf16[16,8,4608]{2,1,0:T(8,128)(2,1)}), bf16[16,8,4608]{2,1,0:T(8,128)(2,1)S(1)}, u32[]{:S(2)}, u32[]{:S(2)}) async-start(bf16[16,8,4608]{2,1,0:T(8,128)(2,1)} %get-tuple-element.9), calls=%async_computation.1 | async-start | bytes 2359296 | tf_op jit(solution)/shard_map/all_to_all | solution.py:390
  37.1 23.5 %copy-start = (s32[32,32]{1,0:T(8,128)S(1)}, s32[32,32]{1,0:T(8,128)}, u32[]{:S(2)}) copy-start(s32[32,32]{1,0:T(8,128)} %table.1) | copy-start | bytes 12292
  39.4 21.2 %collective-permute-start = (bf16[256,2048]{1,0:T(8,128)(2,1)S(1)}, bf16[256,2048]{1,0:T(8,128)(2,1)S(1)}, u32[]{:S(2)}, u32[]{:S(2)}) collective-permute-start(bf16[256,2048]{1,0:T(8,128)(2,1)S(1)} %shard_map.55), channel_id=1, source_target_pairs={{0,1},{1,0},{2,3},{3,2},{4,5},{5,4},{6,7},{7,6},{8,9},{9,8},{10,11... | collective-permute-start | bytes 3145736 | tf_op jit(solution)/shard_map/ppermute | solution.py:389
  46.0 9.6 %collective-permute-start.3 = (bf16[8,4608]{1,0:T(8,128)(2,1)S(1)}, bf16[8,4608]{1,0:T(8,128)(2,1)S(1)}, u32[]{:S(2)}, u32[]{:S(2)}) collective-permute-start(bf16[8,4608]{1,0:T(8,128)(2,1)S(1)} %get-tuple-element.10.c_keep), channel_id=1, source_target_pairs={{0,257},{1,256},{2,259},{3,258},{4,261},{5,260},{6,263},{7,262},{8... | collective-permute-start | bytes 221192 | tf_op jit(solution)/shard_map/ppermute | solution.py:388
  51.0 4.6 %collective-permute-start.2 = (bf16[8,4608]{1,0:T(8,128)(2,1)S(1)}, bf16[8,4608]{1,0:T(8,128)(2,1)S(1)}, u32[]{:S(2)}, u32[]{:S(2)}) collective-permute-start(bf16[8,4608]{1,0:T(8,128)(2,1)S(1)} %get-tuple-element.10.c_keep), channel_id=1, source_target_pairs={{0,1},{1,0},{2,3},{3,2},{4,5},{5,4},{6,7},{7,6},{8,9},{9,8},{10,11... | collective-permute-start | bytes 221192 | tf_op jit(solution)/shard_map/ppermute | solution.py:386
  53.4 7.3 %collective-permute-start.1 = (bf16[8,4608]{1,0:T(8,128)(2,1)S(1)}, bf16[8,4608]{1,0:T(8,128)(2,1)S(1)}, u32[]{:S(2)}, u32[]{:S(2)}) collective-permute-start(bf16[8,4608]{1,0:T(8,128)(2,1)S(1)} %get-tuple-element.10.c_keep), channel_id=1, source_target_pairs={{0,256},{16,272},{32,288},{48,304},{64,320},{80,336},{96,352},{112... | collective-permute-start | bytes 221192 | tf_op jit(solution)/shard_map/ppermute | solution.py:387

commit v13 on v12

--- a/solution.py
+++ b/solution.py
@@ -61,7 +61,7 @@
 
 
 def tile_kernel(
-    table, place, w_own, w_mate, vale, c_keep, c_y, c_core, c_diag, out, plan,
+    table, place, w_own, w_mate, vale, c_keep, c_core, c_y, c_diag, out, plan,
     slabs, far_v, far_c, c_all, pv, pc, image, wide, arrived, joined,
 ):
     blocks = vale.shape[0] // 2
@@ -168,7 +168,7 @@
     out[...] = wide[...].astype(jnp.bfloat16)
 
 
-def tiles(table, place, w_own, w_mate, vale, c_keep, c_y, c_core, c_diag):
+def tiles(table, place, w_own, w_mate, vale, c_keep, c_core, c_y, c_diag):
     sources = vale.shape[0]
     width = w_own.shape[0]
     n_z = table.shape[0] // 2
@@ -196,7 +196,7 @@
             pltpu.SemaphoreType.DMA((2, 2)),
         ],
         compiler_params=pltpu.CompilerParams(vmem_limit_bytes=28 * 1024 * 1024),
-    )(table, place, *in_hbm(w_own), w_mate, vale, c_keep, c_y, c_core, c_diag)
+    )(table, place, *in_hbm(w_own), w_mate, vale, c_keep, c_core, c_y, c_diag)
 
 
 def spread_kernel(place, cond_in, vale_in, gmap_in, out, cond, vale, gmap, arrived):
@@ -389,7 +389,7 @@
     w_mate = lax.ppermute(w_mate, "ga", swap_core)
     v_all = lax.all_to_all(v_sent, ("ka", "ga"), 0, 0, axis_index_groups=same_core)
 
-    part, plan = tiles(qtable, place, slab, w_mate, v_all, c_keep, c_y, c_core, c_diag)
+    part, plan = tiles(qtable, place, slab, w_mate, v_all, c_keep, c_core, c_y, c_diag)
     shares = lax.all_to_all(part, ("ka", "ga"), 0, 0, axis_index_groups=planes)
     rows = lax.all_to_all(totals(shares), "ka", 0, 0, axis_index_groups=along_z)
     return jnp.transpose(pick(plan, rows), (1, 0, 2))

time: 99.6 us -> 99.6 us (level)
  waiting for transfers between devices: 5.36 us -> 3.6 us
  blocking collectives: 57.9 us -> 59.6 us
    all_to_all x1, blocking collectives: 15.7 us -> 17.9 us  [per_device(): rows = lax.all_to_all(totals(shares), 'ka', 0, 0, axis_index_groups=along_z)]
    ppermute x1, waiting for transfers between devices: 5.08 us -> 3.41 us  [per_device(): c_y = lax.ppermute(c_keep, 'ka', swap_y)]
where the time goes in v13:
time: 99.6 us; the launch traced here: 99.1 us
  blocking collectives  59.6 us (60%)
  starting transfers between devices  22.7 us (23%)
  Pallas kernels  13.1 us (13%)
  waiting for transfers between devices  3.6 us (4%)
    all_to_all x1, blocking collectives, per_device(): got = lax.all_to_all(sent, 'ka', 0, 0, axis_index_groups=along_z)  27.8 us
    all_to_all x1, blocking collectives, per_device(): rows = lax.all_to_all(totals(shares), 'ka', 0, 0, axis_index_groups=along_z)  17.9 us
    all_to_all x1, blocking collectives, per_device(): shares = lax.all_to_all(part, ('ka', 'ga'), 0, 0, axis_index_groups=planes)  13.9 us
    pallas_call x1, Pallas kernels, tiles(): pl.pallas_call(tile_kernel, in_specs=[SMEM, SMEM, HBM, ANY, VMEM] + [ANY]...  7.57 us
    all_to_all x1, starting transfers between devices, per_device(): lax.all_to_all(v_sent, ('ka', 'ga'), 0, 0, axis_index_groups=same_core)  6.77 us
    ppermute x1, starting transfers between devices, per_device(): w_mate = lax.ppermute(w_mate, 'ga', swap_core)  6.56 us
    ppermute x1, starting transfers between devices, per_device(): c_diag = lax.ppermute(c_keep, ('ka', 'ga'), swap_both)  4.95 us
    ppermute x1, waiting for transfers between devices, per_device(): c_y = lax.ppermute(c_keep, 'ka', swap_y)  3.41 us
  transfers between devices with their start and end apart: 5, of which 2 were waited for; matrix products, arithmetic and copies ran while one was open for 0% of the time, Pallas kernels for 2%

profile of v13, /device:TPU:1, one launch (start us, length us, event | category | flops | bytes accessed | tf_op | source)
XLA Modules:
  0.0 99.1 jit_solution(12291558681873252488)
XLA Ops:
  0.0 0.1 pad_add_fusion.place
  0.1 1.3 %shard_map.56 = bf16[16,8,640]{2,1,0:T(8,128)(2,1)S(1)} custom-call(s32[2]{0:T(128)S(1)} %pad_add_fusion.place, bf16[1,8,256]{2,1,0:T(8,128)(2,1)} %cond_in.1, bf16[1,8,256]{2,1,0:T(8,128)(2,1)} %vale_in.1, s32[1,256]{1,0:T(1,128)} %gmap_in.1), custom_call_target="tpu_custom_call" | custom-call | tf_op jit(solution)/shard_map/pallas_call | solution.py:222
  1.4 27.8 %all_to_all.20.got = bf16[16,8,640]{2,1,0:T(8,128)(2,1)S(1)} all-to-all(bf16[16,8,640]{2,1,0:T(8,128)(2,1)S(1)} %shard_map.56), channel_id=1, replica_groups={{0,16,32,48,64,80,96,112,128,144,160,176,192,208,224,240},{256,272,288,..., dimensions={0} | all-to-all | bytes 327680 | tf_op jit(solution)/shard_map/all_to_all | solution.py:381
  29.1 1.2 %shard_map.57 = (bf16[16,8,4608]{2,1,0:T(8,128)(2,1)}, bf16[8,4608]{1,0:T(8,128)(2,1)S(1)}) custom-call(bf16[16,8,640]{2,1,0:T(8,128)(2,1)S(1)} %all_to_all.20.got), custom_call_target="tpu_custom_call" | custom-call | tf_op jit(solution)/shard_map/pallas_call | solution.py:272
  30.3 6.8 %all-to-all-start.1 = ((bf16[16,8,4608]{2,1,0:T(8,128)(2,1)}), bf16[16,8,4608]{2,1,0:T(8,128)(2,1)S(1)}, u32[]{:S(2)}, u32[]{:S(2)}) async-start(bf16[16,8,4608]{2,1,0:T(8,128)(2,1)} %get-tuple-element.9), calls=%async_computation.1 | async-start | bytes 2359296 | tf_op jit(solution)/shard_map/all_to_all | solution.py:390
  37.1 0.0 copy-start
  37.1 2.3 %shard_map.55 = bf16[256,2048]{1,0:T(8,128)(2,1)S(1)} custom-call(s32[2]{0:T(128)S(1)} %pad_add_fusion.place, bf16[256,4096]{1,0:T(8,128)(2,1)} %bitcast.4), custom_call_target="tpu_custom_call" | custom-call | bytes 3145728 | tf_op jit(solution)/shard_map/pallas_call | solution.py:301
  39.4 6.6 %collective-permute-start = (bf16[256,2048]{1,0:T(8,128)(2,1)S(1)}, bf16[256,2048]{1,0:T(8,128)(2,1)S(1)}, u32[]{:S(2)}, u32[]{:S(2)}) collective-permute-start(bf16[256,2048]{1,0:T(8,128)(2,1)S(1)} %shard_map.55), channel_id=1, source_target_pairs={{0,1},{1,0},{2,3},{3,2},{4,5},{5,4},{6,7},{7,6},{8,9},{9,8},{10,11... | collective-permute-start | bytes 3145736 | tf_op jit(solution)/shard_map/ppermute | solution.py:389
  46.0 5.0 %collective-permute-start.3 = (bf16[8,4608]{1,0:T(8,128)(2,1)S(1)}, bf16[8,4608]{1,0:T(8,128)(2,1)S(1)}, u32[]{:S(2)}, u32[]{:S(2)}) collective-permute-start(bf16[8,4608]{1,0:T(8,128)(2,1)S(1)} %get-tuple-element.10.c_keep), channel_id=1, source_target_pairs={{0,257},{1,256},{2,259},{3,258},{4,261},{5,260},{6,263},{7,262},{8... | collective-permute-start | bytes 221192 | tf_op jit(solution)/shard_map/ppermute | solution.py:388
  51.0 2.0 %collective-permute-start.2 = (bf16[8,4608]{1,0:T(8,128)(2,1)S(1)}, bf16[8,4608]{1,0:T(8,128)(2,1)S(1)}, u32[]{:S(2)}, u32[]{:S(2)}) collective-permute-start(bf16[8,4608]{1,0:T(8,128)(2,1)S(1)} %get-tuple-element.10.c_keep), channel_id=1, source_target_pairs={{0,256},{16,272},{32,288},{48,304},{64,320},{80,336},{96,352},{112... | collective-permute-start | bytes 221192 | tf_op jit(solution)/shard_map/ppermute | solution.py:387
  53.0 2.4 %collective-permute-start.1 = (bf16[8,4608]{1,0:T(8,128)(2,1)S(1)}, bf16[8,4608]{1,0:T(8,128)(2,1)S(1)}, u32[]{:S(2)}, u32[]{:S(2)}) collective-permute-start(bf16[8,4608]{1,0:T(8,128)(2,1)S(1)} %get-tuple-element.10.c_keep), channel_id=1, source_target_pairs={{0,1},{1,0},{2,3},{3,2},{4,5},{5,4},{6,7},{7,6},{8,9},{9,8},{10,11... | collective-permute-start | bytes 221192 | tf_op jit(solution)/shard_map/ppermute | solution.py:386
  55.4 0.2 collective-permute-done.3.c_diag
  55.6 3.4 %collective-permute-done.2.c_y = bf16[8,4608]{1,0:T(8,128)(2,1)S(1)} collective-permute-done((bf16[8,4608]{1,0:T(8,128)(2,1)S(1)}, bf16[8,4608]{1,0:T(8,128)(2,1)S(1)}, u32[]{:S(2)}, u32[]{:S(2)}) %collective-permute-start.2) | collective-permute-done | bytes 73760 | tf_op jit(solution)/shard_map/ppermute | solution.py:387
  59.0 0.0 collective-permute-done.1.c_core
  59.0 0.0 collective-permute-done.w_mate
  59.0 0.0 all-to-all-done.1.vale
  59.0 0.0 copy-done
  59.0 7.6 %shard_map.58 = (bf16[32,32,128]{2,1,0:T(8,128)(2,1)S(1)}, s32[16,4,128]{2,1,0:T(4,128)S(1)}) custom-call(s32[32,32]{1,0:T(8,128)S(1)} %copy-done, s32[2]{0:T(128)S(1)} %pad_add_fusion.place, bf16[256,4096]{1,0:T(8,128)(2,1)} %bitcast.5, bf16[256,2048]{1,0:T(8,128)(2,1)S(1)} %collective-permute-done.w_mate, bf16[16,8,4608]{2,1,0:T(8,128)(2,1)S(1)} %all-to-all-done.1.vale, ...), custom_call_target="tpu_custom_call" | custom-call | tf_op jit(solution)/shard_map/pallas_call | solution.py:178
  66.6 13.9 %all_to_all.21.shares = bf16[32,32,128]{2,1,0:T(8,128)(2,1)S(1)} all-to-all(bf16[32,32,128]{2,1,0:T(8,128)(2,1)S(1)} %get-tuple-element.12), channel_id=1, replica_groups={{0,1,2,3,4,5,6,7,8,9,10,11,12,13,14,15,256,257,258,259,260,261,262,263,..., dimensions={0} | all-to-all | bytes 524288 | tf_op jit(solution)/shard_map/all_to_all | solution.py:393
  80.5 0.1 shard_map.59
  80.6 17.9 %all_to_all.22.rows = f32[16,4,128]{2,1,0:T(4,128)S(1)} all-to-all(f32[16,4,128]{2,1,0:T(4,128)S(1)} %shard_map.59), channel_id=1, replica_groups={{0,16,32,48,64,80,96,112,128,144,160,176,192,208,224,240},{256,272,288,..., dimensions={0} | all-to-all | bytes 65536 | tf_op jit(solution)/shard_map/all_to_all | solution.py:394
  98.5 0.6 shard_map.60
Async XLA Ops:
  30.3 28.6 %all-to-all-start.1 = ((bf16[16,8,4608]{2,1,0:T(8,128)(2,1)}), bf16[16,8,4608]{2,1,0:T(8,128)(2,1)S(1)}, u32[]{:S(2)}, u32[]{:S(2)}) async-start(bf16[16,8,4608]{2,1,0:T(8,128)(2,1)} %get-tuple-element.9), calls=%async_computation.1 | async-start | bytes 2359296 | tf_op jit(solution)/shard_map/all_to_all | solution.py:390
  37.1 21.9 %copy-start = (s32[32,32]{1,0:T(8,128)S(1)}, s32[32,32]{1,0:T(8,128)}, u32[]{:S(2)}) copy-start(s32[32,32]{1,0:T(8,128)} %table.1) | copy-start | bytes 12292
  39.4 19.6 %collective-permute-start = (bf16[256,2048]{1,0:T(8,128)(2,1)S(1)}, bf16[256,2048]{1,0:T(8,128)(2,1)S(1)}, u32[]{:S(2)}, u32[]{:S(2)}) collective-permute-start(bf16[256,2048]{1,0:T(8,128)(2,1)S(1)} %shard_map.55), channel_id=1, source_target_pairs={{0,1},{1,0},{2,3},{3,2},{4,5},{5,4},{6,7},{7,6},{8,9},{9,8},{10,11... | collective-permute-start | bytes 3145736 | tf_op jit(solution)/shard_map/ppermute | solution.py:389
  46.0 9.6 %collective-permute-start.3 = (bf16[8,4608]{1,0:T(8,128)(2,1)S(1)}, bf16[8,4608]{1,0:T(8,128)(2,1)S(1)}, u32[]{:S(2)}, u32[]{:S(2)}) collective-permute-start(bf16[8,4608]{1,0:T(8,128)(2,1)S(1)} %get-tuple-element.10.c_keep), channel_id=1, source_target_pairs={{0,257},{1,256},{2,259},{3,258},{4,261},{5,260},{6,263},{7,262},{8... | collective-permute-start | bytes 221192 | tf_op jit(solution)/shard_map/ppermute | solution.py:388
  51.0 8.0 %collective-permute-start.2 = (bf16[8,4608]{1,0:T(8,128)(2,1)S(1)}, bf16[8,4608]{1,0:T(8,128)(2,1)S(1)}, u32[]{:S(2)}, u32[]{:S(2)}) collective-permute-start(bf16[8,4608]{1,0:T(8,128)(2,1)S(1)} %get-tuple-element.10.c_keep), channel_id=1, source_target_pairs={{0,256},{16,272},{32,288},{48,304},{64,320},{80,336},{96,352},{112... | collective-permute-start | bytes 221192 | tf_op jit(solution)/shard_map/ppermute | solution.py:387
  53.0 6.0 %collective-permute-start.1 = (bf16[8,4608]{1,0:T(8,128)(2,1)S(1)}, bf16[8,4608]{1,0:T(8,128)(2,1)S(1)}, u32[]{:S(2)}, u32[]{:S(2)}) collective-permute-start(bf16[8,4608]{1,0:T(8,128)(2,1)S(1)} %get-tuple-element.10.c_keep), channel_id=1, source_target_pairs={{0,1},{1,0},{2,3},{3,2},{4,5},{5,4},{6,7},{7,6},{8,9},{9,8},{10,11... | collective-permute-start | bytes 221192 | tf_op jit(solution)/shard_map/ppermute | solution.py:386
